TPU v7x, 512 devices: a whole 4x8x8 slice. The times are simulated.
512 devices in a mesh: seq: 64 (over z, x, core), head: 8 (over y).
Axes of the slice: x: 4, y: 8, z: 8, core: 2. Of those that a mesh axis runs over, the one named last changes fastest.
Arguments:
- queries: bfloat16 [16384, 2048], P('seq', 'head'), may hold values from -6 to 6
- key_rows: bfloat16 [16384, 2048], P('seq', 'head'), may hold values from -6 to 6
- value_rows: bfloat16 [16384, 4096], P('seq', 'head'), may hold values from -6 to 6
- input_gate: float32 [8, 16384], P('head', 'seq'), may hold values from -6 to 260
- forget_gate: float32 [8, 16384], P('head', 'seq'), as said below
- norm_gain: float32 [4096], P('head'), may hold values from 0.1 to 1.9
- output_gate: bfloat16 [16384, 4096], P('seq', 'head'), may hold values from -6 to 6
- out_weight: bfloat16 [4096, 4096], P('head', 'seq'), may hold values from -0.25 to 0.25
Outputs:
- layer_out: bfloat16 [16384, 4096], P('seq', 'head')
Inputs may be any that keep to these rules, and one draw needn't show every extreme that they name: `forget_gate`: forget-gate preactivations.
All inputs are finite; a program needn't handle non-finite values.
Results may differ from a plain program's by a relative error of at most 0.017.
Values may be sent and summed in bfloat16 or wider, within the bound.
No kernel may reach another device: no remote copies, remote signals or barrier semaphores. Data moves between devices by JAX's collectives and lax.ppermute only.
A program may use at most 128 MiB of HBM per device.

v0:
```python
import math

import jax
import jax.numpy as jnp
from jax import lax
from jax.sharding import PartitionSpec as P

NEG = -1e30


def entering(part, axis, combine, identity):
    place = lax.axis_index(axis)
    gathered = jax.tree.map(lambda a: lax.all_gather(a, axis), part)
    state = jax.tree.map(lambda a, e: jnp.zeros_like(a) + jnp.asarray(e, a.dtype), part, identity)

    def one(step, state):
        return combine(
            state, jax.tree.map(lambda a: lax.dynamic_index_in_dim(a, step, 0, False), gathered)
        )

    return lax.fori_loop(0, place, one, state)


def combine_states(earlier, later):
    state_early, max_early, decay_early = earlier
    state_late, max_late, decay_trailing = later
    new_max = jnp.maximum(decay_trailing + max_early, max_late)
    merged = (
        jnp.exp(decay_trailing + max_early - new_max) * state_early
        + jnp.exp(max_late - new_max) * state_late
    )
    return (merged, new_max, decay_early + decay_trailing)


def local(
    queries, key_rows, value_rows, input_gate, forget_gate, norm_gain, output_gate, out_weight
):
    length = queries.shape[0]
    inv_root = 1.0 / math.sqrt(queries.shape[1])
    cum_forget = jnp.cumsum(jax.nn.log_sigmoid(forget_gate[0]))
    gate_in = input_gate[0]
    places = jnp.arange(length)
    causal = places[:, None] >= places[None, :]
    log_weight = jnp.where(
        causal, cum_forget[:, None] - cum_forget[None, :] + gate_in[None, :], NEG
    )
    local_max = jnp.max(log_weight, axis=1)
    decay = cum_forget[-1]
    end_weight = decay - cum_forget + gate_in
    end_max = jnp.max(end_weight)
    scaled_keys = (key_rows.astype(jnp.float32) * jnp.exp(end_weight - end_max)[:, None]).astype(
        jnp.bfloat16
    )
    local_state = lax.dot_general(
        scaled_keys, value_rows, (((0,), (0,)), ((), ())), preferred_element_type=jnp.float32
    )
    identity = (
        jnp.zeros_like(local_state),
        jnp.full((1,), NEG, jnp.float32),
        jnp.zeros((1,), jnp.float32),
    )
    prev_state, prev_max, unused_decay = entering(
        (local_state, end_max[None], decay[None]), "seq", combine_states, identity
    )
    row_max = jnp.maximum(cum_forget + prev_max[0], local_max)
    scores = (
        lax.dot_general(
            queries, key_rows, (((1,), (1,)), ((), ())), preferred_element_type=jnp.float32
        )
        * inv_root
    )
    weights = (jnp.exp(log_weight - row_max[:, None]) * scores).astype(jnp.bfloat16)
    intra = jnp.dot(weights, value_rows, preferred_element_type=jnp.float32)
    carried = (
        jnp.dot(queries, prev_state.astype(jnp.bfloat16), preferred_element_type=jnp.float32)
        * inv_root
    )
    memory = intra + jnp.exp(cum_forget + prev_max[0] - row_max)[:, None] * carried
    centred = memory - jnp.mean(memory, axis=1, keepdims=True)
    spread = jnp.mean(centred * centred, axis=1, keepdims=True)
    gate_out = jax.nn.sigmoid(output_gate.astype(jnp.float32))
    normed = (centred * lax.rsqrt(spread + 1e-06) * norm_gain * gate_out).astype(jnp.bfloat16)
    terms = jnp.dot(
        normed,
        lax.all_gather(out_weight, "seq", axis=1, tiled=True),
        preferred_element_type=jnp.float32,
    )
    mixed_out = lax.psum_scatter(
        terms.astype(jnp.bfloat16), "head", scatter_dimension=1, tiled=True
    )
    return mixed_out


def solution(mesh):
    in_specs = (
        P("seq", "head"),
        P("seq", "head"),
        P("seq", "head"),
        P("head", "seq"),
        P("head", "seq"),
        P("head"),
        P("seq", "head"),
        P("head", "seq"),
    )
    out_specs = P("seq", "head")
    return jax.shard_map(local, mesh=mesh, in_specs=in_specs, out_specs=out_specs, check_vma=False)
```

profile of v0, /device:TPU:1, one launch (start us, length us, event | category | flops | bytes accessed | tf_op | source)
XLA Modules:
  0.0 458.7 jit_solution(2430965234361640764)
XLA Ops:
  6.5 0.0 copy-start
  6.5 0.0 all-gather.7.cloned.1.call-start
  6.5 0.7 neg.22
  7.3 0.3 reduce-window.9
  7.6 0.1 slice.10
  7.7 0.1 slice_reduce_fusion
  7.8 0.1 add_bitcast_fusion
  7.9 1.3 dynamic-slice
  9.2 1.2 fusion.26
  10.3 1.9 fusion.25
  12.3 1.9 subtract_exponential_fusion
  14.2 0.0 copy-done
  14.2 2.1 fusion.13
  16.3 0.0 all-gather.7.cloned.1.call-update
  16.3 0.0 all-gather.5.cloned.1.call-start
  16.4 0.7 all-gather.5.cloned.1.call-update
  17.1 0.0 reduce-scatter.2.cloned.1.call-start
  17.1 1.3 dynamic-update-slice.1
  18.4 133.2 %all-reduce.2 = (f32[64]{0:T(128)S(1)}, f32[64]{0:T(128)S(1)}) all-reduce(f32[64]{0:T(128)S(1)} %get-tuple-element.87, f32[64]{0:T(128)S(1)} %dynamic-update-slice.1), channel_id=2, replica_groups=mesh['seq'=64,'head'=8] {'seq'}, use_global_device_ids=true, to_apply=%add | all-reduce | flops 128 | bytes 1024
  151.6 0.9 fusion.12
  152.5 19.2 %all-gather.7.cloned.1.call-done = f32[16384,512]{1,0:T(8,128)} async-done(((f32[256,512]{1,0:T(8,128)}), f32[16384,512]{1,0:T(8,128)}) %all-gather.7.cloned.1.call-update) | async-done | bytes 33554448 | tf_op jit(solution)/shard_map/all_gather | solution.py:13
  171.7 0.0 copy-start.1
  171.7 0.0 copy-start.2
  171.8 0.0 copy-start.3
  171.8 0.0 copy-start.4
  171.8 0.0 copy-start.5
  171.8 3.8 while.14
  171.8 0.6 constant_dynamic-slice_fusion.3
  174.3 1.3 bitcast_add_fusion.2
  175.6 0.0 copy-done.1
  175.6 0.0 copy-done.2
  175.7 0.0 copy-done.3
  175.7 0.4 fusion.4
  176.1 0.3 fusion.27
  176.4 0.2 multiply_reduce_fusion
  176.7 79.9 %all-gather.5.cloned.1.call-done = bf16[512,4096]{0,1:T(8,128)(2,1)} async-done(((bf16[512,64]{0,1:T(8,128)(2,1)}), bf16[512,4096]{0,1:T(8,128)(2,1)}) %all-gather.5.cloned.1.call-update) | async-done | bytes 4194320 | tf_op jit(solution)/shard_map/all_gather | solution.py:85
  256.6 0.0 copy-done.4
  256.6 0.0 copy-done.5
  256.6 4.9 %convolution_convert_fusion = bf16[256,4096]{1,0:T(8,128)(2,1)} fusion(bf16[512,4096]{0,1:T(8,128)(2,1)} %all-gather.5.cloned.1.call-done, bf16[256,512]{1,0:T(8,128)(2,1)S(1)} %copy-done.4, f32[256,512]{1,0:T(8,128)S(1)} %get-tuple-element.89, f32[512]{0:T(512)S(1)} %copy-done.5, f32[256]{0:T(256)S(1)} %add_rsqrt_fusion, f32[256]{0:T(256)S(1)} %broadcast_multiply_fusion), kind=kOutput, calls=%fused_computation.3 | convolution fusion | flops 1075970048 | bytes 7081984 | tf_op jit(solution)/shard_map/dot_general | solution.py:83
  261.5 0.0 reduce-scatter.2.cloned.1.call-update
  261.6 190.6 %reduce-scatter.2.cloned.1.call-done = bf16[256,512]{1,0:T(8,128)(2,1)} async-done(((bf16[256,4096]{1,0:T(8,128)(2,1)}), bf16[256,512]{1,0:T(8,128)(2,1)}) %reduce-scatter.2.cloned.1.call-update) | async-done | bytes 262160 | tf_op jit(solution)/shard_map/reduce_scatter | solution.py:88
  (8 shorter events, 0.1 us)
Async XLA Ops:
  6.5 7.7 %copy-start = (bf16[256,512]{1,0:T(8,128)(2,1)S(1)}, bf16[256,512]{1,0:T(8,128)(2,1)}, u32[]{:S(2)}) copy-start(bf16[256,512]{1,0:T(8,128)(2,1)} %param.12) | copy-start | bytes 786436
  6.5 165.1 %all-gather.7.cloned.1.call-start = ((), (), s32[]{:S(2)}) async-start(), calls=%async_computation.3 | async-start | bytes 34078720 | tf_op jit(solution)/shard_map/all_gather | solution.py:13
  16.3 240.3 %all-gather.5.cloned.1.call-start = ((), (), s32[]{:S(2)}) async-start(), calls=%async_computation.1 | async-start | bytes 4259840 | tf_op jit(solution)/shard_map/all_gather | solution.py:85
  17.1 435.1 %reduce-scatter.2.cloned.1.call-start = ((), (), s32[]{:S(2)}) async-start(), calls=%async_computation.2 | async-start | bytes 2359296 | tf_op jit(solution)/shard_map/reduce_scatter | solution.py:88
  171.7 3.9 copy-start.1
  171.7 3.9 copy-start.2
  171.8 3.9 copy-start.3
  171.8 84.8 %copy-start.4 = (bf16[256,512]{1,0:T(8,128)(2,1)S(1)}, bf16[256,512]{1,0:T(8,128)(2,1)}, u32[]{:S(2)}) copy-start(bf16[256,512]{1,0:T(8,128)(2,1)} %param.16) | copy-start | bytes 786436
  171.8 84.8 %copy-start.5 = (f32[512]{0:T(512)S(1)}, f32[512]{0:T(512)}, u32[]{:S(2)}) copy-start(f32[512]{0:T(512)} %param.15) | copy-start | bytes 6148
Sparse Core Ops, SparseCore 0:
  16.4 155.1 all-gather.6
  175.0 81.5 all-gather.4
  261.7 190.4 reduce-scatter.1
where the time goes:
time: 467 us; the launch traced here: 459 us
  waiting for transfers between devices  290 us (62%)
  blocking collectives  133 us (28%)
  between operations  13.2 us (3%)
  matrix products  7.75 us (2%)
  other arithmetic  7.41 us (2%)
    reduce_scatter x1, waiting for transfers between devices, local(): lax.psum_scatter(terms.astype(jnp.bfloat16), 'head', scatter_dimension=1,...  191 us
    unnamed x1, blocking collectives  133 us
    all_gather x1, waiting for transfers between devices, local(): lax.all_gather(out_weight, 'seq', axis=1, tiled=True)  79.9 us
    all_gather x1, waiting for transfers between devices, entering(): gathered = jax.tree.map(lambda a: lax.all_gather(a, axis), part)  19.2 us
  transfers between devices with their start and end apart: 3, of which 3 were waited for; matrix products, arithmetic and copies ran while one was open for 1% of the time, Pallas kernels for 0%

commit v1 on v0

v1 whole, which is shorter than its diff:
```python
import functools
import math

import jax
import jax.numpy as jnp
from jax import lax
from jax.experimental import pallas as pl
from jax.experimental.pallas import tpu as pltpu
from jax.sharding import Mesh, PartitionSpec as P

NEG = -1e30
TILE = (16, 128)
F32 = jnp.float32
BF16 = jnp.bfloat16
VMEM = pl.BlockSpec(memory_space=pltpu.VMEM)
SMEM = pl.BlockSpec(memory_space=pltpu.SMEM)


def call(kernel, out_shape, n_scalar, n_vector, scratch=(), flops=0, vmem=48):
    return pl.pallas_call(
        kernel,
        out_shape=out_shape,
        in_specs=[SMEM] * n_scalar + [VMEM] * n_vector,
        out_specs=jax.tree.map(lambda _: VMEM, out_shape),
        scratch_shapes=list(scratch),
        compiler_params=pltpu.CompilerParams(vmem_limit_bytes=vmem * 2**20),
        cost_estimate=pl.CostEstimate(flops=flops, bytes_accessed=2**20, transcendentals=0),
    )


def tiles(rows, cols):
    return [(r, c) for r in range(0, rows, TILE[0]) for c in range(0, cols, TILE[1])]


def split3(value):
    high = value.astype(BF16).astype(F32)
    middle = (value - high).astype(BF16).astype(F32)
    return high, middle, value - high - middle


def scalar_tile(end_max, decay):
    rows = lax.broadcasted_iota(jnp.int32, TILE, 0)
    held = jnp.zeros(TILE, F32)
    for place, term in enumerate(split3(end_max) + split3(decay)):
        held = jnp.where(rows == place, jnp.broadcast_to(term, TILE), held)
    return held.astype(BF16)


def scalars_of(tile):
    held = tile.astype(F32)
    end_max = held[0:1] + held[1:2] + held[2:3]
    decay = held[3:4] + held[4:5] + held[5:6]
    return end_max, decay


def front_kernel(key_ref, value_ref, in_ref, forget_ref, tiles_ref, cum_ref):
    length = key_ref.shape[0]
    gate = forget_ref[...]
    log_forget = jnp.minimum(gate, 0.0) - jnp.log1p(jnp.exp(-jnp.abs(gate)))
    log_forget = jnp.broadcast_to(log_forget, (8, length))
    before = lax.broadcasted_iota(jnp.int32, (length, length), 0)
    after = lax.broadcasted_iota(jnp.int32, (length, length), 1)
    upper = jnp.where(before <= after, 1.0, 0.0).astype(F32)
    cum = jnp.dot(log_forget, upper, precision=lax.Precision.HIGHEST, preferred_element_type=F32)
    cum_ref[...] = cum
    decay = cum[0:1, length - 1 : length]
    end_weight = decay - cum[0:1] + in_ref[...]
    end_max = jnp.max(end_weight, axis=1, keepdims=True)
    scaled = (key_ref[...].astype(F32).T * jnp.exp(end_weight - end_max)).astype(BF16)
    state = jnp.dot(scaled, value_ref[...], preferred_element_type=F32).astype(BF16)
    places = tiles(*state.shape)
    for place, (row, col) in enumerate(places):
        tiles_ref[place] = state[row : row + TILE[0], col : col + TILE[1]]
    tiles_ref[len(places)] = scalar_tile(end_max, decay)


def pair_kernel(core_ref, both_ref, send_ref):
    core = core_ref[0]
    owners = send_ref.shape[0]
    last = both_ref.shape[1] - 1
    half = last // 2
    per = half // owners
    max_0, decay_0 = scalars_of(both_ref[0, last])
    max_1, decay_1 = scalars_of(both_ref[1, last])
    end_max = jnp.maximum(decay_1 + max_0, max_1)
    scale_0 = jnp.exp(decay_1 + max_0 - end_max)
    scale_1 = jnp.exp(max_1 - end_max)
    scalars = scalar_tile(end_max, decay_0 + decay_1)
    for owner in range(owners):
        for piece in range(per):
            place = core * half + owner * per + piece
            send_ref[owner, piece * 16 : piece * 16 + 16] = (
                scale_0 * both_ref[0, place].astype(F32) + scale_1 * both_ref[1, place].astype(F32)
            ).astype(BF16)
        send_ref[owner, per * 16 : per * 16 + 16] = scalars


def prefix_kernel(chip_ref, held_ref, state_ref, max_ref, maxes):
    chips, rows, lanes = state_ref.shape
    state = jnp.zeros((rows, lanes), F32)
    start_max = jnp.full((1, lanes), NEG, F32)
    for chip in range(chips):
        state_ref[chip] = state.astype(BF16)
        maxes[chip] = jnp.broadcast_to(start_max, (8, lanes))
        end_max, decay = scalars_of(held_ref[chip, rows : rows + 16])
        new_max = jnp.maximum(decay + start_max, end_max)
        state = jnp.exp(decay + start_max - new_max) * state + jnp.exp(
            end_max - new_max
        ) * held_ref[chip, 0:rows].astype(F32)
        start_max = new_max
    max_ref[...] = maxes[chip_ref[0]]


def memory_kernel(
    core_ref, query_ref, key_ref, value_ref, in_ref, cum_ref, gain_ref, gate_ref,
    tiles_ref, both_ref, max_ref, normed_ref, state
):
    length, width = query_ref.shape
    inv_root = 1.0 / math.sqrt(width)
    second = core_ref[0] == 1
    chip_max = max_ref[0:1]
    first_max, first_decay = scalars_of(both_ref[0, both_ref.shape[1] - 1])
    moved = jnp.maximum(first_decay + chip_max, first_max)
    start = jnp.where(second, moved, chip_max)
    keep = jnp.where(second, jnp.exp(first_decay + chip_max - moved), 1.0)
    add = jnp.where(second, jnp.exp(first_max - moved), 0.0)
    for place, (row, col) in enumerate(tiles(*state.shape)):
        state[row : row + TILE[0], col : col + TILE[1]] = (
            keep * tiles_ref[place].astype(F32) + add * both_ref[0, place].astype(F32)
        ).astype(BF16)
    start_max = start[:, 0:1]
    cum_row = cum_ref[0:1]
    cum_col = cum_ref[...].T[:, 0:1]
    at = lax.broadcasted_iota(jnp.int32, (length, length), 0)
    by = lax.broadcasted_iota(jnp.int32, (length, length), 1)
    log_weight = jnp.where(at >= by, cum_col - cum_row + in_ref[...], NEG)
    carried_weight = cum_col + start_max
    row_max = jnp.maximum(carried_weight, jnp.max(log_weight, axis=1, keepdims=True))
    scores = (
        lax.dot_general(
            query_ref[...], key_ref[...], (((1,), (1,)), ((), ())), preferred_element_type=F32
        )
        * inv_root
    )
    weights = (jnp.exp(log_weight - row_max) * scores).astype(BF16)
    intra = jnp.dot(weights, value_ref[...], preferred_element_type=F32)
    carried = jnp.dot(query_ref[...], state[...], preferred_element_type=F32) * inv_root
    memory = intra + jnp.exp(carried_weight - row_max) * carried
    centred = memory - jnp.mean(memory, axis=1, keepdims=True)
    spread = jnp.mean(centred * centred, axis=1, keepdims=True)
    gate_out = jax.nn.sigmoid(gate_ref[...].astype(F32))
    normed_ref[...] = (
        centred * lax.rsqrt(spread + 1e-06) * gain_ref[...] * gate_out
    ).astype(BF16)


def project_kernel(heads, slot_ref, *refs):
    normed, weight_ref, out_ref = refs[:heads], refs[heads], refs[heads + 1]
    width = normed[0].shape[1]
    total = jnp.zeros(out_ref.shape, F32)
    for place in range(heads):
        rows = weight_ref[slot_ref[place]].reshape(out_ref.shape[1], width)
        total += lax.dot_general(
            normed[place][...], rows, (((1,), (1,)), ((), ())), preferred_element_type=F32
        )
    out_ref[...] = total.astype(BF16)


def ring_gather(block, axis, size):
    up = [(i, (i + 1) % size) for i in range(size)]
    down = [(i, (i - 1) % size) for i in range(size)]
    gathered = [(0, block)]
    right = left = block
    for step in range(1, (size + 1) // 2):
        right = lax.ppermute(right, axis, up)
        left = lax.ppermute(left, axis, down)
        gathered += [(-step, right), (step, left)]
    half = block.shape[0] // 2
    right = lax.ppermute(right[:half], axis, up)
    left = lax.ppermute(left[half:], axis, down)
    gathered.append((size // 2, jnp.concatenate([right, left], axis=0)))
    return gathered


def local(sizes, queries, key_rows, value_rows, input_gate, forget_gate, norm_gain, output_gate, out_weight):
    planes, columns, cores, heads = sizes
    chips = planes * columns
    length, key_width = queries.shape
    value_width = value_rows.shape[1]
    core = lax.axis_index("c")
    head = lax.axis_index("y")
    chip = lax.axis_index(("z", "x"))
    count = key_width * value_width // (TILE[0] * TILE[1])
    per = count // 2 // chips

    swap = [
        (z * heads + h, ((h + heads // 2) % heads) * heads + z)
        for z in range(planes)
        for h in range(heads)
    ]
    weight = lax.ppermute(out_weight.T, ("z", "y"), swap)
    weight = lax.all_gather(weight, ("z", "x", "c"))
    weight = weight.reshape(planes, columns * cores, *weight.shape[-2:])

    state_tiles, cum = call(
        front_kernel,
        (
            jax.ShapeDtypeStruct((count + 1, *TILE), BF16),
            jax.ShapeDtypeStruct((8, length), F32),
        ),
        0,
        4,
    )(key_rows, value_rows, input_gate, forget_gate)
    both = lax.all_gather(state_tiles, "c")
    send = call(
        pair_kernel, jax.ShapeDtypeStruct((chips, (per + 1) * TILE[0], TILE[1]), BF16), 1, 1
    )(core[None], both)
    held = lax.all_to_all(send, ("z", "x"), 0, 0, tiled=True)
    starts, start_max = call(
        prefix_kernel,
        (
            jax.ShapeDtypeStruct((chips, per * TILE[0], TILE[1]), BF16),
            jax.ShapeDtypeStruct((8, TILE[1]), F32),
        ),
        1,
        1,
        [pltpu.VMEM((chips, 8, TILE[1]), F32)],
    )(chip[None], held)
    back = lax.all_to_all(starts, ("z", "x"), 0, 0, tiled=True)
    start_tiles = lax.all_gather(back, "c").reshape(count, *TILE)
    normed = call(
        memory_kernel,
        jax.ShapeDtypeStruct((length, value_width), BF16),
        1,
        10,
        [pltpu.VMEM((key_width, value_width), BF16)],
    )(
        core[None], queries, key_rows, value_rows, input_gate, cum, norm_gain[None],
        output_gate, start_tiles, both, start_max
    )
    gathered = ring_gather(normed, "y", heads)
    slots = jnp.stack([(head + place + heads // 2) % heads for place, _ in gathered])
    return call(
        functools.partial(project_kernel, heads),
        jax.ShapeDtypeStruct((length, value_width), BF16),
        1,
        heads + 1,
        flops=2 * length * value_width * value_width * heads,
    )(slots.astype(jnp.int32), *[block for _, block in gathered], weight)


def solution(mesh, sizes=(8, 4, 2, 8)):
    grid = Mesh(mesh.devices.reshape(sizes), ("z", "x", "c", "y"))
    seq = ("z", "x", "c")
    in_specs = (
        P(seq, "y"), P(seq, "y"), P(seq, "y"), P("y", seq), P("y", seq), P("y"), P(seq, "y"), P("y", seq)
    )
    return jax.shard_map(
        functools.partial(local, sizes), mesh=grid, in_specs=in_specs, out_specs=P(seq, "y"), check_vma=False
    )
```

time: 467 us -> 134 us (0.29); the launches traced: 459 us -> 132 us
  waiting for transfers between devices: 290 us -> 28.3 us
  blocking collectives: 133 us -> 22 us
  starting transfers between devices: 0.08 us -> 52 us
  matrix products: 7.75 us -> 0 us
  other arithmetic: 7.41 us -> 0.02 us
  Pallas kernels: 0 us -> 6.84 us
    reduce_scatter x1 -> x0, waiting for transfers between devices: 191 us -> none  [local(): lax.psum_scatter(terms.astype(jnp.bfloat16), 'head', scatter_dimension=1,...]
    unnamed x1 -> x0, blocking collectives: 133 us -> none
    all_gather x2 -> x1, waiting for transfers between devices: 99.1 us -> 0.02 us  [local(): weight = lax.all_gather(weight, ('z', 'x', 'c'))]
    ppermute x0 -> x9, starting transfers between devices: none -> 41.9 us  [the longest x3 17.4 us: ring_gather(): left = lax.ppermute(left, axis, down)]
    ppermute x0 -> x9, waiting for transfers between devices: none -> 16.3 us  [the longest x3 7.67 us: ring_gather(): left = lax.ppermute(left, axis, down)]
    all_to_all x0 -> x1, blocking collectives: none -> 14.1 us  [local(): back = lax.all_to_all(starts, ('z', 'x'), 0, 0, tiled=True)]
    all_to_all x0 -> x1, waiting for transfers between devices: none -> 12 us  [local(): held = lax.all_to_all(send, ('z', 'x'), 0, 0, tiled=True)]
    all_to_all x0 -> x1, starting transfers between devices: none -> 10.1 us  [local(): held = lax.all_to_all(send, ('z', 'x'), 0, 0, tiled=True)]
  transfers between devices with their start and end apart: 3 -> 11, of which waited for: 3 -> 6; matrix products, arithmetic and copies ran while one was open for 1% -> 0% of each run, Pallas kernels for 0% -> 2%
where the time goes in v1:
time: 134 us; the launch traced here: 132 us
  starting transfers between devices  52 us (39%)
  waiting for transfers between devices  28.3 us (21%)
  blocking collectives  22 us (16%)
  between operations  13.6 us (10%)
  local copies, waits for them, and re-layouts  9.01 us (7%)
  Pallas kernels  6.84 us (5%)
    ppermute x3, starting transfers between devices, ring_gather(): left = lax.ppermute(left, axis, down)  17.4 us
    all_to_all x1, blocking collectives, local(): back = lax.all_to_all(starts, ('z', 'x'), 0, 0, tiled=True)  14.1 us
    all_to_all x1, waiting for transfers between devices, local(): held = lax.all_to_all(send, ('z', 'x'), 0, 0, tiled=True)  12 us
    ppermute x1, starting transfers between devices, local(): weight = lax.ppermute(out_weight.T, ('z', 'y'), swap)  11.5 us
    all_to_all x1, starting transfers between devices, local(): held = lax.all_to_all(send, ('z', 'x'), 0, 0, tiled=True)  10.1 us
    unnamed x22, local copies, waits for them, and re-layouts  8.91 us
    ppermute x3, waiting for transfers between devices, ring_gather(): left = lax.ppermute(left, axis, down)  7.67 us
    ppermute x3, starting transfers between devices, ring_gather(): right = lax.ppermute(right, axis, up)  5.76 us
  transfers between devices with their start and end apart: 11, of which 6 were waited for; matrix products, arithmetic and copies ran while one was open for 0% of the time, Pallas kernels for 2%

profile of v1, /device:TPU:1, one launch (start us, length us, event | category | flops | bytes accessed | tf_op | source)
XLA Modules:
  0.0 131.8 jit_solution(15429262458348393226)
XLA Ops:
  6.5 0.0 all-gather.5.cloned.1.call-start
  6.5 11.5 %collective-permute-start.8 = (bf16[64,512]{1,0:T(8,128)(2,1)}, bf16[64,512]{1,0:T(8,128)(2,1)S(1)}, u32[]{:S(2)}, u32[]{:S(2)}) collective-permute-start(bf16[64,512]{1,0:T(8,128)(2,1)} %bitcast.18), channel_id=1, source_target_pairs={{0,256},{1,320},{2,384},{3,448},{4,0},{5,64},{6,128},{7,192},{64,2... | collective-permute-start | bytes 196616 | tf_op jit(solution)/shard_map/ppermute | solution.py:201
  18.0 3.8 %collective-permute-done.8 = bf16[64,512]{1,0:T(8,128)(2,1)S(1)} collective-permute-done((bf16[64,512]{1,0:T(8,128)(2,1)}, bf16[64,512]{1,0:T(8,128)(2,1)S(1)}, u32[]{:S(2)}, u32[]{:S(2)}) %collective-permute-start.8) | collective-permute-done | bytes 65568 | tf_op jit(solution)/shard_map/ppermute | solution.py:201
  21.8 0.0 copy-start.10
  21.8 0.6 copy-done.10
  22.4 0.0 all-gather.5.cloned.1.call-update
  22.5 0.0 copy-start
  22.5 0.9 copy-done
  23.4 0.0 copy-start.2
  23.4 0.9 copy-done.2
  24.3 0.0 copy-start.6
  24.3 0.7 copy-done.6
  25.0 0.0 copy-start.9
  25.0 0.7 copy-done.9
  25.7 0.7 shard_map.82
  26.4 3.7 %all-gather = bf16[130,16,128]{2,1,0:T(8,128)(2,1)S(1)} all-gather(bf16[65,16,128]{2,1,0:T(8,128)(2,1)S(1)} %get-tuple-element.10), channel_id=2, replica_groups=mesh['z'=8,'x'=4,'c'=2,'y'=8] {'c'}, dimensions={0}, use_global_device_ids=true | all-gather | bytes 798720 | tf_op jit(solution)/shard_map/all_gather | solution.py:214
  30.1 0.8 shard_map.83
  30.9 10.1 %all-to-all-start = ((bf16[32,32,128]{2,1,0:T(8,128)(2,1)}), bf16[32,32,128]{2,1,0:T(8,128)(2,1)S(1)}, u32[]{:S(2)}, u32[]{:S(2)}) async-start(bf16[32,32,128]{2,1,0:T(8,128)(2,1)} %shard_map.83), calls=%async_computation | async-start | bytes 524288 | tf_op jit(solution)/shard_map/all_to_all | solution.py:218
  41.0 12.0 %all-to-all-done.held_ref = bf16[32,32,128]{2,1,0:T(8,128)(2,1)S(1)} async-done(((bf16[32,32,128]{2,1,0:T(8,128)(2,1)}), bf16[32,32,128]{2,1,0:T(8,128)(2,1)S(1)}, u32[]{:S(2)}, u32[]{:S(2)}) %all-to-all-start) | async-done | bytes 262176 | tf_op jit(solution)/shard_map/all_to_all | solution.py:218
  52.9 0.1 shard_map.84
  53.1 14.1 %all_to_all.10 = bf16[32,16,128]{2,1,0:T(8,128)(2,1)S(1)} all-to-all(bf16[32,16,128]{2,1,0:T(8,128)(2,1)S(1)} %get-tuple-element.11), channel_id=1, replica_groups=mesh['z'=8,'x'=4,'c'=2,'y'=8] {'z','x'}, dimensions={0} | all-to-all | bytes 262144 | tf_op jit(solution)/shard_map/all_to_all | solution.py:229
  67.2 4.1 %all-gather.1.tiles_ref = bf16[64,16,128]{2,1,0:T(8,128)(2,1)S(1)} all-gather(bf16[32,16,128]{2,1,0:T(8,128)(2,1)S(1)} %all_to_all.10), channel_id=3, replica_groups=mesh['z'=8,'x'=4,'c'=2,'y'=8] {'c'}, dimensions={0}, use_global_device_ids=true | all-gather | bytes 393216 | tf_op jit(solution)/shard_map/all_gather | solution.py:230
  71.4 0.0 copy-start.1
  71.4 0.9 copy-done.1
  72.3 0.0 copy-start.3
  72.3 0.9 copy-done.3
  73.2 0.0 copy-start.4
  73.2 0.9 copy-done.4
  74.2 0.0 copy-start.5
  74.2 0.9 copy-done.5
  75.1 0.0 copy-start.7
  75.1 0.7 copy-done.7
  75.8 0.0 copy-start.8
  75.8 0.7 copy-done.8
  76.4 1.1 shard_map.85.refs_0_
  77.5 6.6 %collective-permute-start.1 = (bf16[256,512]{1,0:T(8,128)(2,1)S(1)}, bf16[256,512]{1,0:T(8,128)(2,1)S(1)}, u32[]{:S(2)}, u32[]{:S(2)}) collective-permute-start(bf16[256,512]{1,0:T(8,128)(2,1)S(1)} %shard_map.85.refs_0_), channel_id=1, source_target_pairs={{0,7},{1,0},{2,1},{3,2},{4,3},{5,4},{6,5},{7,6},{8,15},{9,8},{10,9... | collective-permute-start | bytes 786440 | tf_op jit(solution)/shard_map/ppermute | solution.py:176
  84.1 1.9 %collective-permute-start = (bf16[256,512]{1,0:T(8,128)(2,1)S(1)}, bf16[256,512]{1,0:T(8,128)(2,1)S(1)}, u32[]{:S(2)}, u32[]{:S(2)}) collective-permute-start(bf16[256,512]{1,0:T(8,128)(2,1)S(1)} %shard_map.85.refs_0_), channel_id=1, source_target_pairs={{0,1},{1,2},{2,3},{3,4},{4,5},{5,6},{6,7},{7,0},{8,9},{9,10},{10,1... | collective-permute-start | bytes 786440 | tf_op jit(solution)/shard_map/ppermute | solution.py:175
  86.0 3.4 %collective-permute-done.1.refs_2_ = bf16[256,512]{1,0:T(8,128)(2,1)S(1)} collective-permute-done((bf16[256,512]{1,0:T(8,128)(2,1)S(1)}, bf16[256,512]{1,0:T(8,128)(2,1)S(1)}, u32[]{:S(2)}, u32[]{:S(2)}) %collective-permute-start.1) | collective-permute-done | bytes 262176 | tf_op jit(solution)/shard_map/ppermute | solution.py:176
  89.4 5.4 %collective-permute-start.3 = (bf16[256,512]{1,0:T(8,128)(2,1)S(1)}, bf16[256,512]{1,0:T(8,128)(2,1)S(1)}, u32[]{:S(2)}, u32[]{:S(2)}) collective-permute-start(bf16[256,512]{1,0:T(8,128)(2,1)S(1)} %collective-permute-done.1.refs_2_), channel_id=1, source_target_pairs={{0,7},{1,0},{2,1},{3,2},{4,3},{5,4},{6,5},{7,6},{8,15},{9,8},{10,9... | collective-permute-start | bytes 786440 | tf_op jit(solution)/shard_map/ppermute | solution.py:176
  94.8 0.0 collective-permute-done.refs_1_
  94.8 1.9 %collective-permute-start.2 = (bf16[256,512]{1,0:T(8,128)(2,1)S(1)}, bf16[256,512]{1,0:T(8,128)(2,1)S(1)}, u32[]{:S(2)}, u32[]{:S(2)}) collective-permute-start(bf16[256,512]{1,0:T(8,128)(2,1)S(1)} %collective-permute-done.refs_1_), channel_id=1, source_target_pairs={{0,1},{1,2},{2,3},{3,4},{4,5},{5,6},{6,7},{7,0},{8,9},{9,10},{10,1... | collective-permute-start | bytes 786440 | tf_op jit(solution)/shard_map/ppermute | solution.py:175
  96.8 2.6 %collective-permute-done.3.refs_4_ = bf16[256,512]{1,0:T(8,128)(2,1)S(1)} collective-permute-done((bf16[256,512]{1,0:T(8,128)(2,1)S(1)}, bf16[256,512]{1,0:T(8,128)(2,1)S(1)}, u32[]{:S(2)}, u32[]{:S(2)}) %collective-permute-start.3) | collective-permute-done | bytes 262176 | tf_op jit(solution)/shard_map/ppermute | solution.py:176
  99.3 5.4 %collective-permute-start.5 = (bf16[256,512]{1,0:T(8,128)(2,1)S(1)}, bf16[256,512]{1,0:T(8,128)(2,1)S(1)}, u32[]{:S(2)}, u32[]{:S(2)}) collective-permute-start(bf16[256,512]{1,0:T(8,128)(2,1)S(1)} %collective-permute-done.3.refs_4_), channel_id=1, source_target_pairs={{0,7},{1,0},{2,1},{3,2},{4,3},{5,4},{6,5},{7,6},{8,15},{9,8},{10,9... | collective-permute-start | bytes 786440 | tf_op jit(solution)/shard_map/ppermute | solution.py:176
  104.7 0.0 collective-permute-done.2.refs_3_
  104.8 1.9 %collective-permute-start.4 = (bf16[256,512]{1,0:T(8,128)(2,1)S(1)}, bf16[256,512]{1,0:T(8,128)(2,1)S(1)}, u32[]{:S(2)}, u32[]{:S(2)}) collective-permute-start(bf16[256,512]{1,0:T(8,128)(2,1)S(1)} %collective-permute-done.2.refs_3_), channel_id=1, source_target_pairs={{0,1},{1,2},{2,3},{3,4},{4,5},{5,6},{6,7},{7,0},{8,9},{9,10},{10,1... | collective-permute-start | bytes 786440 | tf_op jit(solution)/shard_map/ppermute | solution.py:175
  106.7 1.7 %collective-permute-done.5.refs_6_ = bf16[256,512]{1,0:T(8,128)(2,1)S(1)} collective-permute-done((bf16[256,512]{1,0:T(8,128)(2,1)S(1)}, bf16[256,512]{1,0:T(8,128)(2,1)S(1)}, u32[]{:S(2)}, u32[]{:S(2)}) %collective-permute-start.5) | collective-permute-done | bytes 262176 | tf_op jit(solution)/shard_map/ppermute | solution.py:176
  108.4 5.3 %collective-permute-start.7 = (bf16[128,512]{1,0:T(8,128)(2,1)S(1)}, bf16[128,512]{1,0:T(8,128)(2,1)S(1)}, u32[]{:S(2)}, u32[]{:S(2)}) collective-permute-start(bf16[128,512]{1,0:T(8,128)(2,1)S(1)} %slice.9), channel_id=1, source_target_pairs={{0,7},{1,0},{2,1},{3,2},{4,3},{5,4},{6,5},{7,6},{8,15},{9,8},{10,9... | collective-permute-start | bytes 393224 | tf_op jit(solution)/shard_map/ppermute | solution.py:180
  113.8 0.0 collective-permute-done.4.refs_5_
  113.8 1.9 %collective-permute-start.6 = (bf16[128,512]{1,0:T(8,128)(2,1)S(1)}, bf16[128,512]{1,0:T(8,128)(2,1)S(1)}, u32[]{:S(2)}, u32[]{:S(2)}) collective-permute-start(bf16[128,512]{1,0:T(8,128)(2,1)S(1)} %slice.8), channel_id=1, source_target_pairs={{0,1},{1,2},{2,3},{3,4},{4,5},{5,6},{6,7},{7,0},{8,9},{9,10},{10,1... | collective-permute-start | bytes 393224 | tf_op jit(solution)/shard_map/ppermute | solution.py:179
  115.8 0.1 stack.35.slot_ref
  115.9 0.0 collective-permute-done.7
  115.9 4.8 %collective-permute-done.6 = bf16[128,512]{1,0:T(8,128)(2,1)S(1)} collective-permute-done((bf16[128,512]{1,0:T(8,128)(2,1)S(1)}, bf16[128,512]{1,0:T(8,128)(2,1)S(1)}, u32[]{:S(2)}, u32[]{:S(2)}) %collective-permute-start.6) | collective-permute-done | bytes 131104 | tf_op jit(solution)/shard_map/ppermute | solution.py:179
  120.7 0.0 all-gather.5.cloned.1.call-done
  120.8 4.2 %shard_map.86 = bf16[256,512]{1,0:T(8,128)(2,1)} custom-call(s32[8]{0:T(128)S(1)} %stack.35.slot_ref, bf16[256,512]{1,0:T(8,128)(2,1)S(1)} %shard_map.85.refs_0_, bf16[256,512]{1,0:T(8,128)(2,1)S(1)} %collective-permute-done.refs_1_, bf16[256,512]{1,0:T(8,128)(2,1)S(1)} %collective-permute-done.1.refs_2_, ...), custom_call_target="tpu_custom_call" | custom-call | flops 1073741824 | bytes 1048576 | tf_op jit(solution)/shard_map/pallas_call | solution.py:243
  (3 shorter events, 0.0 us)
Async XLA Ops:
  6.5 114.2 %all-gather.5.cloned.1.call-start = ((), (), s32[]{:S(2)}) async-start(), calls=%async_computation.2 | async-start | bytes 4259840 | tf_op jit(solution)/shard_map/all_gather | solution.py:202
  6.5 15.3 %collective-permute-start.8 = (bf16[64,512]{1,0:T(8,128)(2,1)}, bf16[64,512]{1,0:T(8,128)(2,1)S(1)}, u32[]{:S(2)}, u32[]{:S(2)}) collective-permute-start(bf16[64,512]{1,0:T(8,128)(2,1)} %bitcast.18), channel_id=1, source_target_pairs={{0,256},{1,320},{2,384},{3,448},{4,0},{5,64},{6,128},{7,192},{64,2... | collective-permute-start | bytes 196616 | tf_op jit(solution)/shard_map/ppermute | solution.py:201
  21.8 0.6 copy-start.10
  22.5 1.0 copy-start
  23.4 0.9 copy-start.2
  24.3 0.7 copy-start.6
  25.0 0.7 copy-start.9
  30.9 22.1 %all-to-all-start = ((bf16[32,32,128]{2,1,0:T(8,128)(2,1)}), bf16[32,32,128]{2,1,0:T(8,128)(2,1)S(1)}, u32[]{:S(2)}, u32[]{:S(2)}) async-start(bf16[32,32,128]{2,1,0:T(8,128)(2,1)} %shard_map.83), calls=%async_computation | async-start | bytes 524288 | tf_op jit(solution)/shard_map/all_to_all | solution.py:218
  71.4 0.9 copy-start.1
  72.3 0.9 copy-start.3
  73.2 0.9 copy-start.4
  74.2 0.9 copy-start.5
  75.1 0.7 copy-start.7
  75.8 0.7 copy-start.8
  77.5 11.9 %collective-permute-start.1 = (bf16[256,512]{1,0:T(8,128)(2,1)S(1)}, bf16[256,512]{1,0:T(8,128)(2,1)S(1)}, u32[]{:S(2)}, u32[]{:S(2)}) collective-permute-start(bf16[256,512]{1,0:T(8,128)(2,1)S(1)} %shard_map.85.refs_0_), channel_id=1, source_target_pairs={{0,7},{1,0},{2,1},{3,2},{4,3},{5,4},{6,5},{7,6},{8,15},{9,8},{10,9... | collective-permute-start | bytes 786440 | tf_op jit(solution)/shard_map/ppermute | solution.py:176
  84.1 10.7 %collective-permute-start = (bf16[256,512]{1,0:T(8,128)(2,1)S(1)}, bf16[256,512]{1,0:T(8,128)(2,1)S(1)}, u32[]{:S(2)}, u32[]{:S(2)}) collective-permute-start(bf16[256,512]{1,0:T(8,128)(2,1)S(1)} %shard_map.85.refs_0_), channel_id=1, source_target_pairs={{0,1},{1,2},{2,3},{3,4},{4,5},{5,6},{6,7},{7,0},{8,9},{9,10},{10,1... | collective-permute-start | bytes 786440 | tf_op jit(solution)/shard_map/ppermute | solution.py:175
  89.4 9.9 %collective-permute-start.3 = (bf16[256,512]{1,0:T(8,128)(2,1)S(1)}, bf16[256,512]{1,0:T(8,128)(2,1)S(1)}, u32[]{:S(2)}, u32[]{:S(2)}) collective-permute-start(bf16[256,512]{1,0:T(8,128)(2,1)S(1)} %collective-permute-done.1.refs_2_), channel_id=1, source_target_pairs={{0,7},{1,0},{2,1},{3,2},{4,3},{5,4},{6,5},{7,6},{8,15},{9,8},{10,9... | collective-permute-start | bytes 786440 | tf_op jit(solution)/shard_map/ppermute | solution.py:176
  94.8 9.9 %collective-permute-start.2 = (bf16[256,512]{1,0:T(8,128)(2,1)S(1)}, bf16[256,512]{1,0:T(8,128)(2,1)S(1)}, u32[]{:S(2)}, u32[]{:S(2)}) collective-permute-start(bf16[256,512]{1,0:T(8,128)(2,1)S(1)} %collective-permute-done.refs_1_), channel_id=1, source_target_pairs={{0,1},{1,2},{2,3},{3,4},{4,5},{5,6},{6,7},{7,0},{8,9},{9,10},{10,1... | collective-permute-start | bytes 786440 | tf_op jit(solution)/shard_map/ppermute | solution.py:175
  99.3 9.1 %collective-permute-start.5 = (bf16[256,512]{1,0:T(8,128)(2,1)S(1)}, bf16[256,512]{1,0:T(8,128)(2,1)S(1)}, u32[]{:S(2)}, u32[]{:S(2)}) collective-permute-start(bf16[256,512]{1,0:T(8,128)(2,1)S(1)} %collective-permute-done.3.refs_4_), channel_id=1, source_target_pairs={{0,7},{1,0},{2,1},{3,2},{4,3},{5,4},{6,5},{7,6},{8,15},{9,8},{10,9... | collective-permute-start | bytes 786440 | tf_op jit(solution)/shard_map/ppermute | solution.py:176
  104.8 9.0 %collective-permute-start.4 = (bf16[256,512]{1,0:T(8,128)(2,1)S(1)}, bf16[256,512]{1,0:T(8,128)(2,1)S(1)}, u32[]{:S(2)}, u32[]{:S(2)}) collective-permute-start(bf16[256,512]{1,0:T(8,128)(2,1)S(1)} %collective-permute-done.2.refs_3_), channel_id=1, source_target_pairs={{0,1},{1,2},{2,3},{3,4},{4,5},{5,6},{6,7},{7,0},{8,9},{9,10},{10,1... | collective-permute-start | bytes 786440 | tf_op jit(solution)/shard_map/ppermute | solution.py:175
  108.4 7.4 %collective-permute-start.7 = (bf16[128,512]{1,0:T(8,128)(2,1)S(1)}, bf16[128,512]{1,0:T(8,128)(2,1)S(1)}, u32[]{:S(2)}, u32[]{:S(2)}) collective-permute-start(bf16[128,512]{1,0:T(8,128)(2,1)S(1)} %slice.9), channel_id=1, source_target_pairs={{0,7},{1,0},{2,1},{3,2},{4,3},{5,4},{6,5},{7,6},{8,15},{9,8},{10,9... | collective-permute-start | bytes 393224 | tf_op jit(solution)/shard_map/ppermute | solution.py:180
  113.8 6.9 %collective-permute-start.6 = (bf16[128,512]{1,0:T(8,128)(2,1)S(1)}, bf16[128,512]{1,0:T(8,128)(2,1)S(1)}, u32[]{:S(2)}, u32[]{:S(2)}) collective-permute-start(bf16[128,512]{1,0:T(8,128)(2,1)S(1)} %slice.8), channel_id=1, source_target_pairs={{0,1},{1,2},{2,3},{3,4},{4,5},{5,6},{6,7},{7,0},{8,9},{9,10},{10,1... | collective-permute-start | bytes 393224 | tf_op jit(solution)/shard_map/ppermute | solution.py:179
Sparse Core Ops, SparseCore 0:
  22.6 89.9 all-gather.4

commit v2 on v1

v2 whole, which is shorter than its diff:
```python
import functools
import math

import jax
import jax.numpy as jnp
from jax import lax
from jax.experimental import pallas as pl
from jax.experimental.pallas import tpu as pltpu
from jax.sharding import Mesh, PartitionSpec as P

NEG = -1e30
TILE = (16, 128)
F32 = jnp.float32
BF16 = jnp.bfloat16
VMEM = pl.BlockSpec(memory_space=pltpu.VMEM)
SMEM = pl.BlockSpec(memory_space=pltpu.SMEM)
HBM = pl.BlockSpec(memory_space=pl.ANY)


def call(kernel, out_shape, places, scratch=(), flops=0, moved=2**20, vmem=48):
    return pl.pallas_call(
        kernel,
        out_shape=out_shape,
        in_specs=[{"s": SMEM, "v": VMEM, "h": HBM}[place] for place in places],
        out_specs=jax.tree.map(lambda _: VMEM, out_shape),
        scratch_shapes=list(scratch),
        compiler_params=pltpu.CompilerParams(vmem_limit_bytes=vmem * 2**20),
        cost_estimate=pl.CostEstimate(flops=flops, bytes_accessed=moved, transcendentals=0),
    )


def fetch(refs, held, semaphores):
    copies = [
        pltpu.make_async_copy(ref, buffer, semaphores.at[place])
        for place, (ref, buffer) in enumerate(zip(refs, held))
    ]
    for copy in copies:
        copy.start()
    return copies


def tiles(rows, cols):
    return [(r, c) for r in range(0, rows, TILE[0]) for c in range(0, cols, TILE[1])]


def split3(value):
    high = value.astype(BF16).astype(F32)
    middle = (value - high).astype(BF16).astype(F32)
    return high, middle, value - high - middle


def scalar_tile(end_max, decay):
    rows = lax.broadcasted_iota(jnp.int32, TILE, 0)
    held = jnp.zeros(TILE, F32)
    for place, term in enumerate(split3(end_max) + split3(decay)):
        held = jnp.where(rows == place, jnp.broadcast_to(term, TILE), held)
    return held.astype(BF16)


def scalars_of(tile):
    held = tile.astype(F32)
    end_max = held[0:1] + held[1:2] + held[2:3]
    decay = held[3:4] + held[4:5] + held[5:6]
    return end_max, decay


def front_kernel(key_hbm, value_hbm, in_hbm, forget_hbm, tiles_ref, cum_ref, keys, values, gates_in, gates, semaphores):
    copies = fetch((forget_hbm, in_hbm, key_hbm, value_hbm), (gates, gates_in, keys, values), semaphores)
    length = keys.shape[0]
    copies[0].wait()
    gate = gates[...]
    log_forget = jnp.minimum(gate, 0.0) - jnp.log1p(jnp.exp(-jnp.abs(gate)))
    log_forget = jnp.broadcast_to(log_forget, (8, length))
    before = lax.broadcasted_iota(jnp.int32, (length, length), 0)
    after = lax.broadcasted_iota(jnp.int32, (length, length), 1)
    upper = jnp.where(before <= after, 1.0, 0.0).astype(F32)
    cum = jnp.dot(log_forget, upper, precision=lax.Precision.HIGHEST, preferred_element_type=F32)
    cum_ref[...] = cum
    decay = cum[0:1, length - 1 : length]
    copies[1].wait()
    end_weight = decay - cum[0:1] + gates_in[...]
    end_max = jnp.max(end_weight, axis=1, keepdims=True)
    copies[2].wait()
    scaled = (keys[...].astype(F32).T * jnp.exp(end_weight - end_max)).astype(BF16)
    copies[3].wait()
    state = jnp.dot(scaled, values[...], preferred_element_type=F32).astype(BF16)
    places = tiles(*state.shape)
    for place, (row, col) in enumerate(places):
        tiles_ref[place] = state[row : row + TILE[0], col : col + TILE[1]]
    tiles_ref[len(places)] = scalar_tile(end_max, decay)


def pair_kernel(core_ref, both_ref, send_ref):
    core = core_ref[0]
    owners = send_ref.shape[0]
    last = both_ref.shape[1] - 1
    half = last // 2
    per = half // owners
    max_0, decay_0 = scalars_of(both_ref[0, last])
    max_1, decay_1 = scalars_of(both_ref[1, last])
    end_max = jnp.maximum(decay_1 + max_0, max_1)
    scale_0 = jnp.exp(decay_1 + max_0 - end_max)
    scale_1 = jnp.exp(max_1 - end_max)
    scalars = scalar_tile(end_max, decay_0 + decay_1)
    for owner in range(owners):
        for piece in range(per):
            place = core * half + owner * per + piece
            send_ref[owner, piece * 16 : piece * 16 + 16] = (
                scale_0 * both_ref[0, place].astype(F32) + scale_1 * both_ref[1, place].astype(F32)
            ).astype(BF16)
        send_ref[owner, per * 16 : per * 16 + 8] = scalars[0:8]


def prefix_kernel(chip_ref, held_ref, state_ref, max_ref, maxes):
    chips, rows, lanes = state_ref.shape
    state = jnp.zeros((rows, lanes), F32)
    start_max = jnp.full((1, lanes), NEG, F32)
    for chip in range(chips):
        state_ref[chip] = state.astype(BF16)
        maxes[chip] = jnp.broadcast_to(start_max, (8, lanes))
        end_max, decay = scalars_of(held_ref[chip, rows : rows + 8])
        new_max = jnp.maximum(decay + start_max, end_max)
        state = jnp.exp(decay + start_max - new_max) * state + jnp.exp(
            end_max - new_max
        ) * held_ref[chip, 0:rows].astype(F32)
        start_max = new_max
    max_ref[...] = maxes[chip_ref[0]]


def block_kernel(
    query_hbm, key_hbm, value_hbm, in_hbm, gate_hbm, gain_hbm, cum_ref,
    intra_ref, query_ref, gate_ref, stats_ref, keys, values, gates_in, gates, gains, semaphores
):
    copies = fetch(
        (in_hbm, query_hbm, key_hbm, value_hbm, gate_hbm, gain_hbm),
        (gates_in, query_ref, keys, values, gates, gains),
        semaphores,
    )
    length, width = query_ref.shape
    cum_row = cum_ref[0:1]
    cum_col = cum_ref[...].T[:, 0:1]
    at = lax.broadcasted_iota(jnp.int32, (length, length), 0)
    by = lax.broadcasted_iota(jnp.int32, (length, length), 1)
    copies[0].wait()
    log_weight = jnp.where(at >= by, cum_col - cum_row + gates_in[...], NEG)
    local_max = jnp.max(log_weight, axis=1, keepdims=True)
    lane = lax.broadcasted_iota(jnp.int32, stats_ref.shape, 1)
    stats_ref[...] = jnp.where(lane == 0, cum_col, local_max)
    copies[1].wait()
    copies[2].wait()
    scores = lax.dot_general(
        query_ref[...], keys[...], (((1,), (1,)), ((), ())), preferred_element_type=F32
    ) * (1.0 / math.sqrt(width))
    weights = (jnp.exp(log_weight - local_max) * scores).astype(BF16)
    copies[3].wait()
    intra_ref[...] = jnp.dot(weights, values[...], preferred_element_type=F32)
    copies[4].wait()
    copies[5].wait()
    gate_ref[...] = gains[...] * jax.nn.sigmoid(gates[...].astype(F32))


def memory_kernel(
    core_ref, intra_ref, query_ref, gate_ref, stats_ref, tiles_ref, both_ref, max_ref, normed_ref, state
):
    inv_root = 1.0 / math.sqrt(query_ref.shape[1])
    second = core_ref[0] == 1
    chip_max = max_ref[0:1]
    first_max, first_decay = scalars_of(both_ref[0, both_ref.shape[1] - 1])
    moved = jnp.maximum(first_decay + chip_max, first_max)
    start = jnp.where(second, moved, chip_max)
    keep = jnp.where(second, jnp.exp(first_decay + chip_max - moved), 1.0)
    add = jnp.where(second, jnp.exp(first_max - moved), 0.0)
    for place, (row, col) in enumerate(tiles(*state.shape)):
        state[row : row + TILE[0], col : col + TILE[1]] = (
            keep * tiles_ref[place].astype(F32) + add * both_ref[0, place].astype(F32)
        ).astype(BF16)
    local_max = stats_ref[:, 1:2]
    carried_weight = stats_ref[:, 0:1] + start[:, 0:1]
    row_max = jnp.maximum(carried_weight, local_max)
    carried = jnp.dot(query_ref[...], state[...], preferred_element_type=F32)
    memory = (
        jnp.exp(local_max - row_max) * intra_ref[...]
        + (jnp.exp(carried_weight - row_max) * inv_root) * carried
    )
    centred = memory - jnp.mean(memory, axis=1, keepdims=True)
    spread = jnp.mean(centred * centred, axis=1, keepdims=True)
    normed_ref[...] = (centred * lax.rsqrt(spread + 1e-06) * gate_ref[...]).astype(BF16)


def project_kernel(heads, slot_ref, *refs):
    normed, weight_hbm, out_ref, weight, semaphores = refs[:heads], *refs[heads:]
    copies = [
        pltpu.make_async_copy(weight_hbm.at[slot_ref[place]], weight.at[place], semaphores.at[place])
        for place in range(heads)
    ]
    for copy in copies:
        copy.start()
    width = normed[0].shape[1]
    total = jnp.zeros(out_ref.shape, F32)
    for place in range(heads):
        copies[place].wait()
        rows = weight[place].reshape(out_ref.shape[1], width)
        total += lax.dot_general(
            normed[place][...], rows, (((1,), (1,)), ((), ())), preferred_element_type=F32
        )
    out_ref[...] = total.astype(BF16)


def head_gather(block, axis, size):
    def shift(value, by):
        return lax.ppermute(value, axis, [(i, (i + by) % size) for i in range(size)])

    gathered = [(0, block)]
    half = block.shape[0] // 2
    if size == 8:
        far, back = shift(block, 2), shift(block, -2)
        near, behind = shift(block, 1), shift(block, -1)
        gathered += [(-1, near), (1, behind), (-2, far), (2, back)]
        gathered += [(-3, shift(far, 1)), (3, shift(back, -1))]
        first, last, _, _ = lax.optimization_barrier((far[:half], back[half:], near, behind))
        opposite = [shift(first, 2), shift(last, -2)]
    else:
        right = left = block
        if size == 4:
            right, left = shift(block, 1), shift(block, -1)
            gathered += [(-1, right), (1, left)]
        opposite = [shift(right[:half], 1), shift(left[half:], -1)]
    gathered.append((size // 2, jnp.concatenate(opposite, axis=0)))
    return gathered


def local(sizes, queries, key_rows, value_rows, input_gate, forget_gate, norm_gain, output_gate, out_weight):
    planes, columns, cores, heads = sizes
    chips = planes * columns
    length, key_width = queries.shape
    value_width = value_rows.shape[1]
    core = lax.axis_index("c")
    head = lax.axis_index("y")
    chip = lax.axis_index(("z", "x"))
    count = key_width * value_width // (TILE[0] * TILE[1])
    per = count // 2 // chips

    swap = [
        (z * heads + h, ((h + heads // 2) % heads) * heads + z)
        for z in range(planes)
        for h in range(heads)
    ]
    weight = lax.ppermute(out_weight.T, ("z", "y"), swap)
    tile_array = functools.partial(jax.ShapeDtypeStruct, dtype=BF16)
    state_tiles, cum = call(
        front_kernel,
        (tile_array((count + 1, *TILE)), jax.ShapeDtypeStruct((8, length), F32)),
        "hhhh",
        [
            pltpu.VMEM(key_rows.shape, BF16),
            pltpu.VMEM(value_rows.shape, BF16),
            pltpu.VMEM(input_gate.shape, F32),
            pltpu.VMEM(forget_gate.shape, F32),
            pltpu.SemaphoreType.DMA((4,)),
        ],
        vmem=60,
    )(key_rows, value_rows, input_gate, forget_gate)
    both = lax.all_gather(state_tiles, "c")
    send = call(pair_kernel, tile_array((chips, per * TILE[0] + 8, TILE[1])), "sv")(core[None], both)
    weight, send = lax.optimization_barrier((weight, send))
    weight = lax.all_gather(weight, ("z", "x", "c"))
    weight = weight.reshape(planes, columns * cores, *weight.shape[-2:])

    held = lax.all_to_all(send, ("z", "x"), 0, 0, tiled=True)
    intra, query_held, gates, stats = call(
        block_kernel,
        (
            jax.ShapeDtypeStruct(value_rows.shape, F32),
            jax.ShapeDtypeStruct(queries.shape, BF16),
            jax.ShapeDtypeStruct(value_rows.shape, F32),
            jax.ShapeDtypeStruct((length, 128), F32),
        ),
        "hhhhhhv",
        [
            pltpu.VMEM(key_rows.shape, BF16),
            pltpu.VMEM(value_rows.shape, BF16),
            pltpu.VMEM(input_gate.shape, F32),
            pltpu.VMEM(output_gate.shape, BF16),
            pltpu.VMEM((1, value_width), F32),
            pltpu.SemaphoreType.DMA((6,)),
        ],
        flops=2 * length * length * (key_width + value_width),
    )(queries, key_rows, value_rows, input_gate, output_gate, norm_gain[None], cum)
    held, intra = lax.optimization_barrier((held, intra))
    starts, start_max = call(
        prefix_kernel,
        (tile_array((chips, per * TILE[0], TILE[1])), jax.ShapeDtypeStruct((8, TILE[1]), F32)),
        "sv",
        [pltpu.VMEM((chips, 8, TILE[1]), F32)],
    )(chip[None], held)
    back = lax.all_to_all(starts, ("z", "x"), 0, 0, tiled=True)
    start_tiles = lax.all_gather(back, "c").reshape(count, *TILE)
    normed = call(
        memory_kernel,
        tile_array((length, value_width)),
        "svvvvvvv",
        [pltpu.VMEM((key_width, value_width), BF16)],
    )(core[None], intra, query_held, gates, stats, start_tiles, both, start_max)
    gathered = head_gather(normed, "y", heads)
    slots = jnp.stack([(head + place + heads // 2) % heads for place, _ in gathered])
    return call(
        functools.partial(project_kernel, heads),
        tile_array((length, value_width)),
        "s" + "v" * heads + "h",
        [
            pltpu.VMEM((heads, columns * cores, *weight.shape[-2:]), BF16),
            pltpu.SemaphoreType.DMA((heads,)),
        ],
        flops=2 * length * value_width * value_width * heads,
    )(slots.astype(jnp.int32), *[block for _, block in gathered], weight)


def solution(mesh, sizes=(8, 4, 2, 8)):
    grid = Mesh(mesh.devices.reshape(sizes), ("z", "x", "c", "y"))
    seq = ("z", "x", "c")
    in_specs = (
        P(seq, "y"), P(seq, "y"), P(seq, "y"), P("y", seq), P("y", seq), P("y"), P(seq, "y"), P("y", seq)
    )
    return jax.shard_map(
        functools.partial(local, sizes), mesh=grid, in_specs=in_specs, out_specs=P(seq, "y"), check_vma=False
    )
```

time: 134 us -> 124 us (0.925); the launches traced: 132 us -> 124 us
  waiting for transfers between devices: 28.3 us -> 23.6 us
  starting transfers between devices: 52 us -> 48.7 us
  local copies, waits for them, and re-layouts: 9.01 us -> 6.49 us
  Pallas kernels: 6.84 us -> 9.35 us
    all_gather x1, waiting for transfers between devices: 0.02 us -> 9.93 us  [local(): weight = lax.all_gather(weight, ('z', 'x', 'c'))]
    all_to_all x1, waiting for transfers between devices: 12 us -> 3.45 us  [local(): held = lax.all_to_all(send, ('z', 'x'), 0, 0, tiled=True)]
    ppermute x1, waiting for transfers between devices: 3.8 us -> 0.01 us  [local(): weight = lax.ppermute(out_weight.T, ('z', 'y'), swap)]
    ppermute x8, starting transfers between devices: 30.4 us -> 27.6 us  [shift(): lax.ppermute(value, axis, [(i, (i + by) % size) for i in range(size)])]
    unnamed x22 -> x16, local copies, waits for them, and re-layouts: 8.91 us -> 6.38 us
    pallas_call x5 -> x6, Pallas kernels: 6.84 us -> 9.35 us  [the longest x1 4.3 us: local(): call(functools.partial(project_kernel, heads), tile_array((length, value_...]
    ppermute x8, waiting for transfers between devices: 12.5 us -> 10.2 us  [shift(): lax.ppermute(value, axis, [(i, (i + by) % size) for i in range(size)])]
  transfers between devices with their start and end apart: 11 -> 11, of which waited for: 6 -> 7; matrix products, arithmetic and copies ran while one was open for 0% -> 0% of each run, Pallas kernels for 2% -> 4%
where the time goes in v2:
time: 124 us
  starting transfers between devices  48.7 us (39%)
  waiting for transfers between devices  23.6 us (19%)
  blocking collectives  22 us (18%)
  between operations  13.7 us (11%)
  Pallas kernels  9.35 us (8%)
  local copies, waits for them, and re-layouts  6.49 us (5%)
    ppermute x8, starting transfers between devices, shift(): lax.ppermute(value, axis, [(i, (i + by) % size) for i in range(size)])  27.6 us
    all_to_all x1, blocking collectives, local(): back = lax.all_to_all(starts, ('z', 'x'), 0, 0, tiled=True)  15.5 us
    ppermute x1, starting transfers between devices, local(): weight = lax.ppermute(out_weight.T, ('z', 'y'), swap)  11.5 us
    ppermute x8, waiting for transfers between devices, shift(): lax.ppermute(value, axis, [(i, (i + by) % size) for i in range(size)])  10.2 us
    all_gather x1, waiting for transfers between devices, local(): weight = lax.all_gather(weight, ('z', 'x', 'c'))  9.93 us
    all_to_all x1, starting transfers between devices, local(): held = lax.all_to_all(send, ('z', 'x'), 0, 0, tiled=True)  9.7 us
    unnamed x16, local copies, waits for them, and re-layouts  6.38 us
    pallas_call x1, Pallas kernels, local(): call(functools.partial(project_kernel, heads), tile_array((length, value_...  4.3 us
  transfers between devices with their start and end apart: 11, of which 7 were waited for; matrix products, arithmetic and copies ran while one was open for 0% of the time, Pallas kernels for 4%

profile of v2, /device:TPU:1, one launch (start us, length us, event | category | flops | bytes accessed | tf_op | source)
XLA Modules:
  0.0 123.7 jit_solution(13927091672685862306)
XLA Ops:
  6.5 0.0 all-gather.5.cloned.1.call-start
  6.5 11.5 %collective-permute-start = (bf16[64,512]{1,0:T(8,128)(2,1)}, bf16[64,512]{1,0:T(8,128)(2,1)S(1)}, u32[]{:S(2)}, u32[]{:S(2)}) collective-permute-start(bf16[64,512]{1,0:T(8,128)(2,1)} %bitcast.18), channel_id=1, source_target_pairs={{0,256},{1,320},{2,384},{3,448},{4,0},{5,64},{6,128},{7,192},{64,2... | collective-permute-start | bytes 196616 | tf_op jit(solution)/shard_map/ppermute | solution.py:248
  18.0 2.3 %shard_map.82 = (bf16[65,16,128]{2,1,0:T(8,128)(2,1)}, f32[8,256]{1,0:T(8,128)}) custom-call(bf16[256,256]{1,0:T(8,128)(2,1)} %key_hbm.3, bf16[256,512]{1,0:T(8,128)(2,1)} %value_hbm.3, f32[1,256]{1,0:T(1,128)} %in_hbm.3, f32[1,256]{1,0:T(1,128)} %forget_hbm.1), custom_call_target="tpu_custom_call" | custom-call | bytes 1048576 | tf_op jit(solution)/shard_map/pallas_call | solution.py:250
  20.3 3.0 %all-gather = bf16[130,16,128]{2,1,0:T(8,128)(2,1)S(1)} all-gather(bf16[65,16,128]{2,1,0:T(8,128)(2,1)} %get-tuple-element.19), channel_id=2, replica_groups=mesh['z'=8,'x'=4,'c'=2,'y'=8] {'c'}, dimensions={0}, use_global_device_ids=true | all-gather | bytes 798720 | tf_op jit(solution)/shard_map/all_gather | solution.py:263
  23.3 0.7 shard_map.83
  24.0 0.0 collective-permute-done
  24.0 0.0 copy-start.7
  24.0 0.6 copy-done.7
  24.6 0.0 all-gather.5.cloned.1.call-update
  24.7 9.7 %all-to-all-start = ((bf16[32,24,128]{2,1,0:T(8,128)(2,1)}), bf16[32,24,128]{2,1,0:T(8,128)(2,1)S(1)}, u32[]{:S(2)}, u32[]{:S(2)}) async-start(bf16[32,24,128]{2,1,0:T(8,128)(2,1)} %shard_map.83), calls=%async_computation | async-start | bytes 393216 | tf_op jit(solution)/shard_map/all_to_all | solution.py:269
  34.4 0.0 copy-start
  34.4 0.9 copy-done
  35.3 0.0 copy-start.1
  35.3 0.9 copy-done.1
  36.2 0.0 copy-start.2
  36.2 0.9 copy-done.2
  37.2 0.0 copy-start.3
  37.2 0.9 copy-done.3
  38.1 0.0 copy-start.4
  38.1 0.7 copy-done.4
  38.8 0.0 copy-start.5
  38.8 0.7 copy-done.5
  39.5 0.0 copy-start.6
  39.5 0.7 copy-done.6
  40.1 1.3 %shard_map.84 = (f32[256,512]{1,0:T(8,128)S(1)}, bf16[256,256]{1,0:T(8,128)(2,1)S(1)}, f32[256,512]{1,0:T(8,128)S(1)}, f32[256,128]{1,0:T(8,128)S(1)}) custom-call(bf16[256,256]{1,0:T(8,128)(2,1)S(1)} %copy-done.3, bf16[256,256]{1,0:T(8,128)(2,1)S(1)} %copy-done.1, bf16[256,512]{1,0:T(8,128)(2,1)S(1)} %copy-done, f32[1,256]{1,0:T(1,128)S(1)} %copy-done.5, ...), custom_call_target="tpu_custom_call" | custom-call | flops 100663296 | bytes 1048576 | tf_op jit(solution)/shard_map/pallas_call | solution.py:270
  41.5 3.5 %all-to-all-done.held_ref = bf16[32,24,128]{2,1,0:T(8,128)(2,1)S(1)} async-done(((bf16[32,24,128]{2,1,0:T(8,128)(2,1)}), bf16[32,24,128]{2,1,0:T(8,128)(2,1)S(1)}, u32[]{:S(2)}, u32[]{:S(2)}) %all-to-all-start) | async-done | bytes 196640 | tf_op jit(solution)/shard_map/all_to_all | solution.py:269
  44.9 0.1 shard_map.85
  45.1 15.5 %all_to_all.10 = bf16[32,16,128]{2,1,0:T(8,128)(2,1)S(1)} all-to-all(bf16[32,16,128]{2,1,0:T(8,128)(2,1)S(1)} %get-tuple-element.28), channel_id=1, replica_groups=mesh['z'=8,'x'=4,'c'=2,'y'=8] {'z','x'}, dimensions={0} | all-to-all | bytes 262144 | tf_op jit(solution)/shard_map/all_to_all | solution.py:296
  60.5 3.5 %all-gather.1.tiles_ref = bf16[64,16,128]{2,1,0:T(8,128)(2,1)S(1)} all-gather(bf16[32,16,128]{2,1,0:T(8,128)(2,1)S(1)} %all_to_all.10), channel_id=3, replica_groups=mesh['z'=8,'x'=4,'c'=2,'y'=8] {'c'}, dimensions={0}, use_global_device_ids=true | all-gather | bytes 393216 | tf_op jit(solution)/shard_map/all_gather | solution.py:297
  64.0 0.6 shard_map.86.refs_0_
  64.6 5.2 %collective-permute-start.3 = (bf16[256,512]{1,0:T(8,128)(2,1)S(1)}, bf16[256,512]{1,0:T(8,128)(2,1)S(1)}, u32[]{:S(2)}, u32[]{:S(2)}) collective-permute-start(bf16[256,512]{1,0:T(8,128)(2,1)S(1)} %shard_map.86.refs_0_), channel_id=1, source_target_pairs={{0,2},{1,3},{2,4},{3,5},{4,6},{5,7},{6,0},{7,1},{8,10},{9,11},{10,... | collective-permute-start | bytes 786440 | tf_op jit(solution)/shard_map/ppermute | solution.py:211
  69.8 2.2 %collective-permute-start.4 = (bf16[256,512]{1,0:T(8,128)(2,1)S(1)}, bf16[256,512]{1,0:T(8,128)(2,1)S(1)}, u32[]{:S(2)}, u32[]{:S(2)}) collective-permute-start(bf16[256,512]{1,0:T(8,128)(2,1)S(1)} %shard_map.86.refs_0_), channel_id=1, source_target_pairs={{0,6},{1,7},{2,0},{3,1},{4,2},{5,3},{6,4},{7,5},{8,14},{9,15},{10,... | collective-permute-start | bytes 786440 | tf_op jit(solution)/shard_map/ppermute | solution.py:211
  72.0 4.0 %collective-permute-start.1 = (bf16[256,512]{1,0:T(8,128)(2,1)S(1)}, bf16[256,512]{1,0:T(8,128)(2,1)S(1)}, u32[]{:S(2)}, u32[]{:S(2)}) collective-permute-start(bf16[256,512]{1,0:T(8,128)(2,1)S(1)} %shard_map.86.refs_0_), channel_id=1, source_target_pairs={{0,1},{1,2},{2,3},{3,4},{4,5},{5,6},{6,7},{7,0},{8,9},{9,10},{10,1... | collective-permute-start | bytes 786440 | tf_op jit(solution)/shard_map/ppermute | solution.py:211
  76.0 3.1 %collective-permute-start.2 = (bf16[256,512]{1,0:T(8,128)(2,1)S(1)}, bf16[256,512]{1,0:T(8,128)(2,1)S(1)}, u32[]{:S(2)}, u32[]{:S(2)}) collective-permute-start(bf16[256,512]{1,0:T(8,128)(2,1)S(1)} %shard_map.86.refs_0_), channel_id=1, source_target_pairs={{0,7},{1,0},{2,1},{3,2},{4,3},{5,4},{6,5},{7,6},{8,15},{9,8},{10,9... | collective-permute-start | bytes 786440 | tf_op jit(solution)/shard_map/ppermute | solution.py:211
  79.1 2.1 %collective-permute-done.3.refs_3_ = bf16[256,512]{1,0:T(8,128)(2,1)S(1)} collective-permute-done((bf16[256,512]{1,0:T(8,128)(2,1)S(1)}, bf16[256,512]{1,0:T(8,128)(2,1)S(1)}, u32[]{:S(2)}, u32[]{:S(2)}) %collective-permute-start.3) | collective-permute-done | bytes 262176 | tf_op jit(solution)/shard_map/ppermute | solution.py:211
  81.2 3.8 %collective-permute-start.5 = (bf16[256,512]{1,0:T(8,128)(2,1)S(1)}, bf16[256,512]{1,0:T(8,128)(2,1)S(1)}, u32[]{:S(2)}, u32[]{:S(2)}) collective-permute-start(bf16[256,512]{1,0:T(8,128)(2,1)S(1)} %collective-permute-done.3.refs_3_), channel_id=1, source_target_pairs={{0,1},{1,2},{2,3},{3,4},{4,5},{5,6},{6,7},{7,0},{8,9},{9,10},{10,1... | collective-permute-start | bytes 786440 | tf_op jit(solution)/shard_map/ppermute | solution.py:211
  85.1 1.9 %collective-permute-done.4.refs_4_ = bf16[256,512]{1,0:T(8,128)(2,1)S(1)} collective-permute-done((bf16[256,512]{1,0:T(8,128)(2,1)S(1)}, bf16[256,512]{1,0:T(8,128)(2,1)S(1)}, u32[]{:S(2)}, u32[]{:S(2)}) %collective-permute-start.4) | collective-permute-done | bytes 262176 | tf_op jit(solution)/shard_map/ppermute | solution.py:211
  86.9 1.9 %collective-permute-start.6 = (bf16[256,512]{1,0:T(8,128)(2,1)S(1)}, bf16[256,512]{1,0:T(8,128)(2,1)S(1)}, u32[]{:S(2)}, u32[]{:S(2)}) collective-permute-start(bf16[256,512]{1,0:T(8,128)(2,1)S(1)} %collective-permute-done.4.refs_4_), channel_id=1, source_target_pairs={{0,7},{1,0},{2,1},{3,2},{4,3},{5,4},{6,5},{7,6},{8,15},{9,8},{10,9... | collective-permute-start | bytes 786440 | tf_op jit(solution)/shard_map/ppermute | solution.py:211
  88.9 0.0 collective-permute-done.1.refs_1_
  88.9 2.6 %collective-permute-done.2.refs_2_ = bf16[256,512]{1,0:T(8,128)(2,1)S(1)} collective-permute-done((bf16[256,512]{1,0:T(8,128)(2,1)S(1)}, bf16[256,512]{1,0:T(8,128)(2,1)S(1)}, u32[]{:S(2)}, u32[]{:S(2)}) %collective-permute-start.2) | collective-permute-done | bytes 262176 | tf_op jit(solution)/shard_map/ppermute | solution.py:211
  91.5 4.4 %collective-permute-start.7 = (bf16[128,512]{1,0:T(8,128)(2,1)S(1)}, bf16[128,512]{1,0:T(8,128)(2,1)S(1)}, u32[]{:S(2)}, u32[]{:S(2)}) collective-permute-start(bf16[128,512]{1,0:T(8,128)(2,1)S(1)} %slice.8), channel_id=1, source_target_pairs={{0,2},{1,3},{2,4},{3,5},{4,6},{5,7},{6,0},{7,1},{8,10},{9,11},{10,... | collective-permute-start | bytes 393224 | tf_op jit(solution)/shard_map/ppermute | solution.py:211
  95.9 3.0 %collective-permute-start.8 = (bf16[128,512]{1,0:T(8,128)(2,1)S(1)}, bf16[128,512]{1,0:T(8,128)(2,1)S(1)}, u32[]{:S(2)}, u32[]{:S(2)}) collective-permute-start(bf16[128,512]{1,0:T(8,128)(2,1)S(1)} %slice.9), channel_id=1, source_target_pairs={{0,6},{1,7},{2,0},{3,1},{4,2},{5,3},{6,4},{7,5},{8,14},{9,15},{10,... | collective-permute-start | bytes 393224 | tf_op jit(solution)/shard_map/ppermute | solution.py:211
  99.0 0.1 stack.35.slot_ref
  99.1 0.6 collective-permute-done.7
  99.6 3.0 %collective-permute-done.8 = bf16[128,512]{1,0:T(8,128)(2,1)S(1)} collective-permute-done((bf16[128,512]{1,0:T(8,128)(2,1)S(1)}, bf16[128,512]{1,0:T(8,128)(2,1)S(1)}, u32[]{:S(2)}, u32[]{:S(2)}) %collective-permute-start.8) | collective-permute-done | bytes 131104 | tf_op jit(solution)/shard_map/ppermute | solution.py:211
  102.6 0.0 collective-permute-done.5.refs_5_
  102.6 0.0 collective-permute-done.6.refs_6_
  102.7 9.9 %all-gather.5.cloned.1.call-done = bf16[4096,512]{1,0:T(8,128)(2,1)} async-done(((bf16[64,512]{1,0:T(8,128)(2,1)}), bf16[4096,512]{1,0:T(8,128)(2,1)}) %all-gather.5.cloned.1.call-update) | async-done | bytes 4194320 | tf_op jit(solution)/shard_map/all_gather | solution.py:266
  112.6 4.3 %shard_map.87 = bf16[256,512]{1,0:T(8,128)(2,1)} custom-call(s32[8]{0:T(128)S(1)} %stack.35.slot_ref, bf16[256,512]{1,0:T(8,128)(2,1)S(1)} %shard_map.86.refs_0_, bf16[256,512]{1,0:T(8,128)(2,1)S(1)} %collective-permute-done.1.refs_1_, bf16[256,512]{1,0:T(8,128)(2,1)S(1)} %collective-permute-done.2.refs_2_, ...), custom_call_target="tpu_custom_call" | custom-call | flops 1073741824 | bytes 1048576 | tf_op jit(solution)/shard_map/pallas_call | solution.py:306
  (3 shorter events, 0.0 us)
Async XLA Ops:
  6.5 106.0 %all-gather.5.cloned.1.call-start = ((), (), s32[]{:S(2)}) async-start(), calls=%async_computation.2 | async-start | bytes 4259840 | tf_op jit(solution)/shard_map/all_gather | solution.py:266
  6.5 17.5 %collective-permute-start = (bf16[64,512]{1,0:T(8,128)(2,1)}, bf16[64,512]{1,0:T(8,128)(2,1)S(1)}, u32[]{:S(2)}, u32[]{:S(2)}) collective-permute-start(bf16[64,512]{1,0:T(8,128)(2,1)} %bitcast.18), channel_id=1, source_target_pairs={{0,256},{1,320},{2,384},{3,448},{4,0},{5,64},{6,128},{7,192},{64,2... | collective-permute-start | bytes 196616 | tf_op jit(solution)/shard_map/ppermute | solution.py:248
  24.0 0.6 copy-start.7
  24.7 20.3 %all-to-all-start = ((bf16[32,24,128]{2,1,0:T(8,128)(2,1)}), bf16[32,24,128]{2,1,0:T(8,128)(2,1)S(1)}, u32[]{:S(2)}, u32[]{:S(2)}) async-start(bf16[32,24,128]{2,1,0:T(8,128)(2,1)} %shard_map.83), calls=%async_computation | async-start | bytes 393216 | tf_op jit(solution)/shard_map/all_to_all | solution.py:269
  34.4 1.0 copy-start
  35.3 0.9 copy-start.1
  36.2 0.9 copy-start.2
  37.2 0.9 copy-start.3
  38.1 0.7 copy-start.4
  38.8 0.7 copy-start.5
  39.5 0.7 copy-start.6
  64.6 16.6 %collective-permute-start.3 = (bf16[256,512]{1,0:T(8,128)(2,1)S(1)}, bf16[256,512]{1,0:T(8,128)(2,1)S(1)}, u32[]{:S(2)}, u32[]{:S(2)}) collective-permute-start(bf16[256,512]{1,0:T(8,128)(2,1)S(1)} %shard_map.86.refs_0_), channel_id=1, source_target_pairs={{0,2},{1,3},{2,4},{3,5},{4,6},{5,7},{6,0},{7,1},{8,10},{9,11},{10,... | collective-permute-start | bytes 786440 | tf_op jit(solution)/shard_map/ppermute | solution.py:211
  69.8 17.1 %collective-permute-start.4 = (bf16[256,512]{1,0:T(8,128)(2,1)S(1)}, bf16[256,512]{1,0:T(8,128)(2,1)S(1)}, u32[]{:S(2)}, u32[]{:S(2)}) collective-permute-start(bf16[256,512]{1,0:T(8,128)(2,1)S(1)} %shard_map.86.refs_0_), channel_id=1, source_target_pairs={{0,6},{1,7},{2,0},{3,1},{4,2},{5,3},{6,4},{7,5},{8,14},{9,15},{10,... | collective-permute-start | bytes 786440 | tf_op jit(solution)/shard_map/ppermute | solution.py:211
  72.0 16.9 %collective-permute-start.1 = (bf16[256,512]{1,0:T(8,128)(2,1)S(1)}, bf16[256,512]{1,0:T(8,128)(2,1)S(1)}, u32[]{:S(2)}, u32[]{:S(2)}) collective-permute-start(bf16[256,512]{1,0:T(8,128)(2,1)S(1)} %shard_map.86.refs_0_), channel_id=1, source_target_pairs={{0,1},{1,2},{2,3},{3,4},{4,5},{5,6},{6,7},{7,0},{8,9},{9,10},{10,1... | collective-permute-start | bytes 786440 | tf_op jit(solution)/shard_map/ppermute | solution.py:211
  76.0 15.5 %collective-permute-start.2 = (bf16[256,512]{1,0:T(8,128)(2,1)S(1)}, bf16[256,512]{1,0:T(8,128)(2,1)S(1)}, u32[]{:S(2)}, u32[]{:S(2)}) collective-permute-start(bf16[256,512]{1,0:T(8,128)(2,1)S(1)} %shard_map.86.refs_0_), channel_id=1, source_target_pairs={{0,7},{1,0},{2,1},{3,2},{4,3},{5,4},{6,5},{7,6},{8,15},{9,8},{10,9... | collective-permute-start | bytes 786440 | tf_op jit(solution)/shard_map/ppermute | solution.py:211
  81.2 21.4 %collective-permute-start.5 = (bf16[256,512]{1,0:T(8,128)(2,1)S(1)}, bf16[256,512]{1,0:T(8,128)(2,1)S(1)}, u32[]{:S(2)}, u32[]{:S(2)}) collective-permute-start(bf16[256,512]{1,0:T(8,128)(2,1)S(1)} %collective-permute-done.3.refs_3_), channel_id=1, source_target_pairs={{0,1},{1,2},{2,3},{3,4},{4,5},{5,6},{6,7},{7,0},{8,9},{9,10},{10,1... | collective-permute-start | bytes 786440 | tf_op jit(solution)/shard_map/ppermute | solution.py:211
  86.9 15.7 %collective-permute-start.6 = (bf16[256,512]{1,0:T(8,128)(2,1)S(1)}, bf16[256,512]{1,0:T(8,128)(2,1)S(1)}, u32[]{:S(2)}, u32[]{:S(2)}) collective-permute-start(bf16[256,512]{1,0:T(8,128)(2,1)S(1)} %collective-permute-done.4.refs_4_), channel_id=1, source_target_pairs={{0,7},{1,0},{2,1},{3,2},{4,3},{5,4},{6,5},{7,6},{8,15},{9,8},{10,9... | collective-permute-start | bytes 786440 | tf_op jit(solution)/shard_map/ppermute | solution.py:211
  91.5 8.1 %collective-permute-start.7 = (bf16[128,512]{1,0:T(8,128)(2,1)S(1)}, bf16[128,512]{1,0:T(8,128)(2,1)S(1)}, u32[]{:S(2)}, u32[]{:S(2)}) collective-permute-start(bf16[128,512]{1,0:T(8,128)(2,1)S(1)} %slice.8), channel_id=1, source_target_pairs={{0,2},{1,3},{2,4},{3,5},{4,6},{5,7},{6,0},{7,1},{8,10},{9,11},{10,... | collective-permute-start | bytes 393224 | tf_op jit(solution)/shard_map/ppermute | solution.py:211
  95.9 6.7 %collective-permute-start.8 = (bf16[128,512]{1,0:T(8,128)(2,1)S(1)}, bf16[128,512]{1,0:T(8,128)(2,1)S(1)}, u32[]{:S(2)}, u32[]{:S(2)}) collective-permute-start(bf16[128,512]{1,0:T(8,128)(2,1)S(1)} %slice.9), channel_id=1, source_target_pairs={{0,6},{1,7},{2,0},{3,1},{4,2},{5,3},{6,4},{7,5},{8,14},{9,15},{10,... | collective-permute-start | bytes 393224 | tf_op jit(solution)/shard_map/ppermute | solution.py:211
Sparse Core Ops, SparseCore 0:
  24.8 87.7 all-gather.4

commit v3 on v2

--- a/solution.py
+++ b/solution.py
@@ -64,7 +64,7 @@
     return end_max, decay
 
 
-def front_kernel(key_hbm, value_hbm, in_hbm, forget_hbm, tiles_ref, cum_ref, keys, values, gates_in, gates, semaphores):
+def front_kernel(key_hbm, value_hbm, in_hbm, forget_hbm, tiles_ref, rows_ref, keys, values, gates_in, gates, semaphores):
     copies = fetch((forget_hbm, in_hbm, key_hbm, value_hbm), (gates, gates_in, keys, values), semaphores)
     length = keys.shape[0]
     copies[0].wait()
@@ -75,9 +75,10 @@
     after = lax.broadcasted_iota(jnp.int32, (length, length), 1)
     upper = jnp.where(before <= after, 1.0, 0.0).astype(F32)
     cum = jnp.dot(log_forget, upper, precision=lax.Precision.HIGHEST, preferred_element_type=F32)
-    cum_ref[...] = cum
+    rows_ref[0:8] = cum
     decay = cum[0:1, length - 1 : length]
     copies[1].wait()
+    rows_ref[8:16] = jnp.broadcast_to(gates_in[...], (8, length))
     end_weight = decay - cum[0:1] + gates_in[...]
     end_max = jnp.max(end_weight, axis=1, keepdims=True)
     copies[2].wait()
@@ -128,35 +129,30 @@
 
 
 def block_kernel(
-    query_hbm, key_hbm, value_hbm, in_hbm, gate_hbm, gain_hbm, cum_ref,
-    intra_ref, query_ref, gate_ref, stats_ref, keys, values, gates_in, gates, gains, semaphores
+    query_hbm, key_hbm, value_hbm, rows_ref, intra_ref, query_ref, stats_ref, keys, values, semaphores
 ):
-    copies = fetch(
-        (in_hbm, query_hbm, key_hbm, value_hbm, gate_hbm, gain_hbm),
-        (gates_in, query_ref, keys, values, gates, gains),
-        semaphores,
-    )
+    copies = fetch((query_hbm, key_hbm, value_hbm), (query_ref, keys, values), semaphores)
     length, width = query_ref.shape
-    cum_row = cum_ref[0:1]
-    cum_col = cum_ref[...].T[:, 0:1]
+    cum_row = rows_ref[0:1]
+    cum_col = rows_ref[0:8].T[:, 0:1]
     at = lax.broadcasted_iota(jnp.int32, (length, length), 0)
     by = lax.broadcasted_iota(jnp.int32, (length, length), 1)
-    copies[0].wait()
-    log_weight = jnp.where(at >= by, cum_col - cum_row + gates_in[...], NEG)
+    log_weight = jnp.where(at >= by, cum_col - cum_row + rows_ref[8:9], NEG)
     local_max = jnp.max(log_weight, axis=1, keepdims=True)
     lane = lax.broadcasted_iota(jnp.int32, stats_ref.shape, 1)
     stats_ref[...] = jnp.where(lane == 0, cum_col, local_max)
+    copies[0].wait()
     copies[1].wait()
-    copies[2].wait()
     scores = lax.dot_general(
         query_ref[...], keys[...], (((1,), (1,)), ((), ())), preferred_element_type=F32
     ) * (1.0 / math.sqrt(width))
     weights = (jnp.exp(log_weight - local_max) * scores).astype(BF16)
-    copies[3].wait()
+    copies[2].wait()
     intra_ref[...] = jnp.dot(weights, values[...], preferred_element_type=F32)
-    copies[4].wait()
-    copies[5].wait()
-    gate_ref[...] = gains[...] * jax.nn.sigmoid(gates[...].astype(F32))
+
+
+def gate_kernel(gain_ref, gate_ref, out_ref):
+    out_ref[...] = gain_ref[...] * jax.nn.sigmoid(gate_ref[...].astype(F32))
 
 
 def memory_kernel(
@@ -187,23 +183,36 @@
     normed_ref[...] = (centred * lax.rsqrt(spread + 1e-06) * gate_ref[...]).astype(BF16)
 
 
-def project_kernel(heads, slot_ref, *refs):
-    normed, weight_hbm, out_ref, weight, semaphores = refs[:heads], *refs[heads:]
+def head_product(normed, weight):
+    rows = weight.reshape(-1, weight.shape[-1])
+    return lax.dot_general(normed, rows, (((1,), (1,)), ((), ())), preferred_element_type=F32)
+
+
+def project_kernel(where_ref, weight_hbm, *refs):
+    normed, (total_ref, last_ref, weight, semaphores) = refs[:-4], refs[-4:]
     copies = [
-        pltpu.make_async_copy(weight_hbm.at[slot_ref[place]], weight.at[place], semaphores.at[place])
-        for place in range(heads)
+        pltpu.make_async_copy(
+            weight_hbm.at[where_ref[2 * place], :, where_ref[2 * place + 1]],
+            weight.at[place] if place < len(normed) else last_ref,
+            semaphores.at[place],
+        )
+        for place in range(len(normed) + 1)
     ]
     for copy in copies:
         copy.start()
-    width = normed[0].shape[1]
-    total = jnp.zeros(out_ref.shape, F32)
-    for place in range(heads):
+    total = jnp.zeros(total_ref.shape, F32)
+    for place, block in enumerate(normed):
         copies[place].wait()
-        rows = weight[place].reshape(out_ref.shape[1], width)
-        total += lax.dot_general(
-            normed[place][...], rows, (((1,), (1,)), ((), ())), preferred_element_type=F32
-        )
-    out_ref[...] = total.astype(BF16)
+        total += head_product(block[...], weight[place])
+    total_ref[...] = total
+    copies[-1].wait()
+
+
+def finish_kernel(total_ref, weight_ref, first_ref, last_ref, out_ref):
+    half = first_ref.shape[0]
+    for start, part in ((0, first_ref), (half, last_ref)):
+        rows = pl.ds(start, half)
+        out_ref[rows] = (total_ref[rows] + head_product(part[...], weight_ref[...])).astype(BF16)
 
 
 def head_gather(block, axis, size):
@@ -225,8 +234,7 @@
             right, left = shift(block, 1), shift(block, -1)
             gathered += [(-1, right), (1, left)]
         opposite = [shift(right[:half], 1), shift(left[half:], -1)]
-    gathered.append((size // 2, jnp.concatenate(opposite, axis=0)))
-    return gathered
+    return gathered, opposite
 
 
 def local(sizes, queries, key_rows, value_rows, input_gate, forget_gate, norm_gain, output_gate, out_weight):
@@ -240,16 +248,23 @@
     count = key_width * value_width // (TILE[0] * TILE[1])
     per = count // 2 // chips
 
-    swap = [
-        (z * heads + h, ((h + heads // 2) % heads) * heads + z)
-        for z in range(planes)
-        for h in range(heads)
+    offsets = (heads // 2, heads // 2 + 1)
+    shards = [
+        lax.ppermute(
+            out_weight.T,
+            ("z", "y"),
+            [
+                (z * heads + h, (h + offset) % heads * heads + z)
+                for z in range(planes)
+                for h in range(heads)
+            ],
+        )
+        for offset in offsets
     ]
-    weight = lax.ppermute(out_weight.T, ("z", "y"), swap)
     tile_array = functools.partial(jax.ShapeDtypeStruct, dtype=BF16)
-    state_tiles, cum = call(
+    state_tiles, rows = call(
         front_kernel,
-        (tile_array((count + 1, *TILE)), jax.ShapeDtypeStruct((8, length), F32)),
+        (tile_array((count + 1, *TILE)), jax.ShapeDtypeStruct((16, length), F32)),
         "hhhh",
         [
             pltpu.VMEM(key_rows.shape, BF16),
@@ -262,30 +277,30 @@
     )(key_rows, value_rows, input_gate, forget_gate)
     both = lax.all_gather(state_tiles, "c")
     send = call(pair_kernel, tile_array((chips, per * TILE[0] + 8, TILE[1])), "sv")(core[None], both)
-    weight, send = lax.optimization_barrier((weight, send))
-    weight = lax.all_gather(weight, ("z", "x", "c"))
-    weight = weight.reshape(planes, columns * cores, *weight.shape[-2:])
+    shards, send = lax.optimization_barrier((shards, send))
+    groups = [
+        [(z * columns + x) * cores + c for z in range(first, planes, 2) for x in range(columns) for c in range(cores)]
+        for first in range(2)
+    ]
+    weight = lax.all_gather(jnp.concatenate(shards, axis=0), ("z", "x", "c"), axis_index_groups=groups)
+    weight = weight.reshape(planes // 2, columns * cores, 2, *out_weight.shape[::-1])
 
     held = lax.all_to_all(send, ("z", "x"), 0, 0, tiled=True)
-    intra, query_held, gates, stats = call(
+    intra, query_held, stats = call(
         block_kernel,
         (
             jax.ShapeDtypeStruct(value_rows.shape, F32),
             jax.ShapeDtypeStruct(queries.shape, BF16),
-            jax.ShapeDtypeStruct(value_rows.shape, F32),
             jax.ShapeDtypeStruct((length, 128), F32),
         ),
-        "hhhhhhv",
+        "hhhv",
         [
             pltpu.VMEM(key_rows.shape, BF16),
             pltpu.VMEM(value_rows.shape, BF16),
-            pltpu.VMEM(input_gate.shape, F32),
-            pltpu.VMEM(output_gate.shape, BF16),
-            pltpu.VMEM((1, value_width), F32),
-            pltpu.SemaphoreType.DMA((6,)),
+            pltpu.SemaphoreType.DMA((3,)),
         ],
         flops=2 * length * length * (key_width + value_width),
-    )(queries, key_rows, value_rows, input_gate, output_gate, norm_gain[None], cum)
+    )(queries, key_rows, value_rows, rows)
     held, intra = lax.optimization_barrier((held, intra))
     starts, start_max = call(
         prefix_kernel,
@@ -294,6 +309,10 @@
         [pltpu.VMEM((chips, 8, TILE[1]), F32)],
     )(chip[None], held)
     back = lax.all_to_all(starts, ("z", "x"), 0, 0, tiled=True)
+    gates = call(gate_kernel, jax.ShapeDtypeStruct(value_rows.shape, F32), "vv", moved=2**20)(
+        norm_gain[None], output_gate
+    )
+    back, gates = lax.optimization_barrier((back, gates))
     start_tiles = lax.all_gather(back, "c").reshape(count, *TILE)
     normed = call(
         memory_kernel,
@@ -301,18 +320,28 @@
         "svvvvvvv",
         [pltpu.VMEM((key_width, value_width), BF16)],
     )(core[None], intra, query_held, gates, stats, start_tiles, both, start_max)
-    gathered = head_gather(normed, "y", heads)
-    slots = jnp.stack([(head + place + heads // 2) % heads for place, _ in gathered])
-    return call(
-        functools.partial(project_kernel, heads),
-        tile_array((length, value_width)),
-        "s" + "v" * heads + "h",
+    gathered, opposite = head_gather(normed, "y", heads)
+    parity = lax.axis_index("z") % 2
+    where = []
+    for place in [place for place, _ in gathered] + [heads // 2]:
+        owners = [(head + place + offset) % heads for offset in offsets]
+        part = (owners[0] % 2 != parity).astype(jnp.int32)
+        where += [jnp.where(part == 0, owners[0], owners[1]) // 2, part]
+    total, last = call(
+        project_kernel,
+        (
+            jax.ShapeDtypeStruct((length, value_width), F32),
+            tile_array((columns * cores, *weight.shape[3:])),
+        ),
+        "sh" + "v" * len(gathered),
         [
-            pltpu.VMEM((heads, columns * cores, *weight.shape[-2:]), BF16),
-            pltpu.SemaphoreType.DMA((heads,)),
+            pltpu.VMEM((len(gathered), columns * cores, *weight.shape[3:]), BF16),
+            pltpu.SemaphoreType.DMA((len(gathered) + 1,)),
         ],
         flops=2 * length * value_width * value_width * heads,
-    )(slots.astype(jnp.int32), *[block for _, block in gathered], weight)
+        moved=2**23,
+    )(jnp.stack(where).astype(jnp.int32), weight, *[block for _, block in gathered])
+    return call(finish_kernel, tile_array((length, value_width)), "vvvv")(total, last, *opposite)
 
 
 def solution(mesh, sizes=(8, 4, 2, 8)):

time: 124 us -> 122 us (0.984)
  blocking collectives: 22 us -> 7.95 us
  starting transfers between devices: 48.7 us -> 60.8 us
  waiting for transfers between devices: 23.6 us -> 22 us
  local copies, waits for them, and re-layouts: 6.49 us -> 5.22 us
    all_to_all x1 -> x0, blocking collectives: 15.5 us -> none  [local(): back = lax.all_to_all(starts, ('z', 'x'), 0, 0, tiled=True)]
    all_gather x1, waiting for transfers between devices: 9.93 us -> 0.02 us  [local(): lax.all_gather(jnp.concatenate(shards, axis=0), ('z', 'x', 'c'), axis_ind...]
    all_to_all x0 -> x1, waiting for transfers between devices: none -> 7.54 us  [local(): back = lax.all_to_all(starts, ('z', 'x'), 0, 0, tiled=True)]
    ppermute x1 -> x2, starting transfers between devices: 11.5 us -> 18.1 us  [local(): lax.ppermute(out_weight.T, ('z', 'y'), [(z * heads + h, (h + offset) % he...]
    all_to_all x0 -> x1, starting transfers between devices: none -> 4.19 us  [local(): back = lax.all_to_all(starts, ('z', 'x'), 0, 0, tiled=True)]
    all_to_all x1, waiting for transfers between devices: 3.45 us -> 5.75 us  [local(): held = lax.all_to_all(send, ('z', 'x'), 0, 0, tiled=True)]
    all_to_all x1, starting transfers between devices: 9.7 us -> 11.5 us  [local(): held = lax.all_to_all(send, ('z', 'x'), 0, 0, tiled=True)]
    ppermute x8, waiting for transfers between devices: 10.2 us -> 8.65 us  [shift(): lax.ppermute(value, axis, [(i, (i + by) % size) for i in range(size)])]
  transfers between devices with their start and end apart: 11 -> 13, of which waited for: 7 -> 6; matrix products, arithmetic and copies ran while one was open for 0% -> 0% of each run, Pallas kernels for 4% -> 7%
where the time goes in v3:
time: 122 us; the launch traced here: 121 us
  starting transfers between devices  60.8 us (50%)
  waiting for transfers between devices  22 us (18%)
  between operations  14.1 us (12%)
  Pallas kernels  10.2 us (8%)
  blocking collectives  7.95 us (7%)
  local copies, waits for them, and re-layouts  5.22 us (4%)
    ppermute x8, starting transfers between devices, shift(): lax.ppermute(value, axis, [(i, (i + by) % size) for i in range(size)])  26.9 us
    ppermute x2, starting transfers between devices, local(): lax.ppermute(out_weight.T, ('z', 'y'), [(z * heads + h, (h + offset) % he...  18.1 us
    all_to_all x1, starting transfers between devices, local(): held = lax.all_to_all(send, ('z', 'x'), 0, 0, tiled=True)  11.5 us
    ppermute x8, waiting for transfers between devices, shift(): lax.ppermute(value, axis, [(i, (i + by) % size) for i in range(size)])  8.65 us
    all_to_all x1, waiting for transfers between devices, local(): back = lax.all_to_all(starts, ('z', 'x'), 0, 0, tiled=True)  7.54 us
    all_to_all x1, waiting for transfers between devices, local(): held = lax.all_to_all(send, ('z', 'x'), 0, 0, tiled=True)  5.75 us
    unnamed x12, local copies, waits for them, and re-layouts  5.1 us
    all_gather x1, blocking collectives, local(): start_tiles = lax.all_gather(back, 'c').reshape(count, *TILE)  4.69 us
  transfers between devices with their start and end apart: 13, of which 6 were waited for; matrix products, arithmetic and copies ran while one was open for 0% of the time, Pallas kernels for 7%

profile of v3, /device:TPU:1, one launch (start us, length us, event | category | flops | bytes accessed | tf_op | source)
XLA Modules:
  0.0 120.8 jit_solution(6829375289814117972)
XLA Ops:
  6.5 0.0 all-gather.5.cloned.1.call-start
  6.5 11.5 %collective-permute-start = (bf16[64,512]{1,0:T(8,128)(2,1)}, bf16[64,512]{1,0:T(8,128)(2,1)S(1)}, u32[]{:S(2)}, u32[]{:S(2)}) collective-permute-start(bf16[64,512]{1,0:T(8,128)(2,1)} %bitcast.26), channel_id=1, source_target_pairs={{0,256},{1,320},{2,384},{3,448},{4,0},{5,64},{6,128},{7,192},{64,2... | collective-permute-start | bytes 196616 | tf_op jit(solution)/shard_map/ppermute | solution.py:253
  18.0 6.7 %collective-permute-start.1 = (bf16[64,512]{1,0:T(8,128)(2,1)}, bf16[64,512]{1,0:T(8,128)(2,1)S(1)}, u32[]{:S(2)}, u32[]{:S(2)}) collective-permute-start(bf16[64,512]{1,0:T(8,128)(2,1)} %bitcast.27), channel_id=1, source_target_pairs={{0,320},{1,384},{2,448},{3,0},{4,64},{5,128},{6,192},{7,256},{64,3... | collective-permute-start | bytes 196616 | tf_op jit(solution)/shard_map/ppermute | solution.py:253
  24.7 2.3 %shard_map.82 = (bf16[65,16,128]{2,1,0:T(8,128)(2,1)}, f32[16,256]{1,0:T(8,128)}) custom-call(bf16[256,256]{1,0:T(8,128)(2,1)} %key_hbm.3, bf16[256,512]{1,0:T(8,128)(2,1)} %value_hbm.3, f32[1,256]{1,0:T(1,128)} %in_hbm.1, f32[1,256]{1,0:T(1,128)} %forget_hbm.1), custom_call_target="tpu_custom_call" | custom-call | bytes 1048576 | tf_op jit(solution)/shard_map/pallas_call | solution.py:265
  26.9 3.3 %all-gather = bf16[130,16,128]{2,1,0:T(8,128)(2,1)S(1)} all-gather(bf16[65,16,128]{2,1,0:T(8,128)(2,1)} %get-tuple-element.23), channel_id=2, replica_groups=mesh['z'=8,'x'=4,'c'=2,'y'=8] {'c'}, dimensions={0}, use_global_device_ids=true | all-gather | bytes 798720 | tf_op jit(solution)/shard_map/all_gather | solution.py:278
  30.2 0.7 shard_map.83
  31.0 0.0 collective-permute-done
  31.0 0.0 collective-permute-done.1
  31.0 0.7 pad_maximum_fusion
  31.6 0.0 all-gather.5.cloned.1.call-update
  31.7 11.5 %all-to-all-start = ((bf16[32,24,128]{2,1,0:T(8,128)(2,1)}), bf16[32,24,128]{2,1,0:T(8,128)(2,1)S(1)}, u32[]{:S(2)}, u32[]{:S(2)}) async-start(bf16[32,24,128]{2,1,0:T(8,128)(2,1)} %shard_map.83), calls=%async_computation | async-start | bytes 393216 | tf_op jit(solution)/shard_map/all_to_all | solution.py:288
  43.2 0.0 copy-start
  43.2 0.9 copy-done
  44.2 0.0 copy-start.1
  44.2 0.9 copy-done.1
  45.1 0.0 copy-start.3
  45.1 0.9 copy-done.3
  46.0 0.0 copy-start.4
  46.0 0.7 copy-done.4
  46.7 1.2 shard_map.84
  47.9 5.8 %all-to-all-done.held_ref = bf16[32,24,128]{2,1,0:T(8,128)(2,1)S(1)} async-done(((bf16[32,24,128]{2,1,0:T(8,128)(2,1)}), bf16[32,24,128]{2,1,0:T(8,128)(2,1)S(1)}, u32[]{:S(2)}, u32[]{:S(2)}) %all-to-all-start) | async-done | bytes 196640 | tf_op jit(solution)/shard_map/all_to_all | solution.py:288
  53.6 0.8 shard_map.85
  54.4 4.2 %all-to-all-start.1 = ((bf16[32,16,128]{2,1,0:T(8,128)(2,1)}), bf16[32,16,128]{2,1,0:T(8,128)(2,1)S(1)}, u32[]{:S(2)}, u32[]{:S(2)}) async-start(bf16[32,16,128]{2,1,0:T(8,128)(2,1)} %get-tuple-element.32), calls=%async_computation.1 | async-start | bytes 262144 | tf_op jit(solution)/shard_map/all_to_all | solution.py:311
  58.6 0.0 copy-start.2
  58.6 0.9 copy-done.2
  59.6 0.0 copy-start.5
  59.6 0.7 copy-done.5
  60.3 0.1 shard_map.86.gate_ref
  60.3 7.5 %all-to-all-done.1 = bf16[32,16,128]{2,1,0:T(8,128)(2,1)S(1)} async-done(((bf16[32,16,128]{2,1,0:T(8,128)(2,1)}), bf16[32,16,128]{2,1,0:T(8,128)(2,1)S(1)}, u32[]{:S(2)}, u32[]{:S(2)}) %all-to-all-start.1) | async-done | bytes 131104 | tf_op jit(solution)/shard_map/all_to_all | solution.py:311
  67.9 4.7 %all-gather.2.tiles_ref = bf16[64,16,128]{2,1,0:T(8,128)(2,1)S(1)} all-gather(bf16[32,16,128]{2,1,0:T(8,128)(2,1)S(1)} %all-to-all-done.1), channel_id=4, replica_groups=mesh['z'=8,'x'=4,'c'=2,'y'=8] {'c'}, dimensions={0}, use_global_device_ids=true | all-gather | bytes 393216 | tf_op jit(solution)/shard_map/all_gather | solution.py:316
  72.6 0.6 shard_map.87.refs_0_
  73.2 2.2 %collective-permute-start.4 = (bf16[256,512]{1,0:T(8,128)(2,1)S(1)}, bf16[256,512]{1,0:T(8,128)(2,1)S(1)}, u32[]{:S(2)}, u32[]{:S(2)}) collective-permute-start(bf16[256,512]{1,0:T(8,128)(2,1)S(1)} %shard_map.87.refs_0_), channel_id=1, source_target_pairs={{0,2},{1,3},{2,4},{3,5},{4,6},{5,7},{6,0},{7,1},{8,10},{9,11},{10,... | collective-permute-start | bytes 786440 | tf_op jit(solution)/shard_map/ppermute | solution.py:220
  75.3 5.2 %collective-permute-start.5 = (bf16[256,512]{1,0:T(8,128)(2,1)S(1)}, bf16[256,512]{1,0:T(8,128)(2,1)S(1)}, u32[]{:S(2)}, u32[]{:S(2)}) collective-permute-start(bf16[256,512]{1,0:T(8,128)(2,1)S(1)} %shard_map.87.refs_0_), channel_id=1, source_target_pairs={{0,6},{1,7},{2,0},{3,1},{4,2},{5,3},{6,4},{7,5},{8,14},{9,15},{10,... | collective-permute-start | bytes 786440 | tf_op jit(solution)/shard_map/ppermute | solution.py:220
  80.6 1.9 %collective-permute-start.2 = (bf16[256,512]{1,0:T(8,128)(2,1)S(1)}, bf16[256,512]{1,0:T(8,128)(2,1)S(1)}, u32[]{:S(2)}, u32[]{:S(2)}) collective-permute-start(bf16[256,512]{1,0:T(8,128)(2,1)S(1)} %shard_map.87.refs_0_), channel_id=1, source_target_pairs={{0,1},{1,2},{2,3},{3,4},{4,5},{5,6},{6,7},{7,0},{8,9},{9,10},{10,1... | collective-permute-start | bytes 786440 | tf_op jit(solution)/shard_map/ppermute | solution.py:220
  82.5 4.6 %collective-permute-start.3 = (bf16[256,512]{1,0:T(8,128)(2,1)S(1)}, bf16[256,512]{1,0:T(8,128)(2,1)S(1)}, u32[]{:S(2)}, u32[]{:S(2)}) collective-permute-start(bf16[256,512]{1,0:T(8,128)(2,1)S(1)} %shard_map.87.refs_0_), channel_id=1, source_target_pairs={{0,7},{1,0},{2,1},{3,2},{4,3},{5,4},{6,5},{7,6},{8,15},{9,8},{10,9... | collective-permute-start | bytes 786440 | tf_op jit(solution)/shard_map/ppermute | solution.py:220
  87.1 2.7 %collective-permute-done.4.refs_3_ = bf16[256,512]{1,0:T(8,128)(2,1)S(1)} collective-permute-done((bf16[256,512]{1,0:T(8,128)(2,1)S(1)}, bf16[256,512]{1,0:T(8,128)(2,1)S(1)}, u32[]{:S(2)}, u32[]{:S(2)}) %collective-permute-start.4) | collective-permute-done | bytes 262176 | tf_op jit(solution)/shard_map/ppermute | solution.py:220
  89.7 1.9 %collective-permute-start.6 = (bf16[256,512]{1,0:T(8,128)(2,1)S(1)}, bf16[256,512]{1,0:T(8,128)(2,1)S(1)}, u32[]{:S(2)}, u32[]{:S(2)}) collective-permute-start(bf16[256,512]{1,0:T(8,128)(2,1)S(1)} %collective-permute-done.4.refs_3_), channel_id=1, source_target_pairs={{0,1},{1,2},{2,3},{3,4},{4,5},{5,6},{6,7},{7,0},{8,9},{9,10},{10,1... | collective-permute-start | bytes 786440 | tf_op jit(solution)/shard_map/ppermute | solution.py:220
  91.6 0.8 collective-permute-done.5.refs_4_
  92.5 3.7 %collective-permute-start.7 = (bf16[256,512]{1,0:T(8,128)(2,1)S(1)}, bf16[256,512]{1,0:T(8,128)(2,1)S(1)}, u32[]{:S(2)}, u32[]{:S(2)}) collective-permute-start(bf16[256,512]{1,0:T(8,128)(2,1)S(1)} %collective-permute-done.5.refs_4_), channel_id=1, source_target_pairs={{0,7},{1,0},{2,1},{3,2},{4,3},{5,4},{6,5},{7,6},{8,15},{9,8},{10,9... | collective-permute-start | bytes 786440 | tf_op jit(solution)/shard_map/ppermute | solution.py:220
  96.3 0.0 collective-permute-done.2.refs_1_
  96.3 2.0 %collective-permute-done.3.refs_2_ = bf16[256,512]{1,0:T(8,128)(2,1)S(1)} collective-permute-done((bf16[256,512]{1,0:T(8,128)(2,1)S(1)}, bf16[256,512]{1,0:T(8,128)(2,1)S(1)}, u32[]{:S(2)}, u32[]{:S(2)}) %collective-permute-start.3) | collective-permute-done | bytes 262176 | tf_op jit(solution)/shard_map/ppermute | solution.py:220
  98.3 3.5 %collective-permute-start.8 = (bf16[128,512]{1,0:T(8,128)(2,1)S(1)}, bf16[128,512]{1,0:T(8,128)(2,1)S(1)}, u32[]{:S(2)}, u32[]{:S(2)}) collective-permute-start(bf16[128,512]{1,0:T(8,128)(2,1)S(1)} %slice.8), channel_id=1, source_target_pairs={{0,2},{1,3},{2,4},{3,5},{4,6},{5,7},{6,0},{7,1},{8,10},{9,11},{10,... | collective-permute-start | bytes 393224 | tf_op jit(solution)/shard_map/ppermute | solution.py:220
  101.8 3.9 %collective-permute-start.9 = (bf16[128,512]{1,0:T(8,128)(2,1)S(1)}, bf16[128,512]{1,0:T(8,128)(2,1)S(1)}, u32[]{:S(2)}, u32[]{:S(2)}) collective-permute-start(bf16[128,512]{1,0:T(8,128)(2,1)S(1)} %slice.9), channel_id=1, source_target_pairs={{0,6},{1,7},{2,0},{3,1},{4,2},{5,3},{6,4},{7,5},{8,14},{9,15},{10,... | collective-permute-start | bytes 393224 | tf_op jit(solution)/shard_map/ppermute | solution.py:220
  106.1 0.1 stack.67.where_ref
  106.2 0.0 collective-permute-done.6.refs_5_
  106.3 0.0 collective-permute-done.7.refs_6_
  106.3 0.0 all-gather.5.cloned.1.call-done
  106.3 3.4 %shard_map.88 = (f32[256,512]{1,0:T(8,128)S(1)}, bf16[8,64,512]{2,1,0:T(8,128)(2,1)S(1)}) custom-call(s32[16]{0:T(128)S(1)} %stack.67.where_ref, bf16[4,8,2,64,512]{4,3,2,1,0:T(8,128)(2,1)} %bitcast.25, bf16[256,512]{1,0:T(8,128)(2,1)S(1)} %shard_map.87.refs_0_, bf16[256,512]{1,0:T(8,128)(2,1)S(1)} %collective-permute-done.2.refs_1_, ...), custom_call_target="tpu_custom_call" | custom-call | flops 1073741824 | bytes 8388608 | tf_op jit(solution)/shard_map/pallas_call | solution.py:330
  109.7 0.0 collective-permute-done.8.first_ref
  109.7 3.1 %collective-permute-done.9.last_ref = bf16[128,512]{1,0:T(8,128)(2,1)S(1)} collective-permute-done((bf16[128,512]{1,0:T(8,128)(2,1)S(1)}, bf16[128,512]{1,0:T(8,128)(2,1)S(1)}, u32[]{:S(2)}, u32[]{:S(2)}) %collective-permute-start.9) | collective-permute-done | bytes 131104 | tf_op jit(solution)/shard_map/ppermute | solution.py:220
  112.8 1.2 shard_map.89
  (2 shorter events, 0.0 us)
Async XLA Ops:
  6.5 99.8 %all-gather.5.cloned.1.call-start = ((), (), s32[]{:S(2)}) async-start(), calls=%async_computation.2 | async-start | bytes 4325376 | tf_op jit(solution)/shard_map/all_gather | solution.py:285
  6.5 24.4 %collective-permute-start = (bf16[64,512]{1,0:T(8,128)(2,1)}, bf16[64,512]{1,0:T(8,128)(2,1)S(1)}, u32[]{:S(2)}, u32[]{:S(2)}) collective-permute-start(bf16[64,512]{1,0:T(8,128)(2,1)} %bitcast.26), channel_id=1, source_target_pairs={{0,256},{1,320},{2,384},{3,448},{4,0},{5,64},{6,128},{7,192},{64,2... | collective-permute-start | bytes 196616 | tf_op jit(solution)/shard_map/ppermute | solution.py:253
  18.0 13.0 %collective-permute-start.1 = (bf16[64,512]{1,0:T(8,128)(2,1)}, bf16[64,512]{1,0:T(8,128)(2,1)S(1)}, u32[]{:S(2)}, u32[]{:S(2)}) collective-permute-start(bf16[64,512]{1,0:T(8,128)(2,1)} %bitcast.27), channel_id=1, source_target_pairs={{0,320},{1,384},{2,448},{3,0},{4,64},{5,128},{6,192},{7,256},{64,3... | collective-permute-start | bytes 196616 | tf_op jit(solution)/shard_map/ppermute | solution.py:253
  31.7 22.0 %all-to-all-start = ((bf16[32,24,128]{2,1,0:T(8,128)(2,1)}), bf16[32,24,128]{2,1,0:T(8,128)(2,1)S(1)}, u32[]{:S(2)}, u32[]{:S(2)}) async-start(bf16[32,24,128]{2,1,0:T(8,128)(2,1)} %shard_map.83), calls=%async_computation | async-start | bytes 393216 | tf_op jit(solution)/shard_map/all_to_all | solution.py:288
  43.2 1.0 copy-start
  44.2 0.9 copy-start.1
  45.1 0.9 copy-start.3
  46.0 0.7 copy-start.4
  54.4 13.5 %all-to-all-start.1 = ((bf16[32,16,128]{2,1,0:T(8,128)(2,1)}), bf16[32,16,128]{2,1,0:T(8,128)(2,1)S(1)}, u32[]{:S(2)}, u32[]{:S(2)}) async-start(bf16[32,16,128]{2,1,0:T(8,128)(2,1)} %get-tuple-element.32), calls=%async_computation.1 | async-start | bytes 262144 | tf_op jit(solution)/shard_map/all_to_all | solution.py:311
  58.6 1.0 copy-start.2
  59.6 0.7 copy-start.5
  73.2 16.6 %collective-permute-start.4 = (bf16[256,512]{1,0:T(8,128)(2,1)S(1)}, bf16[256,512]{1,0:T(8,128)(2,1)S(1)}, u32[]{:S(2)}, u32[]{:S(2)}) collective-permute-start(bf16[256,512]{1,0:T(8,128)(2,1)S(1)} %shard_map.87.refs_0_), channel_id=1, source_target_pairs={{0,2},{1,3},{2,4},{3,5},{4,6},{5,7},{6,0},{7,1},{8,10},{9,11},{10,... | collective-permute-start | bytes 786440 | tf_op jit(solution)/shard_map/ppermute | solution.py:220
  75.3 17.2 %collective-permute-start.5 = (bf16[256,512]{1,0:T(8,128)(2,1)S(1)}, bf16[256,512]{1,0:T(8,128)(2,1)S(1)}, u32[]{:S(2)}, u32[]{:S(2)}) collective-permute-start(bf16[256,512]{1,0:T(8,128)(2,1)S(1)} %shard_map.87.refs_0_), channel_id=1, source_target_pairs={{0,6},{1,7},{2,0},{3,1},{4,2},{5,3},{6,4},{7,5},{8,14},{9,15},{10,... | collective-permute-start | bytes 786440 | tf_op jit(solution)/shard_map/ppermute | solution.py:220
  80.6 15.7 %collective-permute-start.2 = (bf16[256,512]{1,0:T(8,128)(2,1)S(1)}, bf16[256,512]{1,0:T(8,128)(2,1)S(1)}, u32[]{:S(2)}, u32[]{:S(2)}) collective-permute-start(bf16[256,512]{1,0:T(8,128)(2,1)S(1)} %shard_map.87.refs_0_), channel_id=1, source_target_pairs={{0,1},{1,2},{2,3},{3,4},{4,5},{5,6},{6,7},{7,0},{8,9},{9,10},{10,1... | collective-permute-start | bytes 786440 | tf_op jit(solution)/shard_map/ppermute | solution.py:220
  82.5 15.8 %collective-permute-start.3 = (bf16[256,512]{1,0:T(8,128)(2,1)S(1)}, bf16[256,512]{1,0:T(8,128)(2,1)S(1)}, u32[]{:S(2)}, u32[]{:S(2)}) collective-permute-start(bf16[256,512]{1,0:T(8,128)(2,1)S(1)} %shard_map.87.refs_0_), channel_id=1, source_target_pairs={{0,7},{1,0},{2,1},{3,2},{4,3},{5,4},{6,5},{7,6},{8,15},{9,8},{10,9... | collective-permute-start | bytes 786440 | tf_op jit(solution)/shard_map/ppermute | solution.py:220
  89.7 16.5 %collective-permute-start.6 = (bf16[256,512]{1,0:T(8,128)(2,1)S(1)}, bf16[256,512]{1,0:T(8,128)(2,1)S(1)}, u32[]{:S(2)}, u32[]{:S(2)}) collective-permute-start(bf16[256,512]{1,0:T(8,128)(2,1)S(1)} %collective-permute-done.4.refs_3_), channel_id=1, source_target_pairs={{0,1},{1,2},{2,3},{3,4},{4,5},{5,6},{6,7},{7,0},{8,9},{9,10},{10,1... | collective-permute-start | bytes 786440 | tf_op jit(solution)/shard_map/ppermute | solution.py:220
  92.5 13.8 %collective-permute-start.7 = (bf16[256,512]{1,0:T(8,128)(2,1)S(1)}, bf16[256,512]{1,0:T(8,128)(2,1)S(1)}, u32[]{:S(2)}, u32[]{:S(2)}) collective-permute-start(bf16[256,512]{1,0:T(8,128)(2,1)S(1)} %collective-permute-done.5.refs_4_), channel_id=1, source_target_pairs={{0,7},{1,0},{2,1},{3,2},{4,3},{5,4},{6,5},{7,6},{8,15},{9,8},{10,9... | collective-permute-start | bytes 786440 | tf_op jit(solution)/shard_map/ppermute | solution.py:220
  98.3 11.4 %collective-permute-start.8 = (bf16[128,512]{1,0:T(8,128)(2,1)S(1)}, bf16[128,512]{1,0:T(8,128)(2,1)S(1)}, u32[]{:S(2)}, u32[]{:S(2)}) collective-permute-start(bf16[128,512]{1,0:T(8,128)(2,1)S(1)} %slice.8), channel_id=1, source_target_pairs={{0,2},{1,3},{2,4},{3,5},{4,6},{5,7},{6,0},{7,1},{8,10},{9,11},{10,... | collective-permute-start | bytes 393224 | tf_op jit(solution)/shard_map/ppermute | solution.py:220
  101.8 11.0 %collective-permute-start.9 = (bf16[128,512]{1,0:T(8,128)(2,1)S(1)}, bf16[128,512]{1,0:T(8,128)(2,1)S(1)}, u32[]{:S(2)}, u32[]{:S(2)}) collective-permute-start(bf16[128,512]{1,0:T(8,128)(2,1)S(1)} %slice.9), channel_id=1, source_target_pairs={{0,6},{1,7},{2,0},{3,1},{4,2},{5,3},{6,4},{7,5},{8,14},{9,15},{10,... | collective-permute-start | bytes 393224 | tf_op jit(solution)/shard_map/ppermute | solution.py:220
Sparse Core Ops, SparseCore 0:
  31.8 68.1 all-gather.4

commit v4 on v3

--- a/solution.py
+++ b/solution.py
@@ -226,8 +226,7 @@
         near, behind = shift(block, 1), shift(block, -1)
         gathered += [(-1, near), (1, behind), (-2, far), (2, back)]
         gathered += [(-3, shift(far, 1)), (3, shift(back, -1))]
-        first, last, _, _ = lax.optimization_barrier((far[:half], back[half:], near, behind))
-        opposite = [shift(first, 2), shift(last, -2)]
+        opposite = [shift(far[:half], 2), shift(back[half:], -2)]
     else:
         right = left = block
         if size == 4:
@@ -248,7 +247,7 @@
     count = key_width * value_width // (TILE[0] * TILE[1])
     per = count // 2 // chips
 
-    offsets = (heads // 2, heads // 2 + 1)
+    offsets = (heads // 2 + 1, heads // 2)
     shards = [
         lax.ppermute(
             out_weight.T,

time: 122 us -> 118 us (0.967)
  waiting for transfers between devices: 22 us -> 17.2 us
  blocking collectives: 7.95 us -> 10.5 us
  starting transfers between devices: 60.8 us -> 58.7 us
    all_to_all x1, starting transfers between devices: 11.5 us -> 7.04 us  [local(): held = lax.all_to_all(send, ('z', 'x'), 0, 0, tiled=True)]
    ppermute x8, waiting for transfers between devices: 8.65 us -> 4.19 us  [shift(): lax.ppermute(value, axis, [(i, (i + by) % size) for i in range(size)])]
    all_gather x1, blocking collectives: 4.69 us -> 7.2 us  [local(): start_tiles = lax.all_gather(back, 'c').reshape(count, *TILE)]
    ppermute x2, starting transfers between devices: 18.1 us -> 19.8 us  [local(): lax.ppermute(out_weight.T, ('z', 'y'), [(z * heads + h, (h + offset) % he...]
  transfers between devices with their start and end apart: 13 -> 13, of which waited for: 6 -> 5; matrix products, arithmetic and copies ran while one was open for 0% -> 0% of each run, Pallas kernels for 7% -> 8%
where the time goes in v4:
time: 118 us; the launch traced here: 117 us
  starting transfers between devices  58.7 us (50%)
  waiting for transfers between devices  17.2 us (15%)
  between operations  14.1 us (12%)
  blocking collectives  10.5 us (9%)
  Pallas kernels  10.2 us (9%)
  local copies, waits for them, and re-layouts  5.22 us (4%)
    ppermute x8, starting transfers between devices, shift(): lax.ppermute(value, axis, [(i, (i + by) % size) for i in range(size)])  27.9 us
    ppermute x2, starting transfers between devices, local(): lax.ppermute(out_weight.T, ('z', 'y'), [(z * heads + h, (h + offset) % he...  19.8 us
    all_to_all x1, waiting for transfers between devices, local(): back = lax.all_to_all(starts, ('z', 'x'), 0, 0, tiled=True)  7.72 us
    all_gather x1, blocking collectives, local(): start_tiles = lax.all_gather(back, 'c').reshape(count, *TILE)  7.2 us
    all_to_all x1, starting transfers between devices, local(): held = lax.all_to_all(send, ('z', 'x'), 0, 0, tiled=True)  7.04 us
    all_to_all x1, waiting for transfers between devices, local(): held = lax.all_to_all(send, ('z', 'x'), 0, 0, tiled=True)  5.27 us
    unnamed x12, local copies, waits for them, and re-layouts  5.1 us
    ppermute x8, waiting for transfers between devices, shift(): lax.ppermute(value, axis, [(i, (i + by) % size) for i in range(size)])  4.19 us
  transfers between devices with their start and end apart: 13, of which 5 were waited for; matrix products, arithmetic and copies ran while one was open for 0% of the time, Pallas kernels for 8%

profile of v4, /device:TPU:1, one launch (start us, length us, event | category | flops | bytes accessed | tf_op | source)
XLA Modules:
  0.0 116.5 jit_solution(5972149960036204838)
XLA Ops:
  6.5 0.0 all-gather.5.cloned.1.call-start
  6.5 11.5 %collective-permute-start = (bf16[64,512]{1,0:T(8,128)(2,1)}, bf16[64,512]{1,0:T(8,128)(2,1)S(1)}, u32[]{:S(2)}, u32[]{:S(2)}) collective-permute-start(bf16[64,512]{1,0:T(8,128)(2,1)} %bitcast.26), channel_id=1, source_target_pairs={{0,320},{1,384},{2,448},{3,0},{4,64},{5,128},{6,192},{7,256},{64,3... | collective-permute-start | bytes 196616 | tf_op jit(solution)/shard_map/ppermute | solution.py:252
  18.0 8.4 %collective-permute-start.1 = (bf16[64,512]{1,0:T(8,128)(2,1)}, bf16[64,512]{1,0:T(8,128)(2,1)S(1)}, u32[]{:S(2)}, u32[]{:S(2)}) collective-permute-start(bf16[64,512]{1,0:T(8,128)(2,1)} %bitcast.27), channel_id=1, source_target_pairs={{0,256},{1,320},{2,384},{3,448},{4,0},{5,64},{6,128},{7,192},{64,2... | collective-permute-start | bytes 196616 | tf_op jit(solution)/shard_map/ppermute | solution.py:252
  26.4 2.3 %shard_map.82 = (bf16[65,16,128]{2,1,0:T(8,128)(2,1)}, f32[16,256]{1,0:T(8,128)}) custom-call(bf16[256,256]{1,0:T(8,128)(2,1)} %key_hbm.3, bf16[256,512]{1,0:T(8,128)(2,1)} %value_hbm.3, f32[1,256]{1,0:T(1,128)} %in_hbm.1, f32[1,256]{1,0:T(1,128)} %forget_hbm.1), custom_call_target="tpu_custom_call" | custom-call | bytes 1048576 | tf_op jit(solution)/shard_map/pallas_call | solution.py:264
  28.6 3.3 %all-gather = bf16[130,16,128]{2,1,0:T(8,128)(2,1)S(1)} all-gather(bf16[65,16,128]{2,1,0:T(8,128)(2,1)} %get-tuple-element.21), channel_id=2, replica_groups=mesh['z'=8,'x'=4,'c'=2,'y'=8] {'c'}, dimensions={0}, use_global_device_ids=true | all-gather | bytes 798720 | tf_op jit(solution)/shard_map/all_gather | solution.py:277
  31.9 0.7 shard_map.83
  32.6 0.0 collective-permute-done
  32.6 0.0 collective-permute-done.1
  32.7 0.7 pad_maximum_fusion
  33.3 0.0 all-gather.5.cloned.1.call-update
  33.3 7.0 %all-to-all-start = ((bf16[32,24,128]{2,1,0:T(8,128)(2,1)}), bf16[32,24,128]{2,1,0:T(8,128)(2,1)S(1)}, u32[]{:S(2)}, u32[]{:S(2)}) async-start(bf16[32,24,128]{2,1,0:T(8,128)(2,1)} %shard_map.83), calls=%async_computation | async-start | bytes 393216 | tf_op jit(solution)/shard_map/all_to_all | solution.py:287
  40.4 0.0 copy-start
  40.4 0.9 copy-done
  41.4 0.0 copy-start.1
  41.4 0.9 copy-done.1
  42.3 0.0 copy-start.3
  42.3 0.9 copy-done.3
  43.2 0.0 copy-start.4
  43.2 0.7 copy-done.4
  43.9 1.2 %shard_map.84 = (f32[256,512]{1,0:T(8,128)S(1)}, bf16[256,256]{1,0:T(8,128)(2,1)S(1)}, f32[256,128]{1,0:T(8,128)S(1)}) custom-call(bf16[256,256]{1,0:T(8,128)(2,1)S(1)} %copy-done.3, bf16[256,256]{1,0:T(8,128)(2,1)S(1)} %copy-done.1, bf16[256,512]{1,0:T(8,128)(2,1)S(1)} %copy-done, f32[16,256]{1,0:T(8,128)S(1)} %copy-done.4), custom_call_target="tpu_custom_call" | custom-call | flops 100663296 | bytes 1048576 | tf_op jit(solution)/shard_map/pallas_call | solution.py:288
  45.1 5.3 %all-to-all-done.held_ref = bf16[32,24,128]{2,1,0:T(8,128)(2,1)S(1)} async-done(((bf16[32,24,128]{2,1,0:T(8,128)(2,1)}), bf16[32,24,128]{2,1,0:T(8,128)(2,1)S(1)}, u32[]{:S(2)}, u32[]{:S(2)}) %all-to-all-start) | async-done | bytes 196640 | tf_op jit(solution)/shard_map/all_to_all | solution.py:287
  50.4 0.8 shard_map.85
  51.1 4.0 %all-to-all-start.1 = ((bf16[32,16,128]{2,1,0:T(8,128)(2,1)}), bf16[32,16,128]{2,1,0:T(8,128)(2,1)S(1)}, u32[]{:S(2)}, u32[]{:S(2)}) async-start(bf16[32,16,128]{2,1,0:T(8,128)(2,1)} %get-tuple-element.30), calls=%async_computation.1 | async-start | bytes 262144 | tf_op jit(solution)/shard_map/all_to_all | solution.py:310
  55.1 0.0 copy-start.2
  55.1 0.9 copy-done.2
  56.1 0.0 copy-start.5
  56.1 0.7 copy-done.5
  56.7 0.1 shard_map.86.gate_ref
  56.8 7.7 %all-to-all-done.1 = bf16[32,16,128]{2,1,0:T(8,128)(2,1)S(1)} async-done(((bf16[32,16,128]{2,1,0:T(8,128)(2,1)}), bf16[32,16,128]{2,1,0:T(8,128)(2,1)S(1)}, u32[]{:S(2)}, u32[]{:S(2)}) %all-to-all-start.1) | async-done | bytes 131104 | tf_op jit(solution)/shard_map/all_to_all | solution.py:310
  64.5 7.2 %all-gather.2.tiles_ref = bf16[64,16,128]{2,1,0:T(8,128)(2,1)S(1)} all-gather(bf16[32,16,128]{2,1,0:T(8,128)(2,1)S(1)} %all-to-all-done.1), channel_id=4, replica_groups=mesh['z'=8,'x'=4,'c'=2,'y'=8] {'c'}, dimensions={0}, use_global_device_ids=true | all-gather | bytes 393216 | tf_op jit(solution)/shard_map/all_gather | solution.py:315
  71.7 0.6 shard_map.87.refs_0_
  72.3 4.0 %collective-permute-start.4 = (bf16[256,512]{1,0:T(8,128)(2,1)S(1)}, bf16[256,512]{1,0:T(8,128)(2,1)S(1)}, u32[]{:S(2)}, u32[]{:S(2)}) collective-permute-start(bf16[256,512]{1,0:T(8,128)(2,1)S(1)} %shard_map.87.refs_0_), channel_id=1, source_target_pairs={{0,2},{1,3},{2,4},{3,5},{4,6},{5,7},{6,0},{7,1},{8,10},{9,11},{10,... | collective-permute-start | bytes 786440 | tf_op jit(solution)/shard_map/ppermute | solution.py:220
  76.4 3.4 %collective-permute-start.5 = (bf16[256,512]{1,0:T(8,128)(2,1)S(1)}, bf16[256,512]{1,0:T(8,128)(2,1)S(1)}, u32[]{:S(2)}, u32[]{:S(2)}) collective-permute-start(bf16[256,512]{1,0:T(8,128)(2,1)S(1)} %shard_map.87.refs_0_), channel_id=1, source_target_pairs={{0,6},{1,7},{2,0},{3,1},{4,2},{5,3},{6,4},{7,5},{8,14},{9,15},{10,... | collective-permute-start | bytes 786440 | tf_op jit(solution)/shard_map/ppermute | solution.py:220
  79.7 2.8 %collective-permute-start.2 = (bf16[256,512]{1,0:T(8,128)(2,1)S(1)}, bf16[256,512]{1,0:T(8,128)(2,1)S(1)}, u32[]{:S(2)}, u32[]{:S(2)}) collective-permute-start(bf16[256,512]{1,0:T(8,128)(2,1)S(1)} %shard_map.87.refs_0_), channel_id=1, source_target_pairs={{0,1},{1,2},{2,3},{3,4},{4,5},{5,6},{6,7},{7,0},{8,9},{9,10},{10,1... | collective-permute-start | bytes 786440 | tf_op jit(solution)/shard_map/ppermute | solution.py:220
  82.5 3.7 %collective-permute-start.3 = (bf16[256,512]{1,0:T(8,128)(2,1)S(1)}, bf16[256,512]{1,0:T(8,128)(2,1)S(1)}, u32[]{:S(2)}, u32[]{:S(2)}) collective-permute-start(bf16[256,512]{1,0:T(8,128)(2,1)S(1)} %shard_map.87.refs_0_), channel_id=1, source_target_pairs={{0,7},{1,0},{2,1},{3,2},{4,3},{5,4},{6,5},{7,6},{8,15},{9,8},{10,9... | collective-permute-start | bytes 786440 | tf_op jit(solution)/shard_map/ppermute | solution.py:220
  86.2 3.3 %collective-permute-done.4.refs_3_ = bf16[256,512]{1,0:T(8,128)(2,1)S(1)} collective-permute-done((bf16[256,512]{1,0:T(8,128)(2,1)S(1)}, bf16[256,512]{1,0:T(8,128)(2,1)S(1)}, u32[]{:S(2)}, u32[]{:S(2)}) %collective-permute-start.4) | collective-permute-done | bytes 262176 | tf_op jit(solution)/shard_map/ppermute | solution.py:220
  89.5 1.9 %collective-permute-start.6 = (bf16[256,512]{1,0:T(8,128)(2,1)S(1)}, bf16[256,512]{1,0:T(8,128)(2,1)S(1)}, u32[]{:S(2)}, u32[]{:S(2)}) collective-permute-start(bf16[256,512]{1,0:T(8,128)(2,1)S(1)} %collective-permute-done.4.refs_3_), channel_id=1, source_target_pairs={{0,1},{1,2},{2,3},{3,4},{4,5},{5,6},{6,7},{7,0},{8,9},{9,10},{10,1... | collective-permute-start | bytes 786440 | tf_op jit(solution)/shard_map/ppermute | solution.py:220
  91.4 0.3 collective-permute-done.5.refs_4_
  91.8 4.7 %collective-permute-start.7 = (bf16[256,512]{1,0:T(8,128)(2,1)S(1)}, bf16[256,512]{1,0:T(8,128)(2,1)S(1)}, u32[]{:S(2)}, u32[]{:S(2)}) collective-permute-start(bf16[256,512]{1,0:T(8,128)(2,1)S(1)} %collective-permute-done.5.refs_4_), channel_id=1, source_target_pairs={{0,7},{1,0},{2,1},{3,2},{4,3},{5,4},{6,5},{7,6},{8,15},{9,8},{10,9... | collective-permute-start | bytes 786440 | tf_op jit(solution)/shard_map/ppermute | solution.py:220
  96.5 2.7 %collective-permute-start.8 = (bf16[128,512]{1,0:T(8,128)(2,1)S(1)}, bf16[128,512]{1,0:T(8,128)(2,1)S(1)}, u32[]{:S(2)}, u32[]{:S(2)}) collective-permute-start(bf16[128,512]{1,0:T(8,128)(2,1)S(1)} %slice.8), channel_id=1, source_target_pairs={{0,2},{1,3},{2,4},{3,5},{4,6},{5,7},{6,0},{7,1},{8,10},{9,11},{10,... | collective-permute-start | bytes 393224 | tf_op jit(solution)/shard_map/ppermute | solution.py:220
  99.2 0.0 collective-permute-done.2.refs_1_
  99.2 4.7 %collective-permute-start.9 = (bf16[128,512]{1,0:T(8,128)(2,1)S(1)}, bf16[128,512]{1,0:T(8,128)(2,1)S(1)}, u32[]{:S(2)}, u32[]{:S(2)}) collective-permute-start(bf16[128,512]{1,0:T(8,128)(2,1)S(1)} %slice.9), channel_id=1, source_target_pairs={{0,6},{1,7},{2,0},{3,1},{4,2},{5,3},{6,4},{7,5},{8,14},{9,15},{10,... | collective-permute-start | bytes 393224 | tf_op jit(solution)/shard_map/ppermute | solution.py:220
  104.3 0.1 stack.67.where_ref
  104.4 0.0 collective-permute-done.3.refs_2_
  104.5 0.0 collective-permute-done.6.refs_5_
  104.5 0.0 collective-permute-done.7.refs_6_
  104.5 0.0 all-gather.5.cloned.1.call-done
  104.5 3.4 %shard_map.88 = (f32[256,512]{1,0:T(8,128)S(1)}, bf16[8,64,512]{2,1,0:T(8,128)(2,1)S(1)}) custom-call(s32[16]{0:T(128)S(1)} %stack.67.where_ref, bf16[4,8,2,64,512]{4,3,2,1,0:T(8,128)(2,1)} %bitcast.25, bf16[256,512]{1,0:T(8,128)(2,1)S(1)} %shard_map.87.refs_0_, bf16[256,512]{1,0:T(8,128)(2,1)S(1)} %collective-permute-done.2.refs_1_, ...), custom_call_target="tpu_custom_call" | custom-call | flops 1073741824 | bytes 8388608 | tf_op jit(solution)/shard_map/pallas_call | solution.py:329
  107.9 0.0 collective-permute-done.8.first_ref
  107.9 0.6 collective-permute-done.9.last_ref
  108.5 1.2 %shard_map.89 = bf16[256,512]{1,0:T(8,128)(2,1)} custom-call(f32[256,512]{1,0:T(8,128)S(1)} %get-tuple-element.35.total_ref, bf16[8,64,512]{2,1,0:T(8,128)(2,1)S(1)} %get-tuple-element.36.weight_ref, bf16[128,512]{1,0:T(8,128)(2,1)S(1)} %collective-permute-done.8.first_ref, bf16[128,512]{1,0:T(8,128)(2,1)S(1)} %collective-permute-done.9.last_ref), custom_call_target="tpu_custom_call" | custom-call | bytes 1048576 | tf_op jit(solution)/shard_map/pallas_call | solution.py:343
  (2 shorter events, 0.0 us)
Async XLA Ops:
  6.5 98.0 %all-gather.5.cloned.1.call-start = ((), (), s32[]{:S(2)}) async-start(), calls=%async_computation.2 | async-start | bytes 4325376 | tf_op jit(solution)/shard_map/all_gather | solution.py:284
  6.5 26.1 %collective-permute-start = (bf16[64,512]{1,0:T(8,128)(2,1)}, bf16[64,512]{1,0:T(8,128)(2,1)S(1)}, u32[]{:S(2)}, u32[]{:S(2)}) collective-permute-start(bf16[64,512]{1,0:T(8,128)(2,1)} %bitcast.26), channel_id=1, source_target_pairs={{0,320},{1,384},{2,448},{3,0},{4,64},{5,128},{6,192},{7,256},{64,3... | collective-permute-start | bytes 196616 | tf_op jit(solution)/shard_map/ppermute | solution.py:252
  18.0 14.6 %collective-permute-start.1 = (bf16[64,512]{1,0:T(8,128)(2,1)}, bf16[64,512]{1,0:T(8,128)(2,1)S(1)}, u32[]{:S(2)}, u32[]{:S(2)}) collective-permute-start(bf16[64,512]{1,0:T(8,128)(2,1)} %bitcast.27), channel_id=1, source_target_pairs={{0,256},{1,320},{2,384},{3,448},{4,0},{5,64},{6,128},{7,192},{64,2... | collective-permute-start | bytes 196616 | tf_op jit(solution)/shard_map/ppermute | solution.py:252
  33.3 17.0 %all-to-all-start = ((bf16[32,24,128]{2,1,0:T(8,128)(2,1)}), bf16[32,24,128]{2,1,0:T(8,128)(2,1)S(1)}, u32[]{:S(2)}, u32[]{:S(2)}) async-start(bf16[32,24,128]{2,1,0:T(8,128)(2,1)} %shard_map.83), calls=%async_computation | async-start | bytes 393216 | tf_op jit(solution)/shard_map/all_to_all | solution.py:287
  40.4 1.0 copy-start
  41.4 0.9 copy-start.1
  42.3 0.9 copy-start.3
  43.2 0.7 copy-start.4
  51.1 13.4 %all-to-all-start.1 = ((bf16[32,16,128]{2,1,0:T(8,128)(2,1)}), bf16[32,16,128]{2,1,0:T(8,128)(2,1)S(1)}, u32[]{:S(2)}, u32[]{:S(2)}) async-start(bf16[32,16,128]{2,1,0:T(8,128)(2,1)} %get-tuple-element.30), calls=%async_computation.1 | async-start | bytes 262144 | tf_op jit(solution)/shard_map/all_to_all | solution.py:310
  55.1 1.0 copy-start.2
  56.1 0.7 copy-start.5
  72.3 17.2 %collective-permute-start.4 = (bf16[256,512]{1,0:T(8,128)(2,1)S(1)}, bf16[256,512]{1,0:T(8,128)(2,1)S(1)}, u32[]{:S(2)}, u32[]{:S(2)}) collective-permute-start(bf16[256,512]{1,0:T(8,128)(2,1)S(1)} %shard_map.87.refs_0_), channel_id=1, source_target_pairs={{0,2},{1,3},{2,4},{3,5},{4,6},{5,7},{6,0},{7,1},{8,10},{9,11},{10,... | collective-permute-start | bytes 786440 | tf_op jit(solution)/shard_map/ppermute | solution.py:220
  76.4 15.4 %collective-permute-start.5 = (bf16[256,512]{1,0:T(8,128)(2,1)S(1)}, bf16[256,512]{1,0:T(8,128)(2,1)S(1)}, u32[]{:S(2)}, u32[]{:S(2)}) collective-permute-start(bf16[256,512]{1,0:T(8,128)(2,1)S(1)} %shard_map.87.refs_0_), channel_id=1, source_target_pairs={{0,6},{1,7},{2,0},{3,1},{4,2},{5,3},{6,4},{7,5},{8,14},{9,15},{10,... | collective-permute-start | bytes 786440 | tf_op jit(solution)/shard_map/ppermute | solution.py:220
  79.7 19.4 %collective-permute-start.2 = (bf16[256,512]{1,0:T(8,128)(2,1)S(1)}, bf16[256,512]{1,0:T(8,128)(2,1)S(1)}, u32[]{:S(2)}, u32[]{:S(2)}) collective-permute-start(bf16[256,512]{1,0:T(8,128)(2,1)S(1)} %shard_map.87.refs_0_), channel_id=1, source_target_pairs={{0,1},{1,2},{2,3},{3,4},{4,5},{5,6},{6,7},{7,0},{8,9},{9,10},{10,1... | collective-permute-start | bytes 786440 | tf_op jit(solution)/shard_map/ppermute | solution.py:220
  82.5 21.9 %collective-permute-start.3 = (bf16[256,512]{1,0:T(8,128)(2,1)S(1)}, bf16[256,512]{1,0:T(8,128)(2,1)S(1)}, u32[]{:S(2)}, u32[]{:S(2)}) collective-permute-start(bf16[256,512]{1,0:T(8,128)(2,1)S(1)} %shard_map.87.refs_0_), channel_id=1, source_target_pairs={{0,7},{1,0},{2,1},{3,2},{4,3},{5,4},{6,5},{7,6},{8,15},{9,8},{10,9... | collective-permute-start | bytes 786440 | tf_op jit(solution)/shard_map/ppermute | solution.py:220
  89.5 14.9 %collective-permute-start.6 = (bf16[256,512]{1,0:T(8,128)(2,1)S(1)}, bf16[256,512]{1,0:T(8,128)(2,1)S(1)}, u32[]{:S(2)}, u32[]{:S(2)}) collective-permute-start(bf16[256,512]{1,0:T(8,128)(2,1)S(1)} %collective-permute-done.4.refs_3_), channel_id=1, source_target_pairs={{0,1},{1,2},{2,3},{3,4},{4,5},{5,6},{6,7},{7,0},{8,9},{9,10},{10,1... | collective-permute-start | bytes 786440 | tf_op jit(solution)/shard_map/ppermute | solution.py:220
  91.8 12.7 %collective-permute-start.7 = (bf16[256,512]{1,0:T(8,128)(2,1)S(1)}, bf16[256,512]{1,0:T(8,128)(2,1)S(1)}, u32[]{:S(2)}, u32[]{:S(2)}) collective-permute-start(bf16[256,512]{1,0:T(8,128)(2,1)S(1)} %collective-permute-done.5.refs_4_), channel_id=1, source_target_pairs={{0,7},{1,0},{2,1},{3,2},{4,3},{5,4},{6,5},{7,6},{8,15},{9,8},{10,9... | collective-permute-start | bytes 786440 | tf_op jit(solution)/shard_map/ppermute | solution.py:220
  96.5 11.4 %collective-permute-start.8 = (bf16[128,512]{1,0:T(8,128)(2,1)S(1)}, bf16[128,512]{1,0:T(8,128)(2,1)S(1)}, u32[]{:S(2)}, u32[]{:S(2)}) collective-permute-start(bf16[128,512]{1,0:T(8,128)(2,1)S(1)} %slice.8), channel_id=1, source_target_pairs={{0,2},{1,3},{2,4},{3,5},{4,6},{5,7},{6,0},{7,1},{8,10},{9,11},{10,... | collective-permute-start | bytes 393224 | tf_op jit(solution)/shard_map/ppermute | solution.py:220
  99.2 9.3 %collective-permute-start.9 = (bf16[128,512]{1,0:T(8,128)(2,1)S(1)}, bf16[128,512]{1,0:T(8,128)(2,1)S(1)}, u32[]{:S(2)}, u32[]{:S(2)}) collective-permute-start(bf16[128,512]{1,0:T(8,128)(2,1)S(1)} %slice.9), channel_id=1, source_target_pairs={{0,6},{1,7},{2,0},{3,1},{4,2},{5,3},{6,4},{7,5},{8,14},{9,15},{10,... | collective-permute-start | bytes 393224 | tf_op jit(solution)/shard_map/ppermute | solution.py:220
Sparse Core Ops, SparseCore 0:
  33.5 65.8 all-gather.4

commit v5 on v4

--- a/solution.py
+++ b/solution.py
@@ -217,7 +217,8 @@
 
 def head_gather(block, axis, size):
     def shift(value, by):
-        return lax.ppermute(value, axis, [(i, (i + by) % size) for i in range(size)])
+        moves = [(c * size + i, c * size + (i + by * (1 - 2 * c)) % size) for c in range(2) for i in range(size)]
+        return lax.ppermute(value, ("c", axis), moves)
 
     gathered = [(0, block)]
     half = block.shape[0] // 2
@@ -321,9 +322,10 @@
     )(core[None], intra, query_held, gates, stats, start_tiles, both, start_max)
     gathered, opposite = head_gather(normed, "y", heads)
     parity = lax.axis_index("z") % 2
+    way = 1 - 2 * core
     where = []
     for place in [place for place, _ in gathered] + [heads // 2]:
-        owners = [(head + place + offset) % heads for offset in offsets]
+        owners = [(head + way * place + offset) % heads for offset in offsets]
         part = (owners[0] % 2 != parity).astype(jnp.int32)
         where += [jnp.where(part == 0, owners[0], owners[1]) // 2, part]
     total, last = call(

time: 118 us -> 117 us (level)
  starting transfers between devices: 58.7 us -> 57.4 us
  waiting for transfers between devices: 17.2 us -> 18.4 us
    ppermute x8, starting transfers between devices: 27.9 us -> 26.6 us  [shift(): return lax.ppermute(value, ('c', axis), moves)]
where the time goes in v5:
time: 117 us; the launch traced here: 116 us
  starting transfers between devices  57.4 us (49%)
  waiting for transfers between devices  18.4 us (16%)
  between operations  14.1 us (12%)
  blocking collectives  10.5 us (9%)
  Pallas kernels  10.2 us (9%)
  local copies, waits for them, and re-layouts  5.22 us (4%)
    ppermute x8, starting transfers between devices, shift(): return lax.ppermute(value, ('c', axis), moves)  26.6 us
    ppermute x2, starting transfers between devices, local(): lax.ppermute(out_weight.T, ('z', 'y'), [(z * heads + h, (h + offset) % he...  19.8 us
    all_to_all x1, waiting for transfers between devices, local(): back = lax.all_to_all(starts, ('z', 'x'), 0, 0, tiled=True)  7.72 us
    all_gather x1, blocking collectives, local(): start_tiles = lax.all_gather(back, 'c').reshape(count, *TILE)  7.2 us
    all_to_all x1, starting transfers between devices, local(): held = lax.all_to_all(send, ('z', 'x'), 0, 0, tiled=True)  7.04 us
    ppermute x8, waiting for transfers between devices, shift(): return lax.ppermute(value, ('c', axis), moves)  5.37 us
    all_to_all x1, waiting for transfers between devices, local(): held = lax.all_to_all(send, ('z', 'x'), 0, 0, tiled=True)  5.27 us
    unnamed x12, local copies, waits for them, and re-layouts  5.1 us
  transfers between devices with their start and end apart: 13, of which 5 were waited for; matrix products, arithmetic and copies ran while one was open for 0% of the time, Pallas kernels for 8%

profile of v5, /device:TPU:1, one launch (start us, length us, event | category | flops | bytes accessed | tf_op | source)
XLA Modules:
  0.0 116.4 jit_solution(9918197741253243782)
XLA Ops:
  6.5 0.0 all-gather.5.cloned.1.call-start
  6.5 11.5 %collective-permute-start = (bf16[64,512]{1,0:T(8,128)(2,1)}, bf16[64,512]{1,0:T(8,128)(2,1)S(1)}, u32[]{:S(2)}, u32[]{:S(2)}) collective-permute-start(bf16[64,512]{1,0:T(8,128)(2,1)} %bitcast.26), channel_id=1, source_target_pairs={{0,320},{1,384},{2,448},{3,0},{4,64},{5,128},{6,192},{7,256},{64,3... | collective-permute-start | bytes 196616 | tf_op jit(solution)/shard_map/ppermute | solution.py:253
  18.0 8.4 %collective-permute-start.1 = (bf16[64,512]{1,0:T(8,128)(2,1)}, bf16[64,512]{1,0:T(8,128)(2,1)S(1)}, u32[]{:S(2)}, u32[]{:S(2)}) collective-permute-start(bf16[64,512]{1,0:T(8,128)(2,1)} %bitcast.27), channel_id=1, source_target_pairs={{0,256},{1,320},{2,384},{3,448},{4,0},{5,64},{6,128},{7,192},{64,2... | collective-permute-start | bytes 196616 | tf_op jit(solution)/shard_map/ppermute | solution.py:253
  26.4 2.3 %shard_map.82 = (bf16[65,16,128]{2,1,0:T(8,128)(2,1)}, f32[16,256]{1,0:T(8,128)}) custom-call(bf16[256,256]{1,0:T(8,128)(2,1)} %key_hbm.3, bf16[256,512]{1,0:T(8,128)(2,1)} %value_hbm.3, f32[1,256]{1,0:T(1,128)} %in_hbm.1, f32[1,256]{1,0:T(1,128)} %forget_hbm.1), custom_call_target="tpu_custom_call" | custom-call | bytes 1048576 | tf_op jit(solution)/shard_map/pallas_call | solution.py:265
  28.6 3.3 %all-gather = bf16[130,16,128]{2,1,0:T(8,128)(2,1)S(1)} all-gather(bf16[65,16,128]{2,1,0:T(8,128)(2,1)} %get-tuple-element.21), channel_id=2, replica_groups=mesh['z'=8,'x'=4,'c'=2,'y'=8] {'c'}, dimensions={0}, use_global_device_ids=true | all-gather | bytes 798720 | tf_op jit(solution)/shard_map/all_gather | solution.py:278
  31.9 0.7 shard_map.83
  32.6 0.0 collective-permute-done
  32.6 0.0 collective-permute-done.1
  32.7 0.7 pad_maximum_fusion
  33.3 0.0 all-gather.5.cloned.1.call-update
  33.3 7.0 %all-to-all-start = ((bf16[32,24,128]{2,1,0:T(8,128)(2,1)}), bf16[32,24,128]{2,1,0:T(8,128)(2,1)S(1)}, u32[]{:S(2)}, u32[]{:S(2)}) async-start(bf16[32,24,128]{2,1,0:T(8,128)(2,1)} %shard_map.83), calls=%async_computation | async-start | bytes 393216 | tf_op jit(solution)/shard_map/all_to_all | solution.py:288
  40.4 0.0 copy-start
  40.4 0.9 copy-done
  41.4 0.0 copy-start.1
  41.4 0.9 copy-done.1
  42.3 0.0 copy-start.3
  42.3 0.9 copy-done.3
  43.2 0.0 copy-start.4
  43.2 0.7 copy-done.4
  43.9 1.2 %shard_map.84 = (f32[256,512]{1,0:T(8,128)S(1)}, bf16[256,256]{1,0:T(8,128)(2,1)S(1)}, f32[256,128]{1,0:T(8,128)S(1)}) custom-call(bf16[256,256]{1,0:T(8,128)(2,1)S(1)} %copy-done.3, bf16[256,256]{1,0:T(8,128)(2,1)S(1)} %copy-done.1, bf16[256,512]{1,0:T(8,128)(2,1)S(1)} %copy-done, f32[16,256]{1,0:T(8,128)S(1)} %copy-done.4), custom_call_target="tpu_custom_call" | custom-call | flops 100663296 | bytes 1048576 | tf_op jit(solution)/shard_map/pallas_call | solution.py:289
  45.1 5.3 %all-to-all-done.held_ref = bf16[32,24,128]{2,1,0:T(8,128)(2,1)S(1)} async-done(((bf16[32,24,128]{2,1,0:T(8,128)(2,1)}), bf16[32,24,128]{2,1,0:T(8,128)(2,1)S(1)}, u32[]{:S(2)}, u32[]{:S(2)}) %all-to-all-start) | async-done | bytes 196640 | tf_op jit(solution)/shard_map/all_to_all | solution.py:288
  50.4 0.8 shard_map.85
  51.1 4.0 %all-to-all-start.1 = ((bf16[32,16,128]{2,1,0:T(8,128)(2,1)}), bf16[32,16,128]{2,1,0:T(8,128)(2,1)S(1)}, u32[]{:S(2)}, u32[]{:S(2)}) async-start(bf16[32,16,128]{2,1,0:T(8,128)(2,1)} %get-tuple-element.30), calls=%async_computation.1 | async-start | bytes 262144 | tf_op jit(solution)/shard_map/all_to_all | solution.py:311
  55.1 0.0 copy-start.2
  55.1 0.9 copy-done.2
  56.1 0.0 copy-start.5
  56.1 0.7 copy-done.5
  56.7 0.1 shard_map.86.gate_ref
  56.8 7.7 %all-to-all-done.1 = bf16[32,16,128]{2,1,0:T(8,128)(2,1)S(1)} async-done(((bf16[32,16,128]{2,1,0:T(8,128)(2,1)}), bf16[32,16,128]{2,1,0:T(8,128)(2,1)S(1)}, u32[]{:S(2)}, u32[]{:S(2)}) %all-to-all-start.1) | async-done | bytes 131104 | tf_op jit(solution)/shard_map/all_to_all | solution.py:311
  64.5 7.2 %all-gather.2.tiles_ref = bf16[64,16,128]{2,1,0:T(8,128)(2,1)S(1)} all-gather(bf16[32,16,128]{2,1,0:T(8,128)(2,1)S(1)} %all-to-all-done.1), channel_id=4, replica_groups=mesh['z'=8,'x'=4,'c'=2,'y'=8] {'c'}, dimensions={0}, use_global_device_ids=true | all-gather | bytes 393216 | tf_op jit(solution)/shard_map/all_gather | solution.py:316
  71.7 0.6 shard_map.87.refs_0_
  72.3 1.9 %collective-permute-start.4 = (bf16[256,512]{1,0:T(8,128)(2,1)S(1)}, bf16[256,512]{1,0:T(8,128)(2,1)S(1)}, u32[]{:S(2)}, u32[]{:S(2)}) collective-permute-start(bf16[256,512]{1,0:T(8,128)(2,1)S(1)} %shard_map.87.refs_0_), channel_id=1, source_target_pairs={{0,2},{1,3},{2,4},{3,5},{4,6},{5,7},{6,0},{7,1},{8,14},{9,15},{10,... | collective-permute-start | bytes 786440 | tf_op jit(solution)/shard_map/ppermute | solution.py:221
  74.3 4.3 %collective-permute-start.5 = (bf16[256,512]{1,0:T(8,128)(2,1)S(1)}, bf16[256,512]{1,0:T(8,128)(2,1)S(1)}, u32[]{:S(2)}, u32[]{:S(2)}) collective-permute-start(bf16[256,512]{1,0:T(8,128)(2,1)S(1)} %shard_map.87.refs_0_), channel_id=1, source_target_pairs={{0,6},{1,7},{2,0},{3,1},{4,2},{5,3},{6,4},{7,5},{8,10},{9,11},{10,... | collective-permute-start | bytes 786440 | tf_op jit(solution)/shard_map/ppermute | solution.py:221
  78.5 4.8 %collective-permute-start.2 = (bf16[256,512]{1,0:T(8,128)(2,1)S(1)}, bf16[256,512]{1,0:T(8,128)(2,1)S(1)}, u32[]{:S(2)}, u32[]{:S(2)}) collective-permute-start(bf16[256,512]{1,0:T(8,128)(2,1)S(1)} %shard_map.87.refs_0_), channel_id=1, source_target_pairs={{0,1},{1,2},{2,3},{3,4},{4,5},{5,6},{6,7},{7,0},{8,15},{9,8},{10,9... | collective-permute-start | bytes 786440 | tf_op jit(solution)/shard_map/ppermute | solution.py:221
  83.3 1.9 %collective-permute-start.3 = (bf16[256,512]{1,0:T(8,128)(2,1)S(1)}, bf16[256,512]{1,0:T(8,128)(2,1)S(1)}, u32[]{:S(2)}, u32[]{:S(2)}) collective-permute-start(bf16[256,512]{1,0:T(8,128)(2,1)S(1)} %shard_map.87.refs_0_), channel_id=1, source_target_pairs={{0,7},{1,0},{2,1},{3,2},{4,3},{5,4},{6,5},{7,6},{8,9},{9,10},{10,1... | collective-permute-start | bytes 786440 | tf_op jit(solution)/shard_map/ppermute | solution.py:221
  85.2 0.0 collective-permute-done.4.refs_3_
  85.2 4.6 %collective-permute-start.6 = (bf16[256,512]{1,0:T(8,128)(2,1)S(1)}, bf16[256,512]{1,0:T(8,128)(2,1)S(1)}, u32[]{:S(2)}, u32[]{:S(2)}) collective-permute-start(bf16[256,512]{1,0:T(8,128)(2,1)S(1)} %collective-permute-done.4.refs_3_), channel_id=1, source_target_pairs={{0,1},{1,2},{2,3},{3,4},{4,5},{5,6},{6,7},{7,0},{8,15},{9,8},{10,9... | collective-permute-start | bytes 786440 | tf_op jit(solution)/shard_map/ppermute | solution.py:221
  89.8 1.7 %collective-permute-done.5.refs_4_ = bf16[256,512]{1,0:T(8,128)(2,1)S(1)} collective-permute-done((bf16[256,512]{1,0:T(8,128)(2,1)S(1)}, bf16[256,512]{1,0:T(8,128)(2,1)S(1)}, u32[]{:S(2)}, u32[]{:S(2)}) %collective-permute-start.5) | collective-permute-done | bytes 262176 | tf_op jit(solution)/shard_map/ppermute | solution.py:221
  91.6 2.9 %collective-permute-start.7 = (bf16[256,512]{1,0:T(8,128)(2,1)S(1)}, bf16[256,512]{1,0:T(8,128)(2,1)S(1)}, u32[]{:S(2)}, u32[]{:S(2)}) collective-permute-start(bf16[256,512]{1,0:T(8,128)(2,1)S(1)} %collective-permute-done.5.refs_4_), channel_id=1, source_target_pairs={{0,7},{1,0},{2,1},{3,2},{4,3},{5,4},{6,5},{7,6},{8,9},{9,10},{10,1... | collective-permute-start | bytes 786440 | tf_op jit(solution)/shard_map/ppermute | solution.py:221
  94.5 2.1 %collective-permute-start.8 = (bf16[128,512]{1,0:T(8,128)(2,1)S(1)}, bf16[128,512]{1,0:T(8,128)(2,1)S(1)}, u32[]{:S(2)}, u32[]{:S(2)}) collective-permute-start(bf16[128,512]{1,0:T(8,128)(2,1)S(1)} %slice.8), channel_id=1, source_target_pairs={{0,2},{1,3},{2,4},{3,5},{4,6},{5,7},{6,0},{7,1},{8,14},{9,15},{10,... | collective-permute-start | bytes 393224 | tf_op jit(solution)/shard_map/ppermute | solution.py:221
  96.6 0.0 collective-permute-done.2.refs_1_
  96.6 4.1 %collective-permute-start.9 = (bf16[128,512]{1,0:T(8,128)(2,1)S(1)}, bf16[128,512]{1,0:T(8,128)(2,1)S(1)}, u32[]{:S(2)}, u32[]{:S(2)}) collective-permute-start(bf16[128,512]{1,0:T(8,128)(2,1)S(1)} %slice.9), channel_id=1, source_target_pairs={{0,6},{1,7},{2,0},{3,1},{4,2},{5,3},{6,4},{7,5},{8,10},{9,11},{10,... | collective-permute-start | bytes 393224 | tf_op jit(solution)/shard_map/ppermute | solution.py:221
  101.2 0.1 stack.67.where_ref
  101.4 0.0 collective-permute-done.3.refs_2_
  101.4 0.0 collective-permute-done.6.refs_5_
  101.4 1.0 collective-permute-done.7.refs_6_
  102.4 0.0 all-gather.5.cloned.1.call-done
  102.4 3.4 %shard_map.88 = (f32[256,512]{1,0:T(8,128)S(1)}, bf16[8,64,512]{2,1,0:T(8,128)(2,1)S(1)}) custom-call(s32[16]{0:T(128)S(1)} %stack.67.where_ref, bf16[4,8,2,64,512]{4,3,2,1,0:T(8,128)(2,1)} %bitcast.25, bf16[256,512]{1,0:T(8,128)(2,1)S(1)} %shard_map.87.refs_0_, bf16[256,512]{1,0:T(8,128)(2,1)S(1)} %collective-permute-done.2.refs_1_, ...), custom_call_target="tpu_custom_call" | custom-call | flops 1073741824 | bytes 8388608 | tf_op jit(solution)/shard_map/pallas_call | solution.py:331
  105.8 0.0 collective-permute-done.8.first_ref
  105.8 2.6 %collective-permute-done.9.last_ref = bf16[128,512]{1,0:T(8,128)(2,1)S(1)} collective-permute-done((bf16[128,512]{1,0:T(8,128)(2,1)S(1)}, bf16[128,512]{1,0:T(8,128)(2,1)S(1)}, u32[]{:S(2)}, u32[]{:S(2)}) %collective-permute-start.9) | collective-permute-done | bytes 131104 | tf_op jit(solution)/shard_map/ppermute | solution.py:221
  108.4 1.2 %shard_map.89 = bf16[256,512]{1,0:T(8,128)(2,1)} custom-call(f32[256,512]{1,0:T(8,128)S(1)} %get-tuple-element.35.total_ref, bf16[8,64,512]{2,1,0:T(8,128)(2,1)S(1)} %get-tuple-element.36.weight_ref, bf16[128,512]{1,0:T(8,128)(2,1)S(1)} %collective-permute-done.8.first_ref, bf16[128,512]{1,0:T(8,128)(2,1)S(1)} %collective-permute-done.9.last_ref), custom_call_target="tpu_custom_call" | custom-call | bytes 1048576 | tf_op jit(solution)/shard_map/pallas_call | solution.py:345
  (2 shorter events, 0.0 us)
Async XLA Ops:
  6.5 95.8 %all-gather.5.cloned.1.call-start = ((), (), s32[]{:S(2)}) async-start(), calls=%async_computation.2 | async-start | bytes 4325376 | tf_op jit(solution)/shard_map/all_gather | solution.py:285
  6.5 26.1 %collective-permute-start = (bf16[64,512]{1,0:T(8,128)(2,1)}, bf16[64,512]{1,0:T(8,128)(2,1)S(1)}, u32[]{:S(2)}, u32[]{:S(2)}) collective-permute-start(bf16[64,512]{1,0:T(8,128)(2,1)} %bitcast.26), channel_id=1, source_target_pairs={{0,320},{1,384},{2,448},{3,0},{4,64},{5,128},{6,192},{7,256},{64,3... | collective-permute-start | bytes 196616 | tf_op jit(solution)/shard_map/ppermute | solution.py:253
  18.0 14.6 %collective-permute-start.1 = (bf16[64,512]{1,0:T(8,128)(2,1)}, bf16[64,512]{1,0:T(8,128)(2,1)S(1)}, u32[]{:S(2)}, u32[]{:S(2)}) collective-permute-start(bf16[64,512]{1,0:T(8,128)(2,1)} %bitcast.27), channel_id=1, source_target_pairs={{0,256},{1,320},{2,384},{3,448},{4,0},{5,64},{6,128},{7,192},{64,2... | collective-permute-start | bytes 196616 | tf_op jit(solution)/shard_map/ppermute | solution.py:253
  33.3 17.0 %all-to-all-start = ((bf16[32,24,128]{2,1,0:T(8,128)(2,1)}), bf16[32,24,128]{2,1,0:T(8,128)(2,1)S(1)}, u32[]{:S(2)}, u32[]{:S(2)}) async-start(bf16[32,24,128]{2,1,0:T(8,128)(2,1)} %shard_map.83), calls=%async_computation | async-start | bytes 393216 | tf_op jit(solution)/shard_map/all_to_all | solution.py:288
  40.4 1.0 copy-start
  41.4 0.9 copy-start.1
  42.3 0.9 copy-start.3
  43.2 0.7 copy-start.4
  51.1 13.4 %all-to-all-start.1 = ((bf16[32,16,128]{2,1,0:T(8,128)(2,1)}), bf16[32,16,128]{2,1,0:T(8,128)(2,1)S(1)}, u32[]{:S(2)}, u32[]{:S(2)}) async-start(bf16[32,16,128]{2,1,0:T(8,128)(2,1)} %get-tuple-element.30), calls=%async_computation.1 | async-start | bytes 262144 | tf_op jit(solution)/shard_map/all_to_all | solution.py:311
  55.1 1.0 copy-start.2
  56.1 0.7 copy-start.5
  72.3 12.9 %collective-permute-start.4 = (bf16[256,512]{1,0:T(8,128)(2,1)S(1)}, bf16[256,512]{1,0:T(8,128)(2,1)S(1)}, u32[]{:S(2)}, u32[]{:S(2)}) collective-permute-start(bf16[256,512]{1,0:T(8,128)(2,1)S(1)} %shard_map.87.refs_0_), channel_id=1, source_target_pairs={{0,2},{1,3},{2,4},{3,5},{4,6},{5,7},{6,0},{7,1},{8,14},{9,15},{10,... | collective-permute-start | bytes 786440 | tf_op jit(solution)/shard_map/ppermute | solution.py:221
  74.3 17.3 %collective-permute-start.5 = (bf16[256,512]{1,0:T(8,128)(2,1)S(1)}, bf16[256,512]{1,0:T(8,128)(2,1)S(1)}, u32[]{:S(2)}, u32[]{:S(2)}) collective-permute-start(bf16[256,512]{1,0:T(8,128)(2,1)S(1)} %shard_map.87.refs_0_), channel_id=1, source_target_pairs={{0,6},{1,7},{2,0},{3,1},{4,2},{5,3},{6,4},{7,5},{8,10},{9,11},{10,... | collective-permute-start | bytes 786440 | tf_op jit(solution)/shard_map/ppermute | solution.py:221
  78.5 18.1 %collective-permute-start.2 = (bf16[256,512]{1,0:T(8,128)(2,1)S(1)}, bf16[256,512]{1,0:T(8,128)(2,1)S(1)}, u32[]{:S(2)}, u32[]{:S(2)}) collective-permute-start(bf16[256,512]{1,0:T(8,128)(2,1)S(1)} %shard_map.87.refs_0_), channel_id=1, source_target_pairs={{0,1},{1,2},{2,3},{3,4},{4,5},{5,6},{6,7},{7,0},{8,15},{9,8},{10,9... | collective-permute-start | bytes 786440 | tf_op jit(solution)/shard_map/ppermute | solution.py:221
  83.3 18.1 %collective-permute-start.3 = (bf16[256,512]{1,0:T(8,128)(2,1)S(1)}, bf16[256,512]{1,0:T(8,128)(2,1)S(1)}, u32[]{:S(2)}, u32[]{:S(2)}) collective-permute-start(bf16[256,512]{1,0:T(8,128)(2,1)S(1)} %shard_map.87.refs_0_), channel_id=1, source_target_pairs={{0,7},{1,0},{2,1},{3,2},{4,3},{5,4},{6,5},{7,6},{8,9},{9,10},{10,1... | collective-permute-start | bytes 786440 | tf_op jit(solution)/shard_map/ppermute | solution.py:221
  85.2 16.1 %collective-permute-start.6 = (bf16[256,512]{1,0:T(8,128)(2,1)S(1)}, bf16[256,512]{1,0:T(8,128)(2,1)S(1)}, u32[]{:S(2)}, u32[]{:S(2)}) collective-permute-start(bf16[256,512]{1,0:T(8,128)(2,1)S(1)} %collective-permute-done.4.refs_3_), channel_id=1, source_target_pairs={{0,1},{1,2},{2,3},{3,4},{4,5},{5,6},{6,7},{7,0},{8,15},{9,8},{10,9... | collective-permute-start | bytes 786440 | tf_op jit(solution)/shard_map/ppermute | solution.py:221
  91.6 10.8 %collective-permute-start.7 = (bf16[256,512]{1,0:T(8,128)(2,1)S(1)}, bf16[256,512]{1,0:T(8,128)(2,1)S(1)}, u32[]{:S(2)}, u32[]{:S(2)}) collective-permute-start(bf16[256,512]{1,0:T(8,128)(2,1)S(1)} %collective-permute-done.5.refs_4_), channel_id=1, source_target_pairs={{0,7},{1,0},{2,1},{3,2},{4,3},{5,4},{6,5},{7,6},{8,9},{9,10},{10,1... | collective-permute-start | bytes 786440 | tf_op jit(solution)/shard_map/ppermute | solution.py:221
  94.5 11.2 %collective-permute-start.8 = (bf16[128,512]{1,0:T(8,128)(2,1)S(1)}, bf16[128,512]{1,0:T(8,128)(2,1)S(1)}, u32[]{:S(2)}, u32[]{:S(2)}) collective-permute-start(bf16[128,512]{1,0:T(8,128)(2,1)S(1)} %slice.8), channel_id=1, source_target_pairs={{0,2},{1,3},{2,4},{3,5},{4,6},{5,7},{6,0},{7,1},{8,14},{9,15},{10,... | collective-permute-start | bytes 393224 | tf_op jit(solution)/shard_map/ppermute | solution.py:221
  96.6 11.7 %collective-permute-start.9 = (bf16[128,512]{1,0:T(8,128)(2,1)S(1)}, bf16[128,512]{1,0:T(8,128)(2,1)S(1)}, u32[]{:S(2)}, u32[]{:S(2)}) collective-permute-start(bf16[128,512]{1,0:T(8,128)(2,1)S(1)} %slice.9), channel_id=1, source_target_pairs={{0,6},{1,7},{2,0},{3,1},{4,2},{5,3},{6,4},{7,5},{8,10},{9,11},{10,... | collective-permute-start | bytes 393224 | tf_op jit(solution)/shard_map/ppermute | solution.py:221
Sparse Core Ops, SparseCore 0:
  33.5 65.9 all-gather.4

commit v6 on v5

--- a/solution.py
+++ b/solution.py
@@ -208,11 +208,8 @@
     copies[-1].wait()
 
 
-def finish_kernel(total_ref, weight_ref, first_ref, last_ref, out_ref):
-    half = first_ref.shape[0]
-    for start, part in ((0, first_ref), (half, last_ref)):
-        rows = pl.ds(start, half)
-        out_ref[rows] = (total_ref[rows] + head_product(part[...], weight_ref[...])).astype(BF16)
+def finish_kernel(total_ref, weight_ref, normed_ref, out_ref):
+    out_ref[...] = (total_ref[...] + head_product(normed_ref[...], weight_ref[...])).astype(BF16)
 
 
 def head_gather(block, axis, size):
@@ -221,19 +218,18 @@
         return lax.ppermute(value, ("c", axis), moves)
 
     gathered = [(0, block)]
-    half = block.shape[0] // 2
     if size == 8:
         far, back = shift(block, 2), shift(block, -2)
         near, behind = shift(block, 1), shift(block, -1)
         gathered += [(-1, near), (1, behind), (-2, far), (2, back)]
         gathered += [(-3, shift(far, 1)), (3, shift(back, -1))]
-        opposite = [shift(far[:half], 2), shift(back[half:], -2)]
+        opposite = shift(far, 2)
     else:
-        right = left = block
+        right = block
         if size == 4:
             right, left = shift(block, 1), shift(block, -1)
             gathered += [(-1, right), (1, left)]
-        opposite = [shift(right[:half], 1), shift(left[half:], -1)]
+        opposite = shift(right, 1)
     return gathered, opposite
 
 
@@ -248,7 +244,7 @@
     count = key_width * value_width // (TILE[0] * TILE[1])
     per = count // 2 // chips
 
-    offsets = (heads // 2 + 1, heads // 2)
+    offsets = (heads // 2 - 1, heads // 2)
     shards = [
         lax.ppermute(
             out_weight.T,
@@ -342,7 +338,7 @@
         flops=2 * length * value_width * value_width * heads,
         moved=2**23,
     )(jnp.stack(where).astype(jnp.int32), weight, *[block for _, block in gathered])
-    return call(finish_kernel, tile_array((length, value_width)), "vvvv")(total, last, *opposite)
+    return call(finish_kernel, tile_array((length, value_width)), "vvv")(total, last, opposite)
 
 
 def solution(mesh, sizes=(8, 4, 2, 8)):

time: 117 us -> 114 us (0.974)
  the two profiles are of different devices: /device:TPU:1 before, /device:TPU:24 now
where the time goes in v6:
time: 114 us
  starting transfers between devices  50.5 us (44%)
  waiting for transfers between devices  28.8 us (25%)
  between operations  14.1 us (12%)
  Pallas kernels  10.1 us (9%)
  local copies, waits for them, and re-layouts  5.19 us (5%)
  blocking collectives  4.38 us (4%)
    ppermute x7, starting transfers between devices, shift(): return lax.ppermute(value, ('c', axis), moves)  25.2 us
    ppermute x2, starting transfers between devices, local(): lax.ppermute(out_weight.T, ('z', 'y'), [(z * heads + h, (h + offset) % he...  15 us
    all_to_all x1, waiting for transfers between devices, local(): back = lax.all_to_all(starts, ('z', 'x'), 0, 0, tiled=True)  9.1 us
    ppermute x7, waiting for transfers between devices, shift(): return lax.ppermute(value, ('c', axis), moves)  8.41 us
    all_to_all x1, waiting for transfers between devices, local(): held = lax.all_to_all(send, ('z', 'x'), 0, 0, tiled=True)  7.09 us
    all_to_all x1, starting transfers between devices, local(): held = lax.all_to_all(send, ('z', 'x'), 0, 0, tiled=True)  6.42 us
    unnamed x12, local copies, waits for them, and re-layouts  5.1 us
    ppermute x2, waiting for transfers between devices, local(): lax.ppermute(out_weight.T, ('z', 'y'), [(z * heads + h, (h + offset) % he...  4.22 us
  transfers between devices with their start and end apart: 12, of which 6 were waited for; matrix products, arithmetic and copies ran while one was open for 0% of the time, Pallas kernels for 8%

profile of v6, /device:TPU:24, one launch (start us, length us, event | category | flops | bytes accessed | tf_op | source)
XLA Modules:
  0.0 113.7 jit_solution(5868501639463275236)
XLA Ops:
  6.5 0.0 all-gather.5.cloned.1.call-start
  6.5 10.6 %collective-permute-start = (bf16[64,512]{1,0:T(8,128)(2,1)}, bf16[64,512]{1,0:T(8,128)(2,1)S(1)}, u32[]{:S(2)}, u32[]{:S(2)}) collective-permute-start(bf16[64,512]{1,0:T(8,128)(2,1)} %bitcast.26), channel_id=1, source_target_pairs={{0,192},{1,256},{2,320},{3,384},{4,448},{5,0},{6,64},{7,128},{64,1... | collective-permute-start | bytes 196616 | tf_op jit(solution)/shard_map/ppermute | solution.py:249
  17.1 4.4 %collective-permute-start.1 = (bf16[64,512]{1,0:T(8,128)(2,1)}, bf16[64,512]{1,0:T(8,128)(2,1)S(1)}, u32[]{:S(2)}, u32[]{:S(2)}) collective-permute-start(bf16[64,512]{1,0:T(8,128)(2,1)} %bitcast.27), channel_id=1, source_target_pairs={{0,256},{1,320},{2,384},{3,448},{4,0},{5,64},{6,128},{7,192},{64,2... | collective-permute-start | bytes 196616 | tf_op jit(solution)/shard_map/ppermute | solution.py:249
  21.6 2.3 %shard_map.82 = (bf16[65,16,128]{2,1,0:T(8,128)(2,1)}, f32[16,256]{1,0:T(8,128)}) custom-call(bf16[256,256]{1,0:T(8,128)(2,1)} %key_hbm.3, bf16[256,512]{1,0:T(8,128)(2,1)} %value_hbm.3, f32[1,256]{1,0:T(1,128)} %in_hbm.1, f32[1,256]{1,0:T(1,128)} %forget_hbm.1), custom_call_target="tpu_custom_call" | custom-call | bytes 1048576 | tf_op jit(solution)/shard_map/pallas_call | solution.py:261
  23.9 2.4 %all-gather = bf16[130,16,128]{2,1,0:T(8,128)(2,1)S(1)} all-gather(bf16[65,16,128]{2,1,0:T(8,128)(2,1)} %get-tuple-element.21), channel_id=2, replica_groups=mesh['z'=8,'x'=4,'c'=2,'y'=8] {'c'}, dimensions={0}, use_global_device_ids=true | all-gather | bytes 798720 | tf_op jit(solution)/shard_map/all_gather | solution.py:274
  26.3 0.7 shard_map.83
  27.0 0.0 collective-permute-done
  27.0 4.2 %collective-permute-done.1 = bf16[64,512]{1,0:T(8,128)(2,1)S(1)} collective-permute-done((bf16[64,512]{1,0:T(8,128)(2,1)}, bf16[64,512]{1,0:T(8,128)(2,1)S(1)}, u32[]{:S(2)}, u32[]{:S(2)}) %collective-permute-start.1) | collective-permute-done | bytes 65568 | tf_op jit(solution)/shard_map/ppermute | solution.py:249
  31.2 0.7 pad_maximum_fusion
  31.9 0.0 all-gather.5.cloned.1.call-update
  31.9 6.4 %all-to-all-start = ((bf16[32,24,128]{2,1,0:T(8,128)(2,1)}), bf16[32,24,128]{2,1,0:T(8,128)(2,1)S(1)}, u32[]{:S(2)}, u32[]{:S(2)}) async-start(bf16[32,24,128]{2,1,0:T(8,128)(2,1)} %shard_map.83), calls=%async_computation | async-start | bytes 393216 | tf_op jit(solution)/shard_map/all_to_all | solution.py:284
  38.3 0.0 copy-start
  38.4 0.9 copy-done
  39.3 0.0 copy-start.1
  39.3 0.9 copy-done.1
  40.2 0.0 copy-start.3
  40.2 0.9 copy-done.3
  41.1 0.0 copy-start.4
  41.1 0.7 copy-done.4
  41.8 1.2 %shard_map.84 = (f32[256,512]{1,0:T(8,128)S(1)}, bf16[256,256]{1,0:T(8,128)(2,1)S(1)}, f32[256,128]{1,0:T(8,128)S(1)}) custom-call(bf16[256,256]{1,0:T(8,128)(2,1)S(1)} %copy-done.3, bf16[256,256]{1,0:T(8,128)(2,1)S(1)} %copy-done.1, bf16[256,512]{1,0:T(8,128)(2,1)S(1)} %copy-done, f32[16,256]{1,0:T(8,128)S(1)} %copy-done.4), custom_call_target="tpu_custom_call" | custom-call | flops 100663296 | bytes 1048576 | tf_op jit(solution)/shard_map/pallas_call | solution.py:285
  43.0 7.1 %all-to-all-done.held_ref = bf16[32,24,128]{2,1,0:T(8,128)(2,1)S(1)} async-done(((bf16[32,24,128]{2,1,0:T(8,128)(2,1)}), bf16[32,24,128]{2,1,0:T(8,128)(2,1)S(1)}, u32[]{:S(2)}, u32[]{:S(2)}) %all-to-all-start) | async-done | bytes 196640 | tf_op jit(solution)/shard_map/all_to_all | solution.py:284
  50.1 0.8 shard_map.85
  50.9 3.9 %all-to-all-start.1 = ((bf16[32,16,128]{2,1,0:T(8,128)(2,1)}), bf16[32,16,128]{2,1,0:T(8,128)(2,1)S(1)}, u32[]{:S(2)}, u32[]{:S(2)}) async-start(bf16[32,16,128]{2,1,0:T(8,128)(2,1)} %get-tuple-element.30), calls=%async_computation.1 | async-start | bytes 262144 | tf_op jit(solution)/shard_map/all_to_all | solution.py:307
  54.8 0.0 copy-start.2
  54.8 0.9 copy-done.2
  55.7 0.0 copy-start.5
  55.7 0.7 copy-done.5
  56.4 0.1 shard_map.86.gate_ref
  56.5 9.1 %all-to-all-done.1 = bf16[32,16,128]{2,1,0:T(8,128)(2,1)S(1)} async-done(((bf16[32,16,128]{2,1,0:T(8,128)(2,1)}), bf16[32,16,128]{2,1,0:T(8,128)(2,1)S(1)}, u32[]{:S(2)}, u32[]{:S(2)}) %all-to-all-start.1) | async-done | bytes 131104 | tf_op jit(solution)/shard_map/all_to_all | solution.py:307
  65.6 2.0 %all-gather.2.tiles_ref = bf16[64,16,128]{2,1,0:T(8,128)(2,1)S(1)} all-gather(bf16[32,16,128]{2,1,0:T(8,128)(2,1)S(1)} %all-to-all-done.1), channel_id=4, replica_groups=mesh['z'=8,'x'=4,'c'=2,'y'=8] {'c'}, dimensions={0}, use_global_device_ids=true | all-gather | bytes 393216 | tf_op jit(solution)/shard_map/all_gather | solution.py:312
  67.6 0.6 shard_map.87.refs_0_
  68.2 2.6 %collective-permute-start.4 = (bf16[256,512]{1,0:T(8,128)(2,1)S(1)}, bf16[256,512]{1,0:T(8,128)(2,1)S(1)}, u32[]{:S(2)}, u32[]{:S(2)}) collective-permute-start(bf16[256,512]{1,0:T(8,128)(2,1)S(1)} %shard_map.87.refs_0_), channel_id=1, source_target_pairs={{0,2},{1,3},{2,4},{3,5},{4,6},{5,7},{6,0},{7,1},{8,14},{9,15},{10,... | collective-permute-start | bytes 786440 | tf_op jit(solution)/shard_map/ppermute | solution.py:218
  70.8 4.1 %collective-permute-start.5 = (bf16[256,512]{1,0:T(8,128)(2,1)S(1)}, bf16[256,512]{1,0:T(8,128)(2,1)S(1)}, u32[]{:S(2)}, u32[]{:S(2)}) collective-permute-start(bf16[256,512]{1,0:T(8,128)(2,1)S(1)} %shard_map.87.refs_0_), channel_id=1, source_target_pairs={{0,6},{1,7},{2,0},{3,1},{4,2},{5,3},{6,4},{7,5},{8,10},{9,11},{10,... | collective-permute-start | bytes 786440 | tf_op jit(solution)/shard_map/ppermute | solution.py:218
  74.9 6.5 %collective-permute-start.2 = (bf16[256,512]{1,0:T(8,128)(2,1)S(1)}, bf16[256,512]{1,0:T(8,128)(2,1)S(1)}, u32[]{:S(2)}, u32[]{:S(2)}) collective-permute-start(bf16[256,512]{1,0:T(8,128)(2,1)S(1)} %shard_map.87.refs_0_), channel_id=1, source_target_pairs={{0,1},{1,2},{2,3},{3,4},{4,5},{5,6},{6,7},{7,0},{8,15},{9,8},{10,9... | collective-permute-start | bytes 786440 | tf_op jit(solution)/shard_map/ppermute | solution.py:218
  81.4 1.9 %collective-permute-start.3 = (bf16[256,512]{1,0:T(8,128)(2,1)S(1)}, bf16[256,512]{1,0:T(8,128)(2,1)S(1)}, u32[]{:S(2)}, u32[]{:S(2)}) collective-permute-start(bf16[256,512]{1,0:T(8,128)(2,1)S(1)} %shard_map.87.refs_0_), channel_id=1, source_target_pairs={{0,7},{1,0},{2,1},{3,2},{4,3},{5,4},{6,5},{7,6},{8,9},{9,10},{10,1... | collective-permute-start | bytes 786440 | tf_op jit(solution)/shard_map/ppermute | solution.py:218
  83.3 1.5 %collective-permute-done.4.refs_3_ = bf16[256,512]{1,0:T(8,128)(2,1)S(1)} collective-permute-done((bf16[256,512]{1,0:T(8,128)(2,1)S(1)}, bf16[256,512]{1,0:T(8,128)(2,1)S(1)}, u32[]{:S(2)}, u32[]{:S(2)}) %collective-permute-start.4) | collective-permute-done | bytes 262176 | tf_op jit(solution)/shard_map/ppermute | solution.py:218
  84.8 3.7 %collective-permute-start.6 = (bf16[256,512]{1,0:T(8,128)(2,1)S(1)}, bf16[256,512]{1,0:T(8,128)(2,1)S(1)}, u32[]{:S(2)}, u32[]{:S(2)}) collective-permute-start(bf16[256,512]{1,0:T(8,128)(2,1)S(1)} %collective-permute-done.4.refs_3_), channel_id=1, source_target_pairs={{0,1},{1,2},{2,3},{3,4},{4,5},{5,6},{6,7},{7,0},{8,15},{9,8},{10,9... | collective-permute-start | bytes 786440 | tf_op jit(solution)/shard_map/ppermute | solution.py:218
  88.5 0.0 collective-permute-done.5.refs_4_
  88.5 3.7 %collective-permute-start.7 = (bf16[256,512]{1,0:T(8,128)(2,1)S(1)}, bf16[256,512]{1,0:T(8,128)(2,1)S(1)}, u32[]{:S(2)}, u32[]{:S(2)}) collective-permute-start(bf16[256,512]{1,0:T(8,128)(2,1)S(1)} %collective-permute-done.5.refs_4_), channel_id=1, source_target_pairs={{0,7},{1,0},{2,1},{3,2},{4,3},{5,4},{6,5},{7,6},{8,9},{9,10},{10,1... | collective-permute-start | bytes 786440 | tf_op jit(solution)/shard_map/ppermute | solution.py:218
  92.2 2.7 %collective-permute-start.8 = (bf16[256,512]{1,0:T(8,128)(2,1)S(1)}, bf16[256,512]{1,0:T(8,128)(2,1)S(1)}, u32[]{:S(2)}, u32[]{:S(2)}) collective-permute-start(bf16[256,512]{1,0:T(8,128)(2,1)S(1)} %collective-permute-done.4.refs_3_), channel_id=1, source_target_pairs={{0,2},{1,3},{2,4},{3,5},{4,6},{5,7},{6,0},{7,1},{8,14},{9,15},{10,... | collective-permute-start | bytes 786440 | tf_op jit(solution)/shard_map/ppermute | solution.py:218
  95.4 0.1 stack.67.where_ref
  95.5 0.0 collective-permute-done.2.refs_1_
  95.5 0.0 collective-permute-done.3.refs_2_
  95.5 0.8 collective-permute-done.6.refs_5_
  96.3 6.1 %collective-permute-done.7.refs_6_ = bf16[256,512]{1,0:T(8,128)(2,1)S(1)} collective-permute-done((bf16[256,512]{1,0:T(8,128)(2,1)S(1)}, bf16[256,512]{1,0:T(8,128)(2,1)S(1)}, u32[]{:S(2)}, u32[]{:S(2)}) %collective-permute-start.7) | collective-permute-done | bytes 262176 | tf_op jit(solution)/shard_map/ppermute | solution.py:218
  102.4 0.0 all-gather.5.cloned.1.call-done
  102.4 3.4 %shard_map.88 = (f32[256,512]{1,0:T(8,128)S(1)}, bf16[8,64,512]{2,1,0:T(8,128)(2,1)S(1)}) custom-call(s32[16]{0:T(128)S(1)} %stack.67.where_ref, bf16[4,8,2,64,512]{4,3,2,1,0:T(8,128)(2,1)} %bitcast.25, bf16[256,512]{1,0:T(8,128)(2,1)S(1)} %shard_map.87.refs_0_, bf16[256,512]{1,0:T(8,128)(2,1)S(1)} %collective-permute-done.2.refs_1_, ...), custom_call_target="tpu_custom_call" | custom-call | flops 1073741824 | bytes 8388608 | tf_op jit(solution)/shard_map/pallas_call | solution.py:327
  105.8 0.0 collective-permute-done.8.normed_ref
  105.8 1.0 shard_map.89
Async XLA Ops:
  6.5 95.9 %all-gather.5.cloned.1.call-start = ((), (), s32[]{:S(2)}) async-start(), calls=%async_computation.2 | async-start | bytes 4325376 | tf_op jit(solution)/shard_map/all_gather | solution.py:281
  6.5 20.5 %collective-permute-start = (bf16[64,512]{1,0:T(8,128)(2,1)}, bf16[64,512]{1,0:T(8,128)(2,1)S(1)}, u32[]{:S(2)}, u32[]{:S(2)}) collective-permute-start(bf16[64,512]{1,0:T(8,128)(2,1)} %bitcast.26), channel_id=1, source_target_pairs={{0,192},{1,256},{2,320},{3,384},{4,448},{5,0},{6,64},{7,128},{64,1... | collective-permute-start | bytes 196616 | tf_op jit(solution)/shard_map/ppermute | solution.py:249
  17.1 14.1 %collective-permute-start.1 = (bf16[64,512]{1,0:T(8,128)(2,1)}, bf16[64,512]{1,0:T(8,128)(2,1)S(1)}, u32[]{:S(2)}, u32[]{:S(2)}) collective-permute-start(bf16[64,512]{1,0:T(8,128)(2,1)} %bitcast.27), channel_id=1, source_target_pairs={{0,256},{1,320},{2,384},{3,448},{4,0},{5,64},{6,128},{7,192},{64,2... | collective-permute-start | bytes 196616 | tf_op jit(solution)/shard_map/ppermute | solution.py:249
  31.9 18.2 %all-to-all-start = ((bf16[32,24,128]{2,1,0:T(8,128)(2,1)}), bf16[32,24,128]{2,1,0:T(8,128)(2,1)S(1)}, u32[]{:S(2)}, u32[]{:S(2)}) async-start(bf16[32,24,128]{2,1,0:T(8,128)(2,1)} %shard_map.83), calls=%async_computation | async-start | bytes 393216 | tf_op jit(solution)/shard_map/all_to_all | solution.py:284
  38.3 1.0 copy-start
  39.3 0.9 copy-start.1
  40.2 0.9 copy-start.3
  41.1 0.7 copy-start.4
  50.9 14.7 %all-to-all-start.1 = ((bf16[32,16,128]{2,1,0:T(8,128)(2,1)}), bf16[32,16,128]{2,1,0:T(8,128)(2,1)S(1)}, u32[]{:S(2)}, u32[]{:S(2)}) async-start(bf16[32,16,128]{2,1,0:T(8,128)(2,1)} %get-tuple-element.30), calls=%async_computation.1 | async-start | bytes 262144 | tf_op jit(solution)/shard_map/all_to_all | solution.py:307
  54.8 1.0 copy-start.2
  55.7 0.7 copy-start.5
  68.2 16.6 %collective-permute-start.4 = (bf16[256,512]{1,0:T(8,128)(2,1)S(1)}, bf16[256,512]{1,0:T(8,128)(2,1)S(1)}, u32[]{:S(2)}, u32[]{:S(2)}) collective-permute-start(bf16[256,512]{1,0:T(8,128)(2,1)S(1)} %shard_map.87.refs_0_), channel_id=1, source_target_pairs={{0,2},{1,3},{2,4},{3,5},{4,6},{5,7},{6,0},{7,1},{8,14},{9,15},{10,... | collective-permute-start | bytes 786440 | tf_op jit(solution)/shard_map/ppermute | solution.py:218
  70.8 17.7 %collective-permute-start.5 = (bf16[256,512]{1,0:T(8,128)(2,1)S(1)}, bf16[256,512]{1,0:T(8,128)(2,1)S(1)}, u32[]{:S(2)}, u32[]{:S(2)}) collective-permute-start(bf16[256,512]{1,0:T(8,128)(2,1)S(1)} %shard_map.87.refs_0_), channel_id=1, source_target_pairs={{0,6},{1,7},{2,0},{3,1},{4,2},{5,3},{6,4},{7,5},{8,10},{9,11},{10,... | collective-permute-start | bytes 786440 | tf_op jit(solution)/shard_map/ppermute | solution.py:218
  74.9 20.6 %collective-permute-start.2 = (bf16[256,512]{1,0:T(8,128)(2,1)S(1)}, bf16[256,512]{1,0:T(8,128)(2,1)S(1)}, u32[]{:S(2)}, u32[]{:S(2)}) collective-permute-start(bf16[256,512]{1,0:T(8,128)(2,1)S(1)} %shard_map.87.refs_0_), channel_id=1, source_target_pairs={{0,1},{1,2},{2,3},{3,4},{4,5},{5,6},{6,7},{7,0},{8,15},{9,8},{10,9... | collective-permute-start | bytes 786440 | tf_op jit(solution)/shard_map/ppermute | solution.py:218
  81.4 14.1 %collective-permute-start.3 = (bf16[256,512]{1,0:T(8,128)(2,1)S(1)}, bf16[256,512]{1,0:T(8,128)(2,1)S(1)}, u32[]{:S(2)}, u32[]{:S(2)}) collective-permute-start(bf16[256,512]{1,0:T(8,128)(2,1)S(1)} %shard_map.87.refs_0_), channel_id=1, source_target_pairs={{0,7},{1,0},{2,1},{3,2},{4,3},{5,4},{6,5},{7,6},{8,9},{9,10},{10,1... | collective-permute-start | bytes 786440 | tf_op jit(solution)/shard_map/ppermute | solution.py:218
  84.8 11.5 %collective-permute-start.6 = (bf16[256,512]{1,0:T(8,128)(2,1)S(1)}, bf16[256,512]{1,0:T(8,128)(2,1)S(1)}, u32[]{:S(2)}, u32[]{:S(2)}) collective-permute-start(bf16[256,512]{1,0:T(8,128)(2,1)S(1)} %collective-permute-done.4.refs_3_), channel_id=1, source_target_pairs={{0,1},{1,2},{2,3},{3,4},{4,5},{5,6},{6,7},{7,0},{8,15},{9,8},{10,9... | collective-permute-start | bytes 786440 | tf_op jit(solution)/shard_map/ppermute | solution.py:218
  88.5 14.0 %collective-permute-start.7 = (bf16[256,512]{1,0:T(8,128)(2,1)S(1)}, bf16[256,512]{1,0:T(8,128)(2,1)S(1)}, u32[]{:S(2)}, u32[]{:S(2)}) collective-permute-start(bf16[256,512]{1,0:T(8,128)(2,1)S(1)} %collective-permute-done.5.refs_4_), channel_id=1, source_target_pairs={{0,7},{1,0},{2,1},{3,2},{4,3},{5,4},{6,5},{7,6},{8,9},{9,10},{10,1... | collective-permute-start | bytes 786440 | tf_op jit(solution)/shard_map/ppermute | solution.py:218
  92.2 13.6 %collective-permute-start.8 = (bf16[256,512]{1,0:T(8,128)(2,1)S(1)}, bf16[256,512]{1,0:T(8,128)(2,1)S(1)}, u32[]{:S(2)}, u32[]{:S(2)}) collective-permute-start(bf16[256,512]{1,0:T(8,128)(2,1)S(1)} %collective-permute-done.4.refs_3_), channel_id=1, source_target_pairs={{0,2},{1,3},{2,4},{3,5},{4,6},{5,7},{6,0},{7,1},{8,14},{9,15},{10,... | collective-permute-start | bytes 786440 | tf_op jit(solution)/shard_map/ppermute | solution.py:218
Sparse Core Ops, SparseCore 0:
  32.0 64.9 all-gather.4

commit v7 on v6

--- a/solution.py
+++ b/solution.py
@@ -248,14 +248,15 @@
     shards = [
         lax.ppermute(
             out_weight.T,
-            ("z", "y"),
+            ("z", "c", "y"),
             [
-                (z * heads + h, (h + offset) % heads * heads + z)
+                ((z * cores + c) * heads + h, ((h + offsets[turn ^ c]) % heads * cores + c) * heads + z)
                 for z in range(planes)
+                for c in range(cores)
                 for h in range(heads)
             ],
         )
-        for offset in offsets
+        for turn in range(2)
     ]
     tile_array = functools.partial(jax.ShapeDtypeStruct, dtype=BF16)
     state_tiles, rows = call(
@@ -278,6 +279,8 @@
         [(z * columns + x) * cores + c for z in range(first, planes, 2) for x in range(columns) for c in range(cores)]
         for first in range(2)
     ]
+    first, second = shards
+    shards = [jnp.where(core == 0, first, second), jnp.where(core == 0, second, first)]
     weight = lax.all_gather(jnp.concatenate(shards, axis=0), ("z", "x", "c"), axis_index_groups=groups)
     weight = weight.reshape(planes // 2, columns * cores, 2, *out_weight.shape[::-1])
 

time: 114 us -> 117 us (1.026)
  waiting for transfers between devices: 28.8 us -> 31.3 us
    ppermute x7, waiting for transfers between devices: 8.41 us -> 10.2 us  [shift(): return lax.ppermute(value, ('c', axis), moves)]
where the time goes in v7:
time: 117 us; the launch traced here: 116 us
  starting transfers between devices  51 us (44%)
  waiting for transfers between devices  31.3 us (27%)
  between operations  14.1 us (12%)
  Pallas kernels  10.1 us (9%)
  blocking collectives  4.98 us (4%)
  local copies, waits for them, and re-layouts  4.25 us (4%)
    ppermute x7, starting transfers between devices, shift(): return lax.ppermute(value, ('c', axis), moves)  24.9 us
    ppermute x2, starting transfers between devices, local(): lax.ppermute(out_weight.T, ('z', 'c', 'y'), [((z * cores + c) * heads + h...  15.2 us
    ppermute x7, waiting for transfers between devices, shift(): return lax.ppermute(value, ('c', axis), moves)  10.2 us
    all_to_all x1, waiting for transfers between devices, local(): back = lax.all_to_all(starts, ('z', 'x'), 0, 0, tiled=True)  9.93 us
    all_to_all x1, waiting for transfers between devices, local(): held = lax.all_to_all(send, ('z', 'x'), 0, 0, tiled=True)  7.25 us
    all_to_all x1, starting transfers between devices, local(): held = lax.all_to_all(send, ('z', 'x'), 0, 0, tiled=True)  7.05 us
    unnamed x12, local copies, waits for them, and re-layouts  4.15 us
    ppermute x2, waiting for transfers between devices, local(): lax.ppermute(out_weight.T, ('z', 'c', 'y'), [((z * cores + c) * heads + h...  3.91 us
  transfers between devices with their start and end apart: 12, of which 6 were waited for; matrix products, arithmetic and copies ran while one was open for 0% of the time, Pallas kernels for 8%

profile of v7, /device:TPU:24, one launch (start us, length us, event | category | flops | bytes accessed | tf_op | source)
XLA Modules:
  0.0 116.4 jit_solution(18105175744515795749)
XLA Ops:
  6.5 0.0 copy-start.2
  6.5 0.0 all-gather.5.cloned.1.call-start
  6.5 10.7 %collective-permute-start = (bf16[64,512]{1,0:T(8,128)(2,1)}, bf16[64,512]{1,0:T(8,128)(2,1)S(1)}, u32[]{:S(2)}, u32[]{:S(2)}) collective-permute-start(bf16[64,512]{1,0:T(8,128)(2,1)} %bitcast.26), channel_id=1, source_target_pairs={{0,192},{1,256},{2,320},{3,384},{4,448},{5,0},{6,64},{7,128},{8,26... | collective-permute-start | bytes 196616 | tf_op jit(solution)/shard_map/ppermute | solution.py:249
  17.3 4.4 %collective-permute-start.1 = (bf16[64,512]{1,0:T(8,128)(2,1)}, bf16[64,512]{1,0:T(8,128)(2,1)S(1)}, u32[]{:S(2)}, u32[]{:S(2)}) collective-permute-start(bf16[64,512]{1,0:T(8,128)(2,1)} %bitcast.27), channel_id=1, source_target_pairs={{0,256},{1,320},{2,384},{3,448},{4,0},{5,64},{6,128},{7,192},{8,20... | collective-permute-start | bytes 196616 | tf_op jit(solution)/shard_map/ppermute | solution.py:249
  21.7 2.3 %shard_map.82 = (bf16[65,16,128]{2,1,0:T(8,128)(2,1)}, f32[16,256]{1,0:T(8,128)}) custom-call(bf16[256,256]{1,0:T(8,128)(2,1)} %key_hbm.3, bf16[256,512]{1,0:T(8,128)(2,1)} %value_hbm.3, f32[1,256]{1,0:T(1,128)} %in_hbm.1, f32[1,256]{1,0:T(1,128)} %forget_hbm.1), custom_call_target="tpu_custom_call" | custom-call | bytes 1048576 | tf_op jit(solution)/shard_map/pallas_call | solution.py:262
  24.0 3.0 %all-gather = bf16[130,16,128]{2,1,0:T(8,128)(2,1)S(1)} all-gather(bf16[65,16,128]{2,1,0:T(8,128)(2,1)} %get-tuple-element.21), channel_id=2, replica_groups=mesh['z'=8,'x'=4,'c'=2,'y'=8] {'c'}, dimensions={0}, use_global_device_ids=true | all-gather | bytes 798720 | tf_op jit(solution)/shard_map/all_gather | solution.py:275
  27.0 0.7 shard_map.83
  27.7 0.0 collective-permute-done
  27.7 3.9 %collective-permute-done.1 = bf16[64,512]{1,0:T(8,128)(2,1)S(1)} collective-permute-done((bf16[64,512]{1,0:T(8,128)(2,1)}, bf16[64,512]{1,0:T(8,128)(2,1)S(1)}, u32[]{:S(2)}, u32[]{:S(2)}) %collective-permute-start.1) | collective-permute-done | bytes 65568 | tf_op jit(solution)/shard_map/ppermute | solution.py:249
  31.7 0.7 pad_maximum_fusion
  32.3 0.0 all-gather.5.cloned.1.call-update
  32.3 7.0 %all-to-all-start = ((bf16[32,24,128]{2,1,0:T(8,128)(2,1)}), bf16[32,24,128]{2,1,0:T(8,128)(2,1)S(1)}, u32[]{:S(2)}, u32[]{:S(2)}) async-start(bf16[32,24,128]{2,1,0:T(8,128)(2,1)} %shard_map.83), calls=%async_computation | async-start | bytes 393216 | tf_op jit(solution)/shard_map/all_to_all | solution.py:287
  39.4 0.0 copy-start
  39.4 0.9 copy-done
  40.4 0.0 copy-start.1
  40.4 0.9 copy-done.1
  41.3 0.0 copy-start.3
  41.3 0.9 copy-done.3
  42.2 0.0 copy-start.4
  42.2 0.7 copy-done.4
  42.9 1.2 %shard_map.84 = (f32[256,512]{1,0:T(8,128)S(1)}, bf16[256,256]{1,0:T(8,128)(2,1)S(1)}, f32[256,128]{1,0:T(8,128)S(1)}) custom-call(bf16[256,256]{1,0:T(8,128)(2,1)S(1)} %copy-done.3, bf16[256,256]{1,0:T(8,128)(2,1)S(1)} %copy-done.1, bf16[256,512]{1,0:T(8,128)(2,1)S(1)} %copy-done, f32[16,256]{1,0:T(8,128)S(1)} %copy-done.4), custom_call_target="tpu_custom_call" | custom-call | flops 100663296 | bytes 1048576 | tf_op jit(solution)/shard_map/pallas_call | solution.py:288
  44.1 7.2 %all-to-all-done.held_ref = bf16[32,24,128]{2,1,0:T(8,128)(2,1)S(1)} async-done(((bf16[32,24,128]{2,1,0:T(8,128)(2,1)}), bf16[32,24,128]{2,1,0:T(8,128)(2,1)S(1)}, u32[]{:S(2)}, u32[]{:S(2)}) %all-to-all-start) | async-done | bytes 196640 | tf_op jit(solution)/shard_map/all_to_all | solution.py:287
  51.4 0.8 shard_map.85
  52.1 3.9 %all-to-all-start.1 = ((bf16[32,16,128]{2,1,0:T(8,128)(2,1)}), bf16[32,16,128]{2,1,0:T(8,128)(2,1)S(1)}, u32[]{:S(2)}, u32[]{:S(2)}) async-start(bf16[32,16,128]{2,1,0:T(8,128)(2,1)} %get-tuple-element.30), calls=%async_computation.1 | async-start | bytes 262144 | tf_op jit(solution)/shard_map/all_to_all | solution.py:310
  56.0 0.0 copy-done.2
  56.0 0.0 copy-start.5
  56.0 0.7 copy-done.5
  56.7 0.1 shard_map.86.gate_ref
  56.8 9.9 %all-to-all-done.1 = bf16[32,16,128]{2,1,0:T(8,128)(2,1)S(1)} async-done(((bf16[32,16,128]{2,1,0:T(8,128)(2,1)}), bf16[32,16,128]{2,1,0:T(8,128)(2,1)S(1)}, u32[]{:S(2)}, u32[]{:S(2)}) %all-to-all-start.1) | async-done | bytes 131104 | tf_op jit(solution)/shard_map/all_to_all | solution.py:310
  66.7 2.0 %all-gather.2.tiles_ref = bf16[64,16,128]{2,1,0:T(8,128)(2,1)S(1)} all-gather(bf16[32,16,128]{2,1,0:T(8,128)(2,1)S(1)} %all-to-all-done.1), channel_id=4, replica_groups=mesh['z'=8,'x'=4,'c'=2,'y'=8] {'c'}, dimensions={0}, use_global_device_ids=true | all-gather | bytes 393216 | tf_op jit(solution)/shard_map/all_gather | solution.py:315
  68.7 0.6 shard_map.87.refs_0_
  69.3 1.9 %collective-permute-start.4 = (bf16[256,512]{1,0:T(8,128)(2,1)S(1)}, bf16[256,512]{1,0:T(8,128)(2,1)S(1)}, u32[]{:S(2)}, u32[]{:S(2)}) collective-permute-start(bf16[256,512]{1,0:T(8,128)(2,1)S(1)} %shard_map.87.refs_0_), channel_id=1, source_target_pairs={{0,2},{1,3},{2,4},{3,5},{4,6},{5,7},{6,0},{7,1},{8,14},{9,15},{10,... | collective-permute-start | bytes 786440 | tf_op jit(solution)/shard_map/ppermute | solution.py:218
  71.2 4.8 %collective-permute-start.5 = (bf16[256,512]{1,0:T(8,128)(2,1)S(1)}, bf16[256,512]{1,0:T(8,128)(2,1)S(1)}, u32[]{:S(2)}, u32[]{:S(2)}) collective-permute-start(bf16[256,512]{1,0:T(8,128)(2,1)S(1)} %shard_map.87.refs_0_), channel_id=1, source_target_pairs={{0,6},{1,7},{2,0},{3,1},{4,2},{5,3},{6,4},{7,5},{8,10},{9,11},{10,... | collective-permute-start | bytes 786440 | tf_op jit(solution)/shard_map/ppermute | solution.py:218
  76.0 6.2 %collective-permute-start.2 = (bf16[256,512]{1,0:T(8,128)(2,1)S(1)}, bf16[256,512]{1,0:T(8,128)(2,1)S(1)}, u32[]{:S(2)}, u32[]{:S(2)}) collective-permute-start(bf16[256,512]{1,0:T(8,128)(2,1)S(1)} %shard_map.87.refs_0_), channel_id=1, source_target_pairs={{0,1},{1,2},{2,3},{3,4},{4,5},{5,6},{6,7},{7,0},{8,15},{9,8},{10,9... | collective-permute-start | bytes 786440 | tf_op jit(solution)/shard_map/ppermute | solution.py:218
  82.3 1.9 %collective-permute-start.3 = (bf16[256,512]{1,0:T(8,128)(2,1)S(1)}, bf16[256,512]{1,0:T(8,128)(2,1)S(1)}, u32[]{:S(2)}, u32[]{:S(2)}) collective-permute-start(bf16[256,512]{1,0:T(8,128)(2,1)S(1)} %shard_map.87.refs_0_), channel_id=1, source_target_pairs={{0,7},{1,0},{2,1},{3,2},{4,3},{5,4},{6,5},{7,6},{8,9},{9,10},{10,1... | collective-permute-start | bytes 786440 | tf_op jit(solution)/shard_map/ppermute | solution.py:218
  84.2 1.4 %collective-permute-done.4.refs_3_ = bf16[256,512]{1,0:T(8,128)(2,1)S(1)} collective-permute-done((bf16[256,512]{1,0:T(8,128)(2,1)S(1)}, bf16[256,512]{1,0:T(8,128)(2,1)S(1)}, u32[]{:S(2)}, u32[]{:S(2)}) %collective-permute-start.4) | collective-permute-done | bytes 262176 | tf_op jit(solution)/shard_map/ppermute | solution.py:218
  85.6 4.8 %collective-permute-start.6 = (bf16[256,512]{1,0:T(8,128)(2,1)S(1)}, bf16[256,512]{1,0:T(8,128)(2,1)S(1)}, u32[]{:S(2)}, u32[]{:S(2)}) collective-permute-start(bf16[256,512]{1,0:T(8,128)(2,1)S(1)} %collective-permute-done.4.refs_3_), channel_id=1, source_target_pairs={{0,1},{1,2},{2,3},{3,4},{4,5},{5,6},{6,7},{7,0},{8,15},{9,8},{10,9... | collective-permute-start | bytes 786440 | tf_op jit(solution)/shard_map/ppermute | solution.py:218
  90.3 0.0 collective-permute-done.5.refs_4_
  90.3 2.9 %collective-permute-start.7 = (bf16[256,512]{1,0:T(8,128)(2,1)S(1)}, bf16[256,512]{1,0:T(8,128)(2,1)S(1)}, u32[]{:S(2)}, u32[]{:S(2)}) collective-permute-start(bf16[256,512]{1,0:T(8,128)(2,1)S(1)} %collective-permute-done.5.refs_4_), channel_id=1, source_target_pairs={{0,7},{1,0},{2,1},{3,2},{4,3},{5,4},{6,5},{7,6},{8,9},{9,10},{10,1... | collective-permute-start | bytes 786440 | tf_op jit(solution)/shard_map/ppermute | solution.py:218
  93.2 2.4 %collective-permute-start.8 = (bf16[256,512]{1,0:T(8,128)(2,1)S(1)}, bf16[256,512]{1,0:T(8,128)(2,1)S(1)}, u32[]{:S(2)}, u32[]{:S(2)}) collective-permute-start(bf16[256,512]{1,0:T(8,128)(2,1)S(1)} %collective-permute-done.4.refs_3_), channel_id=1, source_target_pairs={{0,2},{1,3},{2,4},{3,5},{4,6},{5,7},{6,0},{7,1},{8,14},{9,15},{10,... | collective-permute-start | bytes 786440 | tf_op jit(solution)/shard_map/ppermute | solution.py:218
  96.2 0.1 stack.67.where_ref
  96.3 0.0 collective-permute-done.2.refs_1_
  96.3 0.0 collective-permute-done.3.refs_2_
  96.3 1.3 %collective-permute-done.6.refs_5_ = bf16[256,512]{1,0:T(8,128)(2,1)S(1)} collective-permute-done((bf16[256,512]{1,0:T(8,128)(2,1)S(1)}, bf16[256,512]{1,0:T(8,128)(2,1)S(1)}, u32[]{:S(2)}, u32[]{:S(2)}) %collective-permute-start.6) | collective-permute-done | bytes 262176 | tf_op jit(solution)/shard_map/ppermute | solution.py:218
  97.6 7.5 %collective-permute-done.7.refs_6_ = bf16[256,512]{1,0:T(8,128)(2,1)S(1)} collective-permute-done((bf16[256,512]{1,0:T(8,128)(2,1)S(1)}, bf16[256,512]{1,0:T(8,128)(2,1)S(1)}, u32[]{:S(2)}, u32[]{:S(2)}) %collective-permute-start.7) | collective-permute-done | bytes 262176 | tf_op jit(solution)/shard_map/ppermute | solution.py:218
  105.1 0.0 all-gather.5.cloned.1.call-done
  105.1 3.4 %shard_map.88 = (f32[256,512]{1,0:T(8,128)S(1)}, bf16[8,64,512]{2,1,0:T(8,128)(2,1)S(1)}) custom-call(s32[16]{0:T(128)S(1)} %stack.67.where_ref, bf16[4,8,2,64,512]{4,3,2,1,0:T(8,128)(2,1)} %bitcast.25, bf16[256,512]{1,0:T(8,128)(2,1)S(1)} %shard_map.87.refs_0_, bf16[256,512]{1,0:T(8,128)(2,1)S(1)} %collective-permute-done.2.refs_1_, ...), custom_call_target="tpu_custom_call" | custom-call | flops 1073741824 | bytes 8388608 | tf_op jit(solution)/shard_map/pallas_call | solution.py:330
  108.5 0.0 collective-permute-done.8.normed_ref
  108.5 1.0 shard_map.89
  (1 shorter events, 0.0 us)
Async XLA Ops:
  6.5 49.5 %copy-start.2 = (bf16[256,512]{1,0:T(8,128)(2,1)S(1)}, bf16[256,512]{1,0:T(8,128)(2,1)}, u32[]{:S(2)}) copy-start(bf16[256,512]{1,0:T(8,128)(2,1)} %gate_ref.1) | copy-start | bytes 786436
  6.5 98.6 %all-gather.5.cloned.1.call-start = ((), (), s32[]{:S(2)}) async-start(), calls=%async_computation.2 | async-start | bytes 4325376 | tf_op jit(solution)/shard_map/all_gather | solution.py:284
  6.5 21.2 %collective-permute-start = (bf16[64,512]{1,0:T(8,128)(2,1)}, bf16[64,512]{1,0:T(8,128)(2,1)S(1)}, u32[]{:S(2)}, u32[]{:S(2)}) collective-permute-start(bf16[64,512]{1,0:T(8,128)(2,1)} %bitcast.26), channel_id=1, source_target_pairs={{0,192},{1,256},{2,320},{3,384},{4,448},{5,0},{6,64},{7,128},{8,26... | collective-permute-start | bytes 196616 | tf_op jit(solution)/shard_map/ppermute | solution.py:249
  17.3 14.4 %collective-permute-start.1 = (bf16[64,512]{1,0:T(8,128)(2,1)}, bf16[64,512]{1,0:T(8,128)(2,1)S(1)}, u32[]{:S(2)}, u32[]{:S(2)}) collective-permute-start(bf16[64,512]{1,0:T(8,128)(2,1)} %bitcast.27), channel_id=1, source_target_pairs={{0,256},{1,320},{2,384},{3,448},{4,0},{5,64},{6,128},{7,192},{8,20... | collective-permute-start | bytes 196616 | tf_op jit(solution)/shard_map/ppermute | solution.py:249
  32.3 19.0 %all-to-all-start = ((bf16[32,24,128]{2,1,0:T(8,128)(2,1)}), bf16[32,24,128]{2,1,0:T(8,128)(2,1)S(1)}, u32[]{:S(2)}, u32[]{:S(2)}) async-start(bf16[32,24,128]{2,1,0:T(8,128)(2,1)} %shard_map.83), calls=%async_computation | async-start | bytes 393216 | tf_op jit(solution)/shard_map/all_to_all | solution.py:287
  39.4 1.0 copy-start
  40.4 0.9 copy-start.1
  41.3 0.9 copy-start.3
  42.2 0.7 copy-start.4
  52.1 14.6 %all-to-all-start.1 = ((bf16[32,16,128]{2,1,0:T(8,128)(2,1)}), bf16[32,16,128]{2,1,0:T(8,128)(2,1)S(1)}, u32[]{:S(2)}, u32[]{:S(2)}) async-start(bf16[32,16,128]{2,1,0:T(8,128)(2,1)} %get-tuple-element.30), calls=%async_computation.1 | async-start | bytes 262144 | tf_op jit(solution)/shard_map/all_to_all | solution.py:310
  56.0 0.7 copy-start.5
  69.3 16.3 %collective-permute-start.4 = (bf16[256,512]{1,0:T(8,128)(2,1)S(1)}, bf16[256,512]{1,0:T(8,128)(2,1)S(1)}, u32[]{:S(2)}, u32[]{:S(2)}) collective-permute-start(bf16[256,512]{1,0:T(8,128)(2,1)S(1)} %shard_map.87.refs_0_), channel_id=1, source_target_pairs={{0,2},{1,3},{2,4},{3,5},{4,6},{5,7},{6,0},{7,1},{8,14},{9,15},{10,... | collective-permute-start | bytes 786440 | tf_op jit(solution)/shard_map/ppermute | solution.py:218
  71.2 19.1 %collective-permute-start.5 = (bf16[256,512]{1,0:T(8,128)(2,1)S(1)}, bf16[256,512]{1,0:T(8,128)(2,1)S(1)}, u32[]{:S(2)}, u32[]{:S(2)}) collective-permute-start(bf16[256,512]{1,0:T(8,128)(2,1)S(1)} %shard_map.87.refs_0_), channel_id=1, source_target_pairs={{0,6},{1,7},{2,0},{3,1},{4,2},{5,3},{6,4},{7,5},{8,10},{9,11},{10,... | collective-permute-start | bytes 786440 | tf_op jit(solution)/shard_map/ppermute | solution.py:218
  76.0 20.2 %collective-permute-start.2 = (bf16[256,512]{1,0:T(8,128)(2,1)S(1)}, bf16[256,512]{1,0:T(8,128)(2,1)S(1)}, u32[]{:S(2)}, u32[]{:S(2)}) collective-permute-start(bf16[256,512]{1,0:T(8,128)(2,1)S(1)} %shard_map.87.refs_0_), channel_id=1, source_target_pairs={{0,1},{1,2},{2,3},{3,4},{4,5},{5,6},{6,7},{7,0},{8,15},{9,8},{10,9... | collective-permute-start | bytes 786440 | tf_op jit(solution)/shard_map/ppermute | solution.py:218
  82.3 14.0 %collective-permute-start.3 = (bf16[256,512]{1,0:T(8,128)(2,1)S(1)}, bf16[256,512]{1,0:T(8,128)(2,1)S(1)}, u32[]{:S(2)}, u32[]{:S(2)}) collective-permute-start(bf16[256,512]{1,0:T(8,128)(2,1)S(1)} %shard_map.87.refs_0_), channel_id=1, source_target_pairs={{0,7},{1,0},{2,1},{3,2},{4,3},{5,4},{6,5},{7,6},{8,9},{9,10},{10,1... | collective-permute-start | bytes 786440 | tf_op jit(solution)/shard_map/ppermute | solution.py:218
  85.6 12.1 %collective-permute-start.6 = (bf16[256,512]{1,0:T(8,128)(2,1)S(1)}, bf16[256,512]{1,0:T(8,128)(2,1)S(1)}, u32[]{:S(2)}, u32[]{:S(2)}) collective-permute-start(bf16[256,512]{1,0:T(8,128)(2,1)S(1)} %collective-permute-done.4.refs_3_), channel_id=1, source_target_pairs={{0,1},{1,2},{2,3},{3,4},{4,5},{5,6},{6,7},{7,0},{8,15},{9,8},{10,9... | collective-permute-start | bytes 786440 | tf_op jit(solution)/shard_map/ppermute | solution.py:218
  90.3 14.8 %collective-permute-start.7 = (bf16[256,512]{1,0:T(8,128)(2,1)S(1)}, bf16[256,512]{1,0:T(8,128)(2,1)S(1)}, u32[]{:S(2)}, u32[]{:S(2)}) collective-permute-start(bf16[256,512]{1,0:T(8,128)(2,1)S(1)} %collective-permute-done.5.refs_4_), channel_id=1, source_target_pairs={{0,7},{1,0},{2,1},{3,2},{4,3},{5,4},{6,5},{7,6},{8,9},{9,10},{10,1... | collective-permute-start | bytes 786440 | tf_op jit(solution)/shard_map/ppermute | solution.py:218
  93.2 15.3 %collective-permute-start.8 = (bf16[256,512]{1,0:T(8,128)(2,1)S(1)}, bf16[256,512]{1,0:T(8,128)(2,1)S(1)}, u32[]{:S(2)}, u32[]{:S(2)}) collective-permute-start(bf16[256,512]{1,0:T(8,128)(2,1)S(1)} %collective-permute-done.4.refs_3_), channel_id=1, source_target_pairs={{0,2},{1,3},{2,4},{3,5},{4,6},{5,7},{6,0},{7,1},{8,14},{9,15},{10,... | collective-permute-start | bytes 786440 | tf_op jit(solution)/shard_map/ppermute | solution.py:218
Sparse Core Ops, SparseCore 0:
  32.5 65.9 all-gather.4

commit v8 on v6

--- a/solution.py
+++ b/solution.py
@@ -223,7 +223,7 @@
         near, behind = shift(block, 1), shift(block, -1)
         gathered += [(-1, near), (1, behind), (-2, far), (2, back)]
         gathered += [(-3, shift(far, 1)), (3, shift(back, -1))]
-        opposite = shift(far, 2)
+        opposite = shift(back, -2)
     else:
         right = block
         if size == 4:
@@ -244,7 +244,7 @@
     count = key_width * value_width // (TILE[0] * TILE[1])
     per = count // 2 // chips
 
-    offsets = (heads // 2 - 1, heads // 2)
+    offsets = (heads // 2 - 1, heads // 2 - 2)
     shards = [
         lax.ppermute(
             out_weight.T,

time: 114 us -> 117 us (1.026)
  the two profiles are of different devices: /device:TPU:24 before, /device:TPU:2 now
where the time goes in v8:
time: 117 us
  starting transfers between devices  60.5 us (52%)
  waiting for transfers between devices  21.7 us (19%)
  between operations  14.1 us (12%)
  Pallas kernels  10.1 us (9%)
  local copies, waits for them, and re-layouts  5.2 us (4%)
  blocking collectives  4.38 us (4%)
    ppermute x7, starting transfers between devices, shift(): return lax.ppermute(value, ('c', axis), moves)  26.7 us
    all_to_all x1, starting transfers between devices, local(): held = lax.all_to_all(send, ('z', 'x'), 0, 0, tiled=True)  15.9 us
    ppermute x2, starting transfers between devices, local(): lax.ppermute(out_weight.T, ('z', 'y'), [(z * heads + h, (h + offset) % he...  12.4 us
    ppermute x7, waiting for transfers between devices, shift(): return lax.ppermute(value, ('c', axis), moves)  8.99 us
    all_to_all x1, waiting for transfers between devices, local(): back = lax.all_to_all(starts, ('z', 'x'), 0, 0, tiled=True)  7.28 us
    all_to_all x1, starting transfers between devices, local(): back = lax.all_to_all(starts, ('z', 'x'), 0, 0, tiled=True)  5.57 us
    all_to_all x1, waiting for transfers between devices, local(): held = lax.all_to_all(send, ('z', 'x'), 0, 0, tiled=True)  5.42 us
    unnamed x12, local copies, waits for them, and re-layouts  5.1 us
  transfers between devices with their start and end apart: 12, of which 4 were waited for; matrix products, arithmetic and copies ran while one was open for 0% of the time, Pallas kernels for 8%

profile of v8, /device:TPU:2, one launch (start us, length us, event | category | flops | bytes accessed | tf_op | source)
XLA Modules:
  0.0 116.6 jit_solution(8265185631743713743)
XLA Ops:
  6.5 0.0 all-gather.5.cloned.1.call-start
  6.5 7.9 %collective-permute-start = (bf16[64,512]{1,0:T(8,128)(2,1)}, bf16[64,512]{1,0:T(8,128)(2,1)S(1)}, u32[]{:S(2)}, u32[]{:S(2)}) collective-permute-start(bf16[64,512]{1,0:T(8,128)(2,1)} %bitcast.26), channel_id=1, source_target_pairs={{0,192},{1,256},{2,320},{3,384},{4,448},{5,0},{6,64},{7,128},{64,1... | collective-permute-start | bytes 196616 | tf_op jit(solution)/shard_map/ppermute | solution.py:249
  14.4 4.5 %collective-permute-start.1 = (bf16[64,512]{1,0:T(8,128)(2,1)}, bf16[64,512]{1,0:T(8,128)(2,1)S(1)}, u32[]{:S(2)}, u32[]{:S(2)}) collective-permute-start(bf16[64,512]{1,0:T(8,128)(2,1)} %bitcast.27), channel_id=1, source_target_pairs={{0,128},{1,192},{2,256},{3,320},{4,384},{5,448},{6,0},{7,64},{64,1... | collective-permute-start | bytes 196616 | tf_op jit(solution)/shard_map/ppermute | solution.py:249
  18.9 2.3 %shard_map.82 = (bf16[65,16,128]{2,1,0:T(8,128)(2,1)}, f32[16,256]{1,0:T(8,128)}) custom-call(bf16[256,256]{1,0:T(8,128)(2,1)} %key_hbm.3, bf16[256,512]{1,0:T(8,128)(2,1)} %value_hbm.3, f32[1,256]{1,0:T(1,128)} %in_hbm.1, f32[1,256]{1,0:T(1,128)} %forget_hbm.1), custom_call_target="tpu_custom_call" | custom-call | bytes 1048576 | tf_op jit(solution)/shard_map/pallas_call | solution.py:261
  21.2 2.4 %all-gather = bf16[130,16,128]{2,1,0:T(8,128)(2,1)S(1)} all-gather(bf16[65,16,128]{2,1,0:T(8,128)(2,1)} %get-tuple-element.21), channel_id=2, replica_groups=mesh['z'=8,'x'=4,'c'=2,'y'=8] {'c'}, dimensions={0}, use_global_device_ids=true | all-gather | bytes 798720 | tf_op jit(solution)/shard_map/all_gather | solution.py:274
  23.6 0.7 shard_map.83
  24.3 0.0 collective-permute-done
  24.4 0.0 collective-permute-done.1
  24.4 0.7 pad_maximum_fusion
  25.0 0.0 all-gather.5.cloned.1.call-update
  25.0 15.9 %all-to-all-start = ((bf16[32,24,128]{2,1,0:T(8,128)(2,1)}), bf16[32,24,128]{2,1,0:T(8,128)(2,1)S(1)}, u32[]{:S(2)}, u32[]{:S(2)}) async-start(bf16[32,24,128]{2,1,0:T(8,128)(2,1)} %shard_map.83), calls=%async_computation | async-start | bytes 393216 | tf_op jit(solution)/shard_map/all_to_all | solution.py:284
  40.9 0.0 copy-start
  40.9 0.9 copy-done
  41.9 0.0 copy-start.1
  41.9 0.9 copy-done.1
  42.8 0.0 copy-start.3
  42.8 0.9 copy-done.3
  43.7 0.0 copy-start.4
  43.7 0.7 copy-done.4
  44.4 1.2 %shard_map.84 = (f32[256,512]{1,0:T(8,128)S(1)}, bf16[256,256]{1,0:T(8,128)(2,1)S(1)}, f32[256,128]{1,0:T(8,128)S(1)}) custom-call(bf16[256,256]{1,0:T(8,128)(2,1)S(1)} %copy-done.3, bf16[256,256]{1,0:T(8,128)(2,1)S(1)} %copy-done.1, bf16[256,512]{1,0:T(8,128)(2,1)S(1)} %copy-done, f32[16,256]{1,0:T(8,128)S(1)} %copy-done.4), custom_call_target="tpu_custom_call" | custom-call | flops 100663296 | bytes 1048576 | tf_op jit(solution)/shard_map/pallas_call | solution.py:285
  45.6 5.4 %all-to-all-done.held_ref = bf16[32,24,128]{2,1,0:T(8,128)(2,1)S(1)} async-done(((bf16[32,24,128]{2,1,0:T(8,128)(2,1)}), bf16[32,24,128]{2,1,0:T(8,128)(2,1)S(1)}, u32[]{:S(2)}, u32[]{:S(2)}) %all-to-all-start) | async-done | bytes 196640 | tf_op jit(solution)/shard_map/all_to_all | solution.py:284
  51.0 0.8 shard_map.85
  51.8 5.6 %all-to-all-start.1 = ((bf16[32,16,128]{2,1,0:T(8,128)(2,1)}), bf16[32,16,128]{2,1,0:T(8,128)(2,1)S(1)}, u32[]{:S(2)}, u32[]{:S(2)}) async-start(bf16[32,16,128]{2,1,0:T(8,128)(2,1)} %get-tuple-element.30), calls=%async_computation.1 | async-start | bytes 262144 | tf_op jit(solution)/shard_map/all_to_all | solution.py:307
  57.4 0.0 copy-start.2
  57.4 0.9 copy-done.2
  58.4 0.0 copy-start.5
  58.4 0.7 copy-done.5
  59.0 0.1 shard_map.86.gate_ref
  59.1 7.3 %all-to-all-done.1 = bf16[32,16,128]{2,1,0:T(8,128)(2,1)S(1)} async-done(((bf16[32,16,128]{2,1,0:T(8,128)(2,1)}), bf16[32,16,128]{2,1,0:T(8,128)(2,1)S(1)}, u32[]{:S(2)}, u32[]{:S(2)}) %all-to-all-start.1) | async-done | bytes 131104 | tf_op jit(solution)/shard_map/all_to_all | solution.py:307
  66.4 2.0 %all-gather.2.tiles_ref = bf16[64,16,128]{2,1,0:T(8,128)(2,1)S(1)} all-gather(bf16[32,16,128]{2,1,0:T(8,128)(2,1)S(1)} %all-to-all-done.1), channel_id=4, replica_groups=mesh['z'=8,'x'=4,'c'=2,'y'=8] {'c'}, dimensions={0}, use_global_device_ids=true | all-gather | bytes 393216 | tf_op jit(solution)/shard_map/all_gather | solution.py:312
  68.4 0.6 shard_map.87.refs_0_
  69.0 2.5 %collective-permute-start.5 = (bf16[256,512]{1,0:T(8,128)(2,1)S(1)}, bf16[256,512]{1,0:T(8,128)(2,1)S(1)}, u32[]{:S(2)}, u32[]{:S(2)}) collective-permute-start(bf16[256,512]{1,0:T(8,128)(2,1)S(1)} %shard_map.87.refs_0_), channel_id=1, source_target_pairs={{0,6},{1,7},{2,0},{3,1},{4,2},{5,3},{6,4},{7,5},{8,10},{9,11},{10,... | collective-permute-start | bytes 786440 | tf_op jit(solution)/shard_map/ppermute | solution.py:218
  71.5 4.3 %collective-permute-start.4 = (bf16[256,512]{1,0:T(8,128)(2,1)S(1)}, bf16[256,512]{1,0:T(8,128)(2,1)S(1)}, u32[]{:S(2)}, u32[]{:S(2)}) collective-permute-start(bf16[256,512]{1,0:T(8,128)(2,1)S(1)} %shard_map.87.refs_0_), channel_id=1, source_target_pairs={{0,2},{1,3},{2,4},{3,5},{4,6},{5,7},{6,0},{7,1},{8,14},{9,15},{10,... | collective-permute-start | bytes 786440 | tf_op jit(solution)/shard_map/ppermute | solution.py:218
  75.7 4.1 %collective-permute-start.2 = (bf16[256,512]{1,0:T(8,128)(2,1)S(1)}, bf16[256,512]{1,0:T(8,128)(2,1)S(1)}, u32[]{:S(2)}, u32[]{:S(2)}) collective-permute-start(bf16[256,512]{1,0:T(8,128)(2,1)S(1)} %shard_map.87.refs_0_), channel_id=1, source_target_pairs={{0,1},{1,2},{2,3},{3,4},{4,5},{5,6},{6,7},{7,0},{8,15},{9,8},{10,9... | collective-permute-start | bytes 786440 | tf_op jit(solution)/shard_map/ppermute | solution.py:218
  79.8 3.0 %collective-permute-start.3 = (bf16[256,512]{1,0:T(8,128)(2,1)S(1)}, bf16[256,512]{1,0:T(8,128)(2,1)S(1)}, u32[]{:S(2)}, u32[]{:S(2)}) collective-permute-start(bf16[256,512]{1,0:T(8,128)(2,1)S(1)} %shard_map.87.refs_0_), channel_id=1, source_target_pairs={{0,7},{1,0},{2,1},{3,2},{4,3},{5,4},{6,5},{7,6},{8,9},{9,10},{10,1... | collective-permute-start | bytes 786440 | tf_op jit(solution)/shard_map/ppermute | solution.py:218
  82.9 0.0 collective-permute-done.5.refs_4_
  82.9 7.5 %collective-permute-start.7 = (bf16[256,512]{1,0:T(8,128)(2,1)S(1)}, bf16[256,512]{1,0:T(8,128)(2,1)S(1)}, u32[]{:S(2)}, u32[]{:S(2)}) collective-permute-start(bf16[256,512]{1,0:T(8,128)(2,1)S(1)} %collective-permute-done.5.refs_4_), channel_id=1, source_target_pairs={{0,7},{1,0},{2,1},{3,2},{4,3},{5,4},{6,5},{7,6},{8,9},{9,10},{10,1... | collective-permute-start | bytes 786440 | tf_op jit(solution)/shard_map/ppermute | solution.py:218
  90.4 0.0 collective-permute-done.4.refs_3_
  90.4 1.9 %collective-permute-start.6 = (bf16[256,512]{1,0:T(8,128)(2,1)S(1)}, bf16[256,512]{1,0:T(8,128)(2,1)S(1)}, u32[]{:S(2)}, u32[]{:S(2)}) collective-permute-start(bf16[256,512]{1,0:T(8,128)(2,1)S(1)} %collective-permute-done.4.refs_3_), channel_id=1, source_target_pairs={{0,1},{1,2},{2,3},{3,4},{4,5},{5,6},{6,7},{7,0},{8,15},{9,8},{10,9... | collective-permute-start | bytes 786440 | tf_op jit(solution)/shard_map/ppermute | solution.py:218
  92.3 3.4 %collective-permute-start.8 = (bf16[256,512]{1,0:T(8,128)(2,1)S(1)}, bf16[256,512]{1,0:T(8,128)(2,1)S(1)}, u32[]{:S(2)}, u32[]{:S(2)}) collective-permute-start(bf16[256,512]{1,0:T(8,128)(2,1)S(1)} %collective-permute-done.5.refs_4_), channel_id=1, source_target_pairs={{0,6},{1,7},{2,0},{3,1},{4,2},{5,3},{6,4},{7,5},{8,10},{9,11},{10,... | collective-permute-start | bytes 786440 | tf_op jit(solution)/shard_map/ppermute | solution.py:218
  96.2 0.1 stack.67.where_ref
  96.3 0.0 collective-permute-done.2.refs_1_
  96.4 0.0 collective-permute-done.3.refs_2_
  96.4 0.8 collective-permute-done.7.refs_6_
  97.2 8.1 %collective-permute-done.6.refs_5_ = bf16[256,512]{1,0:T(8,128)(2,1)S(1)} collective-permute-done((bf16[256,512]{1,0:T(8,128)(2,1)S(1)}, bf16[256,512]{1,0:T(8,128)(2,1)S(1)}, u32[]{:S(2)}, u32[]{:S(2)}) %collective-permute-start.6) | collective-permute-done | bytes 262176 | tf_op jit(solution)/shard_map/ppermute | solution.py:218
  105.3 0.0 all-gather.5.cloned.1.call-done
  105.3 3.4 %shard_map.88 = (f32[256,512]{1,0:T(8,128)S(1)}, bf16[8,64,512]{2,1,0:T(8,128)(2,1)S(1)}) custom-call(s32[16]{0:T(128)S(1)} %stack.67.where_ref, bf16[4,8,2,64,512]{4,3,2,1,0:T(8,128)(2,1)} %bitcast.25, bf16[256,512]{1,0:T(8,128)(2,1)S(1)} %shard_map.87.refs_0_, bf16[256,512]{1,0:T(8,128)(2,1)S(1)} %collective-permute-done.2.refs_1_, ...), custom_call_target="tpu_custom_call" | custom-call | flops 1073741824 | bytes 8388608 | tf_op jit(solution)/shard_map/pallas_call | solution.py:327
  108.7 0.0 collective-permute-done.8.normed_ref
  108.7 1.0 shard_map.89
Async XLA Ops:
  6.5 98.8 %all-gather.5.cloned.1.call-start = ((), (), s32[]{:S(2)}) async-start(), calls=%async_computation.2 | async-start | bytes 4325376 | tf_op jit(solution)/shard_map/all_gather | solution.py:281
  6.5 17.8 %collective-permute-start = (bf16[64,512]{1,0:T(8,128)(2,1)}, bf16[64,512]{1,0:T(8,128)(2,1)S(1)}, u32[]{:S(2)}, u32[]{:S(2)}) collective-permute-start(bf16[64,512]{1,0:T(8,128)(2,1)} %bitcast.26), channel_id=1, source_target_pairs={{0,192},{1,256},{2,320},{3,384},{4,448},{5,0},{6,64},{7,128},{64,1... | collective-permute-start | bytes 196616 | tf_op jit(solution)/shard_map/ppermute | solution.py:249
  14.4 9.9 %collective-permute-start.1 = (bf16[64,512]{1,0:T(8,128)(2,1)}, bf16[64,512]{1,0:T(8,128)(2,1)S(1)}, u32[]{:S(2)}, u32[]{:S(2)}) collective-permute-start(bf16[64,512]{1,0:T(8,128)(2,1)} %bitcast.27), channel_id=1, source_target_pairs={{0,128},{1,192},{2,256},{3,320},{4,384},{5,448},{6,0},{7,64},{64,1... | collective-permute-start | bytes 196616 | tf_op jit(solution)/shard_map/ppermute | solution.py:249
  25.0 26.0 %all-to-all-start = ((bf16[32,24,128]{2,1,0:T(8,128)(2,1)}), bf16[32,24,128]{2,1,0:T(8,128)(2,1)S(1)}, u32[]{:S(2)}, u32[]{:S(2)}) async-start(bf16[32,24,128]{2,1,0:T(8,128)(2,1)} %shard_map.83), calls=%async_computation | async-start | bytes 393216 | tf_op jit(solution)/shard_map/all_to_all | solution.py:284
  40.9 1.0 copy-start
  41.9 0.9 copy-start.1
  42.8 0.9 copy-start.3
  43.7 0.7 copy-start.4
  51.8 14.6 %all-to-all-start.1 = ((bf16[32,16,128]{2,1,0:T(8,128)(2,1)}), bf16[32,16,128]{2,1,0:T(8,128)(2,1)S(1)}, u32[]{:S(2)}, u32[]{:S(2)}) async-start(bf16[32,16,128]{2,1,0:T(8,128)(2,1)} %get-tuple-element.30), calls=%async_computation.1 | async-start | bytes 262144 | tf_op jit(solution)/shard_map/all_to_all | solution.py:307
  57.4 1.0 copy-start.2
  58.4 0.7 copy-start.5
  69.0 13.9 %collective-permute-start.5 = (bf16[256,512]{1,0:T(8,128)(2,1)S(1)}, bf16[256,512]{1,0:T(8,128)(2,1)S(1)}, u32[]{:S(2)}, u32[]{:S(2)}) collective-permute-start(bf16[256,512]{1,0:T(8,128)(2,1)S(1)} %shard_map.87.refs_0_), channel_id=1, source_target_pairs={{0,6},{1,7},{2,0},{3,1},{4,2},{5,3},{6,4},{7,5},{8,10},{9,11},{10,... | collective-permute-start | bytes 786440 | tf_op jit(solution)/shard_map/ppermute | solution.py:218
  71.5 18.9 %collective-permute-start.4 = (bf16[256,512]{1,0:T(8,128)(2,1)S(1)}, bf16[256,512]{1,0:T(8,128)(2,1)S(1)}, u32[]{:S(2)}, u32[]{:S(2)}) collective-permute-start(bf16[256,512]{1,0:T(8,128)(2,1)S(1)} %shard_map.87.refs_0_), channel_id=1, source_target_pairs={{0,2},{1,3},{2,4},{3,5},{4,6},{5,7},{6,0},{7,1},{8,14},{9,15},{10,... | collective-permute-start | bytes 786440 | tf_op jit(solution)/shard_map/ppermute | solution.py:218
  75.7 20.6 %collective-permute-start.2 = (bf16[256,512]{1,0:T(8,128)(2,1)S(1)}, bf16[256,512]{1,0:T(8,128)(2,1)S(1)}, u32[]{:S(2)}, u32[]{:S(2)}) collective-permute-start(bf16[256,512]{1,0:T(8,128)(2,1)S(1)} %shard_map.87.refs_0_), channel_id=1, source_target_pairs={{0,1},{1,2},{2,3},{3,4},{4,5},{5,6},{6,7},{7,0},{8,15},{9,8},{10,9... | collective-permute-start | bytes 786440 | tf_op jit(solution)/shard_map/ppermute | solution.py:218
  79.8 16.5 %collective-permute-start.3 = (bf16[256,512]{1,0:T(8,128)(2,1)S(1)}, bf16[256,512]{1,0:T(8,128)(2,1)S(1)}, u32[]{:S(2)}, u32[]{:S(2)}) collective-permute-start(bf16[256,512]{1,0:T(8,128)(2,1)S(1)} %shard_map.87.refs_0_), channel_id=1, source_target_pairs={{0,7},{1,0},{2,1},{3,2},{4,3},{5,4},{6,5},{7,6},{8,9},{9,10},{10,1... | collective-permute-start | bytes 786440 | tf_op jit(solution)/shard_map/ppermute | solution.py:218
  82.9 14.3 %collective-permute-start.7 = (bf16[256,512]{1,0:T(8,128)(2,1)S(1)}, bf16[256,512]{1,0:T(8,128)(2,1)S(1)}, u32[]{:S(2)}, u32[]{:S(2)}) collective-permute-start(bf16[256,512]{1,0:T(8,128)(2,1)S(1)} %collective-permute-done.5.refs_4_), channel_id=1, source_target_pairs={{0,7},{1,0},{2,1},{3,2},{4,3},{5,4},{6,5},{7,6},{8,9},{9,10},{10,1... | collective-permute-start | bytes 786440 | tf_op jit(solution)/shard_map/ppermute | solution.py:218
  90.4 14.9 %collective-permute-start.6 = (bf16[256,512]{1,0:T(8,128)(2,1)S(1)}, bf16[256,512]{1,0:T(8,128)(2,1)S(1)}, u32[]{:S(2)}, u32[]{:S(2)}) collective-permute-start(bf16[256,512]{1,0:T(8,128)(2,1)S(1)} %collective-permute-done.4.refs_3_), channel_id=1, source_target_pairs={{0,1},{1,2},{2,3},{3,4},{4,5},{5,6},{6,7},{7,0},{8,15},{9,8},{10,9... | collective-permute-start | bytes 786440 | tf_op jit(solution)/shard_map/ppermute | solution.py:218
  92.3 16.4 %collective-permute-start.8 = (bf16[256,512]{1,0:T(8,128)(2,1)S(1)}, bf16[256,512]{1,0:T(8,128)(2,1)S(1)}, u32[]{:S(2)}, u32[]{:S(2)}) collective-permute-start(bf16[256,512]{1,0:T(8,128)(2,1)S(1)} %collective-permute-done.5.refs_4_), channel_id=1, source_target_pairs={{0,6},{1,7},{2,0},{3,1},{4,2},{5,3},{6,4},{7,5},{8,10},{9,11},{10,... | collective-permute-start | bytes 786440 | tf_op jit(solution)/shard_map/ppermute | solution.py:218
Sparse Core Ops, SparseCore 0:
  25.2 71.2 all-gather.4
